TPU v7x, 32 devices: a whole 2x2x4 slice. The times are simulated.
32 devices in a mesh: seq: 4 (over y, core), rows: 8 (over z, x).
Axes of the slice: x: 2, y: 2, z: 4, core: 2. Of those that a mesh axis runs over, the one named last changes fastest.
Arguments:
- tokens: bfloat16 [64, 512, 768], P('rows', 'seq'), may hold values from -6 to 6
- query_weight: bfloat16 [768, 768], replicated, may hold values from -0.21875 to 0.21875
- query_bias: bfloat16 [768], replicated, may hold values from -1.5 to 1.5
- key_weight: bfloat16 [768, 768], replicated, may hold values from -0.21875 to 0.21875
- value_weight: bfloat16 [768, 768], replicated, may hold values from -0.21875 to 0.21875
- value_bias: bfloat16 [768], replicated, may hold values from -1.5 to 1.5
- output_weight: bfloat16 [768, 768], replicated, may hold values from -1.75 to 1.75
- output_bias: bfloat16 [768], replicated, may hold values from -1.5 to 1.5
- attn_gain: bfloat16 [768], replicated, may hold values from 0.5 to 1.5
- attn_shift: bfloat16 [768], replicated, may hold values from -0.5 to 0.5
- inner_weight: bfloat16 [768, 3072], replicated, may hold values from -0.21875 to 0.21875
- inner_bias: bfloat16 [3072], replicated, may hold values from -1.5 to 1.5
- outer_weight: bfloat16 [3072, 768], replicated, may hold values from -0.109375 to 0.109375
- outer_bias: bfloat16 [768], replicated, may hold values from -1.5 to 1.5
- ffn_gain: bfloat16 [768], replicated, may hold values from 0.5 to 1.5
- ffn_shift: bfloat16 [768], replicated, may hold values from -0.5 to 0.5
- segment_ids: int32 [64, 512], P('rows'), may hold values from 0 to 7, as said below
- positives: int32 [512], P('rows'), may hold values from 0 to 511, as said below
Outputs:
- loss_mean: float32 [], replicated
- grad_tokens: float32 [64, 512, 768], P('rows', 'seq')
- grad_query_weight: float32 [768, 768], replicated
- grad_query_bias: float32 [768], replicated
- grad_key_weight: float32 [768, 768], replicated
- grad_value_weight: float32 [768, 768], replicated
- grad_value_bias: float32 [768], replicated
- grad_output_weight: float32 [768, 768], replicated
- grad_output_bias: float32 [768], replicated
- grad_attn_gain: float32 [768], replicated
- grad_attn_shift: float32 [768], replicated
- grad_inner_weight: float32 [768, 3072], replicated
- grad_inner_bias: float32 [3072], replicated
- grad_outer_weight: float32 [3072, 768], replicated
- outer_bias_gradient: float32 [768], replicated
- grad_ffn_gain: float32 [768], replicated
- grad_ffn_shift: float32 [768], replicated
Inputs may be any that keep to these rules, and one draw needn't show every extreme that they name: `segment_ids`: in each row the ids never fall, every id of 0 to 7 occurs, and one segment covers 512 - 127 positions or more. positives[i] differs from i.
All inputs are finite; a program needn't handle non-finite values.
Results may differ from a plain program's by a relative error of at most 0.012.
Values may be sent and summed in bfloat16 or wider, within the bound.
A program may use at most 256 MiB of HBM per device.

v0:
```python
import jax
import jax.numpy as jnp
from jax import lax
from jax.sharding import PartitionSpec as P

HEADS = 12
SEG_ROW = 8


maximal_accuracy_mode = lax.Precision.HIGHEST
norm_eps = 1e-12
pool_eps = 1e-06
softmax_temper = 0.01
masked_score = -1000000000.0
inv_root_two_pi = 0.3989422804014327
inv_root_two = 0.7071067811865476


def layer_norm(resid, gain, shift):
    center = resid - jnp.mean(resid, axis=-1, keepdims=True)
    spread = jnp.mean(center * center, axis=-1, keepdims=True)
    return center * lax.rsqrt(spread + norm_eps) * gain + shift


def softmax_rows(similarity_logits):
    top = jnp.max(similarity_logits, axis=-1, keepdims=True)
    expo = jnp.exp(similarity_logits - top)
    return expo / jnp.sum(expo, axis=-1, keepdims=True)


def contrast_terms(pooled, query_rows, query_start, positives_part):
    normalized_rows = pooled * lax.rsqrt(jnp.sum(pooled * pooled, axis=1, keepdims=True) + pool_eps)
    start = jnp.asarray(query_start)
    selected_entries = lax.dynamic_slice_in_dim(normalized_rows, start, query_rows, 0)
    similarity_logits = (
        jnp.dot(selected_entries, normalized_rows.T, precision=maximal_accuracy_mode)
        / softmax_temper
    )
    row_index = jnp.arange(query_rows, dtype=jnp.int32) + start
    column_index = jnp.arange(pooled.shape[0], dtype=jnp.int32)
    similarity_logits = jnp.where(
        column_index[None, :] == row_index[:, None], masked_score, similarity_logits
    )
    top = jnp.max(similarity_logits, axis=1, keepdims=True)
    spread_log = jnp.log(jnp.sum(jnp.exp(similarity_logits - top), axis=1)) + top[:, 0]
    picked = jnp.sum(
        jnp.where(column_index[None, :] == positives_part[:, None], similarity_logits, 0.0), axis=1
    )
    return jnp.sum(spread_log - picked)


def attention_probs(queries4, key4, query_ids, key_ids, scale):
    raw = jnp.einsum("bqhd,bkhd->bhqk", queries4, key4, preferred_element_type=jnp.float32) * scale
    same = query_ids[:, None, :, None] == key_ids[:, None, None, :]
    return softmax_rows(jnp.where(same, raw, masked_score))


def gelu_slope(inner):
    return (
        0.5 * (1.0 + lax.erf(inner * inv_root_two))
        + inner * jnp.exp(-0.5 * inner * inner) * inv_root_two_pi
    )


def token_contract(left, right):
    return jnp.einsum("nd,ne->de", left, right, preferred_element_type=jnp.float32)


def times_transpose(grad, weight):
    return jnp.einsum("ne,de->nd", grad, weight, preferred_element_type=jnp.float32)


def column_sums(matrix):
    return jnp.sum(matrix.astype(jnp.float32), axis=0)


def local(
    tokens,
    query_weight,
    query_bias,
    key_weight,
    value_weight,
    value_bias,
    output_weight,
    output_bias,
    attn_gain,
    attn_shift,
    inner_weight,
    inner_bias,
    outer_weight,
    outer_bias,
    ffn_gain,
    ffn_shift,
    segment_ids,
    positives,
):
    group_rows, local_len, width = tokens.shape
    seq_count = lax.axis_size("seq")
    seq_place = lax.axis_index("seq")
    head_dim = width // HEADS
    scale = head_dim ** (-0.5)
    query_ids = lax.dynamic_slice_in_dim(segment_ids, seq_place * local_len, local_len, 1)
    batch, query_len, _ = tokens.shape
    flat = tokens.reshape(batch * query_len, width)
    queries = (
        jnp.dot(flat, query_weight, preferred_element_type=jnp.float32)
        + query_bias.astype(jnp.float32)
    ).astype(jnp.bfloat16)
    key_local = jnp.dot(flat, key_weight, preferred_element_type=jnp.float32).astype(jnp.bfloat16)
    value_local = (
        jnp.dot(flat, value_weight, preferred_element_type=jnp.float32)
        + value_bias.astype(jnp.float32)
    ).astype(jnp.bfloat16)
    key_local = key_local.reshape(batch, query_len, width)
    value_local = value_local.reshape(batch, query_len, width)
    key_all, value_all = (
        lax.all_gather(key_local, "seq", axis=1, tiled=True),
        lax.all_gather(value_local, "seq", axis=1, tiled=True),
    )
    key_len = key_all.shape[1]
    queries4 = queries.reshape(batch, query_len, HEADS, head_dim)
    key4 = key_all.reshape(batch, key_len, HEADS, head_dim)
    value4 = value_all.reshape(batch, key_len, HEADS, head_dim)
    probs = attention_probs(queries4, key4, query_ids, segment_ids, scale)
    probs_low = probs.astype(jnp.bfloat16)
    heads_out = jnp.einsum("bhqk,bkhd->bqhd", probs_low, value4, preferred_element_type=jnp.float32)
    heads_out = heads_out.astype(jnp.bfloat16).reshape(batch * query_len, width)
    attn_out = jnp.dot(
        heads_out, output_weight, preferred_element_type=jnp.float32
    ) + output_bias.astype(jnp.float32)
    resid_one = flat.astype(jnp.float32) + attn_out
    hidden, norm_one_pull = jax.vjp(
        layer_norm, resid_one, attn_gain.astype(jnp.float32), attn_shift.astype(jnp.float32)
    )
    hidden_low = hidden.astype(jnp.bfloat16)
    inner = jnp.dot(
        hidden_low, inner_weight, preferred_element_type=jnp.float32
    ) + inner_bias.astype(jnp.float32)
    active_low = jax.nn.gelu(inner, approximate=False).astype(jnp.bfloat16)
    outer = jnp.dot(
        active_low, outer_weight, preferred_element_type=jnp.float32
    ) + outer_bias.astype(jnp.float32)
    output, norm_two_pull = jax.vjp(
        layer_norm, hidden + outer, ffn_gain.astype(jnp.float32), ffn_shift.astype(jnp.float32)
    )
    seg_range = jnp.arange(SEG_ROW, dtype=jnp.int32)
    onehot_query = (query_ids[:, :, None] == seg_range[None, None, :]).astype(jnp.float32)
    onehot_group = (segment_ids[:, :, None] == seg_range[None, None, :]).astype(jnp.float32)
    group_segs = group_rows * SEG_ROW
    counts = jnp.sum(onehot_group, axis=1).reshape(group_segs, 1)
    seg_sums = jnp.einsum(
        "bls,bld->bsd",
        onehot_query,
        output.reshape(batch, query_len, width),
        precision=maximal_accuracy_mode,
    )
    group_sums = lax.psum(seg_sums.reshape(group_segs, width), "seq")
    pooled_group_rows = group_sums / counts
    all_pooled = lax.all_gather(pooled_group_rows, "rows", axis=0, tiled=True)
    total_segs = all_pooled.shape[0]
    group_start = lax.axis_index("rows") * group_segs

    def local_loss(pooled_all):
        return contrast_terms(pooled_all, group_segs, group_start, positives)

    loss_part, loss_pull = jax.vjp(local_loss, all_pooled)
    (pooled_grad,) = loss_pull(jnp.ones_like(loss_part))
    group_grad = lax.psum_scatter(pooled_grad, "rows", scatter_dimension=0, tiled=True) / counts
    group_grad3 = group_grad.reshape(group_rows, SEG_ROW, width)
    output_grad = jnp.einsum(
        "bls,bsd->bld", onehot_query, group_grad3, precision=maximal_accuracy_mode
    ).reshape(batch * query_len, width)
    resid_two_grad, g_ffn_gain, g_ffn_shift = norm_two_pull(output_grad)
    outer_grad = resid_two_grad.astype(jnp.bfloat16)
    g_outer_w = token_contract(active_low, outer_grad)
    g_outer_b = column_sums(outer_grad)
    active_grad = times_transpose(outer_grad, outer_weight)
    inner_grad = (active_grad * gelu_slope(inner)).astype(jnp.bfloat16)
    g_inner_w = token_contract(hidden_low, inner_grad)
    g_inner_b = column_sums(inner_grad)
    hidden_grad = resid_two_grad + times_transpose(inner_grad, inner_weight)
    first_residual_gradient, g_attn_gain, g_attn_shift = norm_one_pull(hidden_grad)
    attn_grad = first_residual_gradient.astype(jnp.bfloat16)
    g_output_w = token_contract(heads_out, attn_grad)
    g_output_b = column_sums(attn_grad)
    heads_grad = times_transpose(attn_grad, output_weight).astype(jnp.bfloat16)
    heads_grad4 = heads_grad.reshape(batch, query_len, HEADS, head_dim)
    probs_grad = jnp.einsum(
        "bqhd,bkhd->bhqk", heads_grad4, value4, preferred_element_type=jnp.float32
    )
    value_grad_all = jnp.einsum(
        "bhqk,bqhd->bkhd", probs_low, heads_grad4, preferred_element_type=jnp.float32
    )
    score_grad = probs * (probs_grad - jnp.sum(probs_grad * probs, axis=-1, keepdims=True))
    score_grad = score_grad.astype(jnp.bfloat16)
    query_grad = (
        jnp.einsum("bhqk,bkhd->bqhd", score_grad, key4, preferred_element_type=jnp.float32) * scale
    )
    query_grad = query_grad.astype(jnp.bfloat16).reshape(batch * query_len, width)
    key_grad_all = (
        jnp.einsum("bhqk,bqhd->bkhd", score_grad, queries4, preferred_element_type=jnp.float32)
        * scale
    )
    key_grad_all = key_grad_all.reshape(batch, key_len, width)
    value_grad_all = value_grad_all.reshape(batch, key_len, width)
    key_grad_sum, value_grad_sum = (
        lax.psum_scatter(
            key_grad_all.astype(jnp.bfloat16), "seq", scatter_dimension=1, tiled=True
        ).astype(jnp.float32),
        lax.psum_scatter(
            value_grad_all.astype(jnp.bfloat16), "seq", scatter_dimension=1, tiled=True
        ).astype(jnp.float32),
    )
    key_grad = key_grad_sum.astype(jnp.bfloat16).reshape(batch * query_len, width)
    value_grad = value_grad_sum.astype(jnp.bfloat16).reshape(batch * query_len, width)
    g_query_w = token_contract(flat, query_grad)
    g_query_b = column_sums(query_grad)
    g_key_w = token_contract(flat, key_grad)
    g_value_w = token_contract(flat, value_grad)
    g_value_b = column_sums(value_grad)
    token_grad = (
        first_residual_gradient
        + times_transpose(query_grad, query_weight)
        + times_transpose(key_grad, key_weight)
        + times_transpose(value_grad, value_weight)
    )
    loss_share = loss_part / seq_count
    (
        g_query_w,
        g_query_b,
        g_key_w,
        g_value_w,
        g_value_b,
        g_output_w,
        g_output_b,
        g_attn_gain,
        g_attn_shift,
        loss_total,
        g_inner_w,
        g_inner_b,
        g_outer_w,
        g_outer_b,
        g_ffn_gain,
        g_ffn_shift,
    ) = lax.psum(
        (
            g_query_w,
            g_query_b,
            g_key_w,
            g_value_w,
            g_value_b,
            g_output_w,
            g_output_b,
            g_attn_gain,
            g_attn_shift,
            loss_share,
            g_inner_w,
            g_inner_b,
            g_outer_w,
            g_outer_b,
            g_ffn_gain,
            g_ffn_shift,
        ),
        ("seq", "rows"),
    )
    grad_tokens = token_grad.reshape(batch, query_len, width)
    return (
        loss_total / total_segs,
        grad_tokens,
        g_query_w,
        g_query_b,
        g_key_w,
        g_value_w,
        g_value_b,
        g_output_w,
        g_output_b,
        g_attn_gain,
        g_attn_shift,
        g_inner_w,
        g_inner_b,
        g_outer_w,
        g_outer_b,
        g_ffn_gain,
        g_ffn_shift,
    )


def solution(mesh):
    placed = (
        P("rows", "seq", None),
        P(),
        P(),
        P(),
        P(),
        P(),
        P(),
        P(),
        P(),
        P(),
        P(),
        P(),
        P(),
        P(),
        P(),
        P(),
        P("rows", None),
        P("rows"),
    )
    return jax.shard_map(
        local,
        mesh=mesh,
        in_specs=placed,
        out_specs=(
            P(),
            P("rows", "seq", None),
            P(),
            P(),
            P(),
            P(),
            P(),
            P(),
            P(),
            P(),
            P(),
            P(),
            P(),
            P(),
            P(),
            P(),
            P(),
        ),
        check_vma=False,
    )
```

profile of v0, /device:TPU:0, one launch (start us, length us, event | category | flops | bytes accessed | tf_op | source)
XLA Modules:
  0.0 1015.9 jit_solution(9172526070412519874)
XLA Ops:
  7.3 4.4 convolution_convert_fusion.1
  11.9 4.0 add_convert_fusion.1
  16.5 3.1 add_convert_fusion
  19.8 1.8 copy.62
  21.6 2.1 copy.80
  26.0 35.0 %all-gather.6.cloned.1.call-done = bf16[8,512,768]{2,1,0:T(8,128)(2,1)} async-done(((bf16[8,128,768]{2,1,0:T(8,128)(2,1)}), bf16[8,512,768]{2,1,0:T(8,128)(2,1)}) %all-gather.6.cloned.1.call-update) | async-done | bytes 6291472 | tf_op jit(solution)/shard_map/all_gather | solution.py:117
  61.0 8.6 copy.63
  69.6 16.2 %fusion.84 = (f32[8,12,128]{2,1,0:T(8,128)S(1)}, f32[8,12,128,512]{3,2,1,0:T(8,128)}) fusion(pred[8,128,512]{2,1,0:T(8,128)(4,1)S(1)} %broadcast_compare_fusion, bf16[8,512,12,64]{1,3,2,0:T(8,128)(2,1)} %bitcast.116, bf16[8,128,12,64]{1,0,3,2:T(8,128)(2,1)S(1)} %bitcast.125), kind=kOutput, calls=%fused_computation.152 | convolution fusion | flops 830472704 | bytes 33603584 | tf_op jit(solution)/shard_map/sub | solution.py:27
  85.8 23.7 %all-gather.4.cloned.1.call-done = bf16[8,512,768]{2,1,0:T(8,128)(2,1)} async-done(((bf16[8,128,768]{2,1,0:T(8,128)(2,1)}), bf16[8,512,768]{2,1,0:T(8,128)(2,1)}) %all-gather.4.cloned.1.call-update) | async-done | bytes 6291472 | tf_op jit(solution)/shard_map/all_gather | solution.py:118
  109.5 8.6 copy.61
  118.1 12.4 %fusion.41 = bf16[8,128,12,64]{1,3,2,0:T(8,128)(2,1)S(1)} fusion(bf16[8,512,12,64]{1,3,2,0:T(8,128)(2,1)} %bitcast.122, f32[8,12,128,512]{3,2,1,0:T(8,128)} %get-tuple-element.101, f32[8,12,128]{2,1,0:T(8,128)S(1)} %get-tuple-element.100), kind=kOutput, calls=%fused_computation.85 | convolution fusion | flops 818675712 | bytes 33079296 | tf_op jit(solution)/shard_map/bhqk,bkhd->bqhd/dot_general | solution.py:126
  134.9 34.8 %fusion.4 = (bf16[1024,3072]{1,0:T(8,128)(2,1)S(1)}, f32[1024,3072]{1,0:T(8,128)}) fusion(f32[3072]{0:T(1024)S(1)} %convert_element_type.134, bf16[768,3072]{1,0:T(8,128)(2,1)S(1)} %bitcast.144, f32[1024,768]{1,0:T(8,128)S(1)} %get-tuple-element.103, f32[768]{0:T(1024)S(1)} %convert_element_type.132, f32[768]{0:T(1024)S(1)} %convert_element_type.131, ...), kind=kOutput, calls=%fused_computation.10 | convolution fusion | flops 5043388416 | bytes 26765312 | tf_op jit(solution)/shard_map/dot_general | solution.py:136
  169.8 5.4 fusion.90
  176.9 1.8 convolution_bitcast_fusion.3
  179.0 31.6 %all-reduce.5.cloned.1.call-done = f32[64,768]{1,0:T(8,128)} async-done(((f32[64,768]{1,0:T(8,128)}), f32[64,768]{1,0:T(8,128)}) %all-reduce.5.cloned.1.call-update) | async-done | bytes 196624 | tf_op jit(solution)/shard_map/psum | solution.py:157
  212.4 45.3 %all-gather.8.cloned.1.call-done = f32[512,768]{1,0:T(8,128)} async-done(((f32[64,768]{1,0:T(8,128)}), f32[512,768]{1,0:T(8,128)}) %all-gather.8.cloned.1.call-update) | async-done | bytes 1572880 | tf_op jit(solution)/shard_map/all_gather | solution.py:159
  260.9 1.7 fusion.91
  268.1 63.7 %reduce-scatter.4.cloned.1.call-done = f32[64,768]{1,0:T(8,128)} async-done(((f32[512,768]{1,0:T(8,128)}), f32[64,768]{1,0:T(8,128)}) %reduce-scatter.4.cloned.1.call-update) | async-done | bytes 196624 | tf_op jit(solution)/shard_map/reduce_scatter | solution.py:168
  331.8 3.1 fusion.92
  336.5 1.8 fusion.83
  339.3 12.9 %convert_reduce_fusion = (f32[3072]{0:T(1024)}, bf16[1024,3072]{1,0:T(8,128)(2,1)S(1)}) fusion(f32[1024,3072]{1,0:T(8,128)} %get-tuple-element.105, f32[3072]{0:T(1024)S(1)} %convert_element_type.134, bf16[1024,768]{1,0:T(8,128)(2,1)S(1)} %get-tuple-element.93, bf16[3072,768]{1,0:T(8,128)(2,1)S(1)} %bitcast.142), kind=kOutput, calls=%fused_computation.17 | convolution fusion | flops 4872729600 | bytes 25190400 | tf_op jit(solution)/shard_map/ne,de->nd/dot_general | solution.py:70
  352.2 6.4 multiply_reduce_fusion.1
  363.8 2.6 convolution_convert_fusion
  368.6 21.9 %multiply_reduce_fusion = (f32[8,12,128]{2,1,0:T(8,128)S(1)}, f32[8,12,128,512]{3,2,1,0:T(8,128)}) fusion(f32[8,12,128,512]{3,2,1,0:T(8,128)} %get-tuple-element.101, f32[8,12,128]{2,1,0:T(8,128)S(1)} %copy-done.37, bf16[8,512,12,64]{1,3,2,0:T(8,128)(2,1)} %bitcast.123, bf16[8,128,12,64]{1,0,3,2:T(8,128)(2,1)S(1)} %bitcast.137), kind=kOutput, calls=%fused_computation.2 | convolution fusion | flops 824168448 | bytes 58294272 | tf_op jit(solution)/shard_map/bqhd,bkhd->bhqk/dot_general | solution.py:188
  390.6 16.7 %multiply_convert_fusion = bf16[8,12,128,512]{3,2,1,0:T(8,128)(2,1)S(1)} fusion(f32[8,12,128,512]{3,2,1,0:T(8,128)} %get-tuple-element.112, f32[8,12,128]{2,1,0:T(8,128)S(1)} %get-tuple-element.111, f32[8,12,128,512]{3,2,1,0:T(8,128)} %get-tuple-element.101, f32[8,12,128]{2,1,0:T(8,128)S(1)} %copy-done.37), kind=kLoop, calls=%fused_computation.1 | loop fusion | flops 25165824 | bytes 63012864 | tf_op jit(solution)/shard_map/convert_element_type | solution.py:195
  407.3 4.2 multiply_convert_fusion.1
  411.4 2.2 copy-done.2
  413.6 8.6 copy.70
  423.6 14.7 %fusion.25 = bf16[8,12,64,512]{3,2,1,0:T(8,128)(2,1)} fusion(bf16[8,128,12,64]{1,0,3,2:T(8,128)(2,1)S(1)} %bitcast.138, f32[8,12,128,512]{3,2,1,0:T(8,128)} %get-tuple-element.101, f32[8,12,128]{2,1,0:T(8,128)S(1)} %copy-done.37), kind=kOutput, calls=%fused_computation.44 | convolution fusion | flops 821035008 | bytes 33079296 | tf_op jit(solution)/shard_map/bhqk,bqhd->bkhd/dot_general | solution.py:191
  438.3 8.7 copy.72
  447.1 10.8 %convert_reduce_fusion.4 = (f32[12,64]{1,0:T(8,128)S(1)}, bf16[8,128,12,64]{1,3,2,0:T(8,128)(2,1)S(1)}) fusion(bf16[8,512,12,64]{1,3,2,0:T(8,128)(2,1)} %bitcast.117, bf16[8,12,128,512]{3,2,1,0:T(8,128)(2,1)} %copy-done.2), kind=kOutput, calls=%fused_computation.52 | convolution fusion | flops 808451328 | bytes 20450304 | tf_op jit(solution)/shard_map/bhqk,bkhd->bqhd/dot_general | solution.py:197
  459.9 2.8 fusion.38
  462.7 2.8 convolution_bitcast_fusion.2
  465.5 11.3 %fusion.78 = f32[768,3072]{1,0:T(8,128)} fusion(bf16[1024,3072]{1,0:T(8,128)(2,1)} %copy-done.11, f32[1024,768]{1,0:T(8,128)S(1)} %copy-done.7, f32[768]{0:T(1024)S(1)} %copy-done.32, f32[768]{0:T(1024)S(1)} %convert_element_type.131, f32[1024]{0:T(1024)S(1)} %fusion.72, f32[1024]{0:T(1024)S(1)} %broadcast_multiply_fusion.2), kind=kOutput, calls=%fused_computation.148 | convolution fusion | flops 4835770368 | bytes 18888704 | tf_op jit(solution)/shard_map/nd,ne->de/dot_general | solution.py:66
  476.8 7.7 fusion.94
  484.6 4.3 convolution_bitcast_fusion.1
  488.8 52.0 %reduce-scatter.8.cloned.1.call-done = bf16[8,128,768]{2,1,0:T(8,128)(2,1)} async-done(((bf16[8,512,768]{2,1,0:T(8,128)(2,1)}), bf16[8,128,768]{2,1,0:T(8,128)(2,1)}) %reduce-scatter.8.cloned.1.call-update) | async-done | bytes 1572880 | tf_op jit(solution)/shard_map/reduce_scatter | solution.py:210
  540.8 4.3 convolution_bitcast_fusion
  547.2 5.0 fusion.36
  552.5 43.0 %all-reduce = (f32[]{:T(128)}, f32[768]{0:T(1024)}, f32[768]{0:T(1024)}, f32[768]{0:T(1024)}, f32[768]{0:T(1024)}, /*index=5*/f32[768]{0:T(1024)}, f32[3072]{0:T...) all-reduce(f32[]{:T(128)S(6)} %div.94, ...), channel_id=1, replica_groups=mesh['seq'=4,'rows'=8] {'seq','rows'}, use_global_device_ids=true, to_apply=%region_13.14 | all-reduce | flops 9217 | bytes 73736 | tf_op jit(solution)/shard_map/psum | solution.py:245
  596.2 3.3 fusion.93
  600.5 3.1 add_add_fusion.2
  603.6 381.0 %all-reduce.7.cloned.1.call-done = (f32[768,768]{0,1:T(8,128)}, f32[768,768]{0,1:T(8,128)}, f32[768,768]{0,1:T(8,128)}, f32[768,768]{1,0:T(8,128)}, f32[768,3072]{1,0:T(8,128)}, /*index=5*/f32[3072,768]{1,0:T(8,128)}) async-done(((f32[768,768]{0,1:T(8,128)}, f32[768,768]{0,1:T(8,128)}, f32[768,768]{0,1:T(8,128)}, f32[768,768]{1,0:T(8,128)}, f32[768,3072]{1,0:T(8,128)}, /*index=5*/f32[3072,768]{1,0:T(8,128)}), ...) | async-done | bytes 28311568 | tf_op jit(solution)/shard_map/psum | solution.py:245
  984.6 3.2 copy.75
  987.8 1.9 copy.76
  989.7 3.2 copy.77
  994.3 9.3 copy.131
  1003.7 3.7 copy.132
  (233 shorter events, 36.9 us)
Async XLA Ops:
  7.2 124.7 %copy-start = (bf16[768,768]{1,0:T(8,128)(2,1)S(1)}, bf16[768,768]{1,0:T(8,128)(2,1)}, u32[]{:S(2)}) copy-start(bf16[768,768]{1,0:T(8,128)(2,1)} %param.24) | copy-start | bytes 3538948
  7.2 53.8 %all-gather.6.cloned.1.call-start = ((), (), s32[]{:S(2)}) async-start(), calls=%async_computation.4 | async-start | bytes 7864320 | tf_op jit(solution)/shard_map/all_gather | solution.py:117
  7.3 4.5 copy-start.56
  7.3 4.5 copy-start.27
  11.7 97.8 %all-gather.4.cloned.1.call-start = ((), (), s32[]{:S(2)}) async-start(), calls=%async_computation.3 | async-start | bytes 7864320 | tf_op jit(solution)/shard_map/all_gather | solution.py:118
  11.8 4.7 copy-start.48
  11.8 4.7 copy-start.58
  11.8 4.7 copy-start.59
  15.8 194.8 %all-reduce.5.cloned.1.call-start = ((), (), s32[]{:S(2)}) async-start(), calls=%async_computation.5 | async-start | bytes 393216 | tf_op jit(solution)/shard_map/psum | solution.py:157
  19.7 4.7 copy-start.63
  19.7 5.3 copy-start.29
  23.7 45.9 %copy-start.12 = (bf16[96,8,8,128]{3,2,1,0:T(8,128)(2,1)}, bf16[96,8,8,128]{3,2,1,0:T(8,128)(2,1)S(1)}, u32[]{:S(2)}) copy-start(bf16[96,8,8,128]{3,2,1,0:T(8,128)(2,1)S(1)} %copy.80) | copy-start | bytes 4718596
  23.7 146.0 %copy-start.31 = (f32[768]{0:T(1024)}, f32[768]{0:T(1024)S(1)}, u32[]{:S(2)}) copy-start(f32[768]{0:T(1024)S(1)} %convert_element_type.132) | copy-start | bytes 9220
  85.8 32.3 %copy-start.36 = (f32[8,12,128]{2,1,0:T(8,128)}, f32[8,12,128]{2,1,0:T(8,128)S(1)}, u32[]{:S(2)}) copy-start(f32[8,12,128]{2,1,0:T(8,128)S(1)} %get-tuple-element.100) | copy-start | bytes 147460
  132.0 37.7 %slice-start.3 = ((s8[4718592]{0:T(1024)(128)(4,1)}), s8[4194304]{0:T(1024)(128)(4,1)S(1)}, s32[]{:S(2)}) async-start(s8[4718592]{0:T(1024)(128)(4,1)} %bitcast.139), calls=%async_computation.14 | async-start | bytes 8388608
  133.7 36.0 %copy-start.5 = (f32[1024,768]{1,0:T(8,128)}, f32[1024,768]{1,0:T(8,128)S(1)}, u32[]{:S(2)}) copy-start(f32[1024,768]{1,0:T(8,128)S(1)} %get-tuple-element.103) | copy-start | bytes 9437188
  134.9 34.9 %copy-start.52 = (f32[768]{0:T(1024)S(1)}, f32[768]{0:T(1024)}, u32[]{:S(2)}) copy-start(f32[768]{0:T(1024)} %convert_element_type.136) | copy-start | bytes 9220
  134.9 34.9 %slice-start.4 = ((s8[4718592]{0:T(1024)(128)(4,1)}), s8[524288]{0:T(1024)(128)(4,1)S(1)}, s32[]{:S(2)}) async-start(s8[4718592]{0:T(1024)(128)(4,1)} %bitcast.139), calls=%async_computation.15 | async-start | bytes 1048576
  169.7 5.5 copy-start.66
  178.8 78.9 %all-gather.8.cloned.1.call-start = ((), (), s32[]{:S(2)}) async-start(), calls=%async_computation.6 | async-start | bytes 1769472 | tf_op jit(solution)/shard_map/all_gather | solution.py:159
  212.3 119.5 %reduce-scatter.4.cloned.1.call-start = ((), (), s32[]{:S(2)}) async-start(), calls=%async_computation.7 | async-start | bytes 1769472 | tf_op jit(solution)/shard_map/reduce_scatter | solution.py:168
  212.4 50.4 %copy-start.49 = (s32[64]{0:T(128)S(1)}, s32[64]{0:T(128)}, u32[]{:S(2)}) copy-start(s32[64]{0:T(128)} %param.35) | copy-start | bytes 772
  260.9 5.4 copy-start.10
  268.0 216.6 %reduce-scatter.6.cloned.1.call-start = ((), (), s32[]{:S(2)}) async-start(), calls=%async_computation.8 | async-start | bytes 7864320 | tf_op jit(solution)/shard_map/reduce_scatter | solution.py:207
  336.5 15.7 %slice-start.9 = ((s8[4718592]{0:T(1024)(128)(4,1)}), s8[4194304]{0:T(1024)(128)(4,1)S(1)}, s32[]{:S(2)}) async-start(s8[4718592]{0:T(1024)(128)(4,1)} %bitcast.145), calls=%async_computation.20 | async-start | bytes 8388608
  339.2 12.9 %copy-start.23 = (bf16[1024,768]{1,0:T(8,128)(2,1)}, bf16[1024,768]{1,0:T(8,128)(2,1)S(1)}, u32[]{:S(2)}) copy-start(bf16[1024,768]{1,0:T(8,128)(2,1)S(1)} %get-tuple-element.93) | copy-start | bytes 4718596
  339.3 12.9 %copy-start.6 = (f32[1024,768]{1,0:T(8,128)S(1)}, f32[1024,768]{1,0:T(8,128)}, u32[]{:S(2)}) copy-start(f32[1024,768]{1,0:T(8,128)} %copy-done.5) | copy-start | bytes 9437188
  339.3 12.9 %slice-start.10 = ((s8[4718592]{0:T(1024)(128)(4,1)}), s8[524288]{0:T(1024)(128)(4,1)S(1)}, s32[]{:S(2)}) async-start(s8[4718592]{0:T(1024)(128)(4,1)} %bitcast.145), calls=%async_computation.21 | async-start | bytes 1048576
  352.1 6.4 copy-start.11
  368.6 22.0 %copy-start.21 = (bf16[96,8,8,128]{3,2,1,0:T(8,128)(2,1)}, bf16[96,8,8,128]{3,2,1,0:T(8,128)(2,1)S(1)}, u32[]{:S(2)}) copy-start(bf16[96,8,8,128]{3,2,1,0:T(8,128)(2,1)S(1)} %copy.82) | copy-start | bytes 4718596
  390.6 16.7 %copy-start.13 = (bf16[96,8,8,128]{3,2,1,0:T(8,128)(2,1)S(1)}, bf16[96,8,8,128]{3,2,1,0:T(8,128)(2,1)}, u32[]{:S(2)}) copy-start(bf16[96,8,8,128]{3,2,1,0:T(8,128)(2,1)} %copy-done.12) | copy-start | bytes 4718596
  407.3 6.4 copy-start.2
  422.3 118.6 %reduce-scatter.8.cloned.1.call-start = ((), (), s32[]{:S(2)}) async-start(), calls=%async_computation.9 | async-start | bytes 7864320 | tf_op jit(solution)/shard_map/reduce_scatter | solution.py:210
  447.1 537.5 %all-reduce.7.cloned.1.call-start = ((), (), s32[]{:S(2)}) async-start(), calls=%async_computation.10 | async-start | bytes 56623104 | tf_op jit(solution)/shard_map/psum | solution.py:245
  462.7 14.1 %slice-start.11 = ((s8[6291456]{0:T(1024)(128)(4,1)}), s8[4194304]{0:T(1024)(128)(4,1)S(1)}, s32[]{:S(2)}) async-start(s8[6291456]{0:T(1024)(128)(4,1)} %bitcast.153), calls=%async_computation.22 | async-start | bytes 8388608
  465.5 11.3 %copy-start.24 = (bf16[1024,768]{1,0:T(8,128)(2,1)S(1)}, bf16[1024,768]{1,0:T(8,128)(2,1)}, u32[]{:S(2)}) copy-start(bf16[1024,768]{1,0:T(8,128)(2,1)} %copy-done.23) | copy-start | bytes 4718596
  465.5 11.3 %slice-start.12 = ((s8[6291456]{0:T(1024)(128)(4,1)}), s8[2097152]{0:T(1024)(128)(4,1)S(1)}, s32[]{:S(2)}) async-start(s8[6291456]{0:T(1024)(128)(4,1)} %bitcast.153), calls=%async_computation.23 | async-start | bytes 4194304
  547.1 5.0 copy-start.14
  547.1 5.3 copy-start.42
  547.1 5.3 copy-start.43
  547.1 5.3 copy-start.44
  547.1 5.3 copy-start.46
  547.1 5.3 copy-start.47
  547.2 5.3 copy-start.50
  547.2 5.3 copy-start.51
  992.9 10.7 %slice-start = ((s8[9437184]{0:T(1024)(128)(4,1)}), s8[4194304]{0:T(1024)(128)(4,1)S(1)}, s32[]{:S(2)}) async-start(s8[9437184]{0:T(1024)(128)(4,1)} %bitcast.120), calls=%async_computation.11 | async-start | bytes 8388608
  994.3 9.3 slice-start.1
  994.3 9.3 slice-start.2
  (40 other events, 99.8 us)
Sparse Core Ops, SparseCore 0:
  11.8 49.0 all-gather.5
  63.1 46.3 all-gather.3
  178.9 31.6 all-reduce.4
  213.5 44.1 all-gather.7
  268.1 63.6 reduce-scatter.3
  422.4 57.3 reduce-scatter.5
  482.4 58.3 reduce-scatter.7
  548.4 436.1 all-reduce.6
where the time goes:
time: 1020 us
  waiting for transfers between devices  632 us (62%)
  matrix products  210 us (21%)
  local copies, waits for them, and re-layouts  77 us (8%)
  blocking collectives  43 us (4%)
  other arithmetic  35.6 us (3%)
  between operations  18.1 us (2%)
    psum x1, waiting for transfers between devices, local(): lax.psum((g_query_w, g_query_b, g_key_w, g_value_w, g_value_b, g_output_w...  381 us
    reduce_scatter x1, waiting for transfers between devices, local(): lax.psum_scatter(pooled_grad, 'rows', scatter_dimension=0, tiled=True)  63.7 us
    reduce_scatter x1, waiting for transfers between devices, local(): lax.psum_scatter(value_grad_all.astype(jnp.bfloat16), 'seq', scatter_dime...  52 us
    all_gather x1, waiting for transfers between devices, local(): all_pooled = lax.all_gather(pooled_group_rows, 'rows', axis=0, tiled=True)  45.3 us
    psum x1, blocking collectives, local(): lax.psum((g_query_w, g_query_b, g_key_w, g_value_w, g_value_b, g_output_w...  43 us
    unnamed x168, local copies, waits for them, and re-layouts  36.2 us
    all_gather x1, waiting for transfers between devices, local(): lax.all_gather(key_local, 'seq', axis=1, tiled=True)  35 us
    dot_general x1, matrix products, local(): jnp.dot(hidden_low, inner_weight, preferred_element_type=jnp.float32)  34.8 us
  transfers between devices with their start and end apart: 8, of which 7 were waited for; matrix products, arithmetic and copies ran while one was open for 11% of the time, Pallas kernels for 0%

commit v1 on v0

v1 whole, which is shorter than its diff:
```python
import jax
import jax.numpy as jnp
from jax import lax
from jax.sharding import PartitionSpec as P

HEADS = 12
SEG_ROW = 8
HIGHEST = lax.Precision.HIGHEST
NORM_EPS = 1e-12
POOL_EPS = 1e-06
INV_TEMPER = 100.0
MASKED = -1000000000.0
INV_ROOT_TWO_PI = 0.3989422804014327
INV_ROOT_TWO = 0.7071067811865476
BF = jnp.bfloat16
F32 = jnp.float32


def exchange(array, partner):
    seqs, rows = lax.axis_size("seq"), lax.axis_size("rows")
    pairs = []
    for s in range(seqs):
        for r in range(rows):
            to_s, to_r = partner(s, r)
            pairs.append((s * rows + r, to_s * rows + to_r))
    return lax.ppermute(array, ("seq", "rows"), pairs)


def halving_steps():
    seq, row = lax.axis_index("seq"), lax.axis_index("rows")
    core = seq % 2
    seq_bit, row_bit = seq // 2 % 2, row % 2

    def first(s, r):
        return (s, r ^ 1) if s % 2 == 0 else (s ^ 2, r)

    def second(s, r):
        return (s ^ 2, r) if s % 2 == 0 else (s, r ^ 1)

    steps = [
        (lambda s, r: (s ^ 1, r), core),
        (first, jnp.where(core == 0, row_bit, seq_bit)),
        (second, jnp.where(core == 0, seq_bit, row_bit)),
    ]
    step = 2
    while step < lax.axis_size("rows"):
        steps.append((lambda s, r, step=step: (s, r ^ step), row // step % 2))
        step *= 2
    return steps


def half(array, bit):
    size = array.shape[0] // 2
    return lax.dynamic_slice_in_dim(array, bit * size, size, 0)


def reduce_scatter(array):
    for partner, bit in halving_steps():
        sent = half(array, 1 - bit)
        came = exchange(sent, partner)
        array = (half(array, bit).astype(F32) + came.astype(F32)).astype(BF)
    return array


def all_gather(array):
    for partner, bit in reversed(halving_steps()):
        came = exchange(array, partner)
        array = jnp.where(
            bit == 0,
            jnp.concatenate([array, came], axis=0),
            jnp.concatenate([came, array], axis=0),
        )
    return array


def all_sum_small(array):
    for partner, _ in halving_steps():
        array = array + exchange(array, partner)
    return array


def gather_embeddings(own):
    return lax.all_gather(own, ("rows", "seq"), axis=0, tiled=True)


def layer_norm(resid, gain, shift):
    center = resid - jnp.mean(resid, axis=-1, keepdims=True)
    spread = jnp.mean(center * center, axis=-1, keepdims=True)
    scale = lax.rsqrt(spread + NORM_EPS)
    xhat = center * scale
    return xhat * gain + shift, xhat, scale


def norm_back(grad, gain, xhat, scale):
    q = grad * gain
    return scale * (
        q - jnp.mean(q, axis=-1, keepdims=True) - xhat * jnp.mean(q * xhat, axis=-1, keepdims=True)
    )


def dot(a, b):
    return jnp.dot(a, b, preferred_element_type=F32)


def dot_t(a, b):
    return lax.dot_general(a, b, (((1,), (1,)), ((), ())), preferred_element_type=F32)


def t_dot(a, b):
    return lax.dot_general(a, b, (((0,), (0,)), ((), ())), preferred_element_type=F32)


def contrast(pooled, own_pooled, own_start, positives_all, own_positives):
    def normalized(e):
        rho = lax.rsqrt(jnp.sum(e * e, axis=1, keepdims=True) + POOL_EPS)
        return e * rho, rho

    n_all, _ = normalized(pooled)
    n_own, rho = normalized(own_pooled)
    total, own = pooled.shape[0], own_pooled.shape[0]
    col = jnp.arange(total, dtype=jnp.int32)
    row_own = jnp.arange(own, dtype=jnp.int32) + own_start
    c_all = jnp.dot(n_all, n_all.T, precision=HIGHEST) * INV_TEMPER
    c_all = jnp.where(col[None, :] == col[:, None], MASKED, c_all)
    top = jnp.max(c_all, axis=1)
    lse = jnp.log(jnp.sum(jnp.exp(c_all - top[:, None]), axis=1)) + top
    c_own = lax.dynamic_slice_in_dim(c_all, own_start, own, 0)
    lse_own = lax.dynamic_slice_in_dim(lse, own_start, own, 0)
    chosen = col[None, :] == own_positives[:, None]
    loss = jnp.sum(lse_own - jnp.sum(jnp.where(chosen, c_own, 0.0), axis=1))
    weight = (
        jnp.exp(c_own - lse_own[:, None])
        + jnp.exp(c_own - lse[None, :])
        - chosen.astype(F32)
        - (positives_all[None, :] == row_own[:, None]).astype(F32)
    )
    d_n = INV_TEMPER * jnp.dot(weight, n_all, precision=HIGHEST)
    d_e = rho * d_n - rho**3 * own_pooled * jnp.sum(own_pooled * d_n, axis=1, keepdims=True)
    return loss, d_e


def local(
    tokens,
    query_weight,
    query_bias,
    key_weight,
    value_weight,
    value_bias,
    output_weight,
    output_bias,
    attn_gain,
    attn_shift,
    inner_weight,
    inner_bias,
    outer_weight,
    outer_bias,
    ffn_gain,
    ffn_shift,
    segment_ids,
    positives,
):
    group_rows, local_len, width = tokens.shape
    ff = inner_weight.shape[1]
    seqs = lax.axis_size("seq")
    seq, row_place = lax.axis_index("seq"), lax.axis_index("rows")
    head_dim = width // HEADS
    scale = head_dim ** (-0.5)
    batch, length = group_rows // seqs, local_len * seqs
    count = batch * length
    ids = lax.dynamic_slice_in_dim(segment_ids, seq * batch, batch, 0)
    own_segs = batch * SEG_ROW
    own_positives = lax.dynamic_slice_in_dim(positives, seq * own_segs, own_segs, 0)
    positives_all = lax.all_gather(positives, "rows", axis=0, tiled=True)
    own_start = row_place * positives.shape[0] + seq * own_segs

    flat = lax.all_to_all(tokens, "seq", split_axis=0, concat_axis=1, tiled=True)
    flat = flat.reshape(count, width)
    f = lambda v: v.astype(F32)
    q = (dot(flat, query_weight) + f(query_bias)).astype(BF)
    k = dot(flat, key_weight).astype(BF)
    v = (dot(flat, value_weight) + f(value_bias)).astype(BF)
    heads = lambda a: a.reshape(batch, length, HEADS, head_dim)
    q4, k4, v4 = heads(q), heads(k), heads(v)
    raw = jnp.einsum("bqhd,bkhd->bhqk", q4, k4, preferred_element_type=F32) * scale
    same = ids[:, None, :, None] == ids[:, None, None, :]
    raw = jnp.where(same, raw, MASKED)
    expo = jnp.exp(raw - jnp.max(raw, axis=-1, keepdims=True))
    probs = expo / jnp.sum(expo, axis=-1, keepdims=True)
    probs_low = probs.astype(BF)
    o = jnp.einsum("bhqk,bkhd->bqhd", probs_low, v4, preferred_element_type=F32)
    o = o.astype(BF).reshape(count, width)
    resid_one = f(flat) + dot(o, output_weight) + f(output_bias)
    hidden, xhat_one, scale_one = layer_norm(resid_one, f(attn_gain), f(attn_shift))
    hidden_low = hidden.astype(BF)
    inner = dot(hidden_low, inner_weight) + f(inner_bias)
    cdf = 0.5 * (1.0 + lax.erf(inner * INV_ROOT_TWO))
    active = (inner * cdf).astype(BF)
    slope = (cdf + inner * jnp.exp(-0.5 * inner * inner) * INV_ROOT_TWO_PI).astype(BF)
    resid_two = hidden + dot(active, outer_weight) + f(outer_bias)
    _, xhat_two, scale_two = layer_norm(resid_two, f(ffn_gain), f(ffn_shift))
    onehot = (ids[:, :, None] == jnp.arange(SEG_ROW, dtype=jnp.int32)).astype(F32)
    counts = jnp.sum(onehot, axis=1).reshape(own_segs, 1)
    pooled_xhat = (
        jnp.einsum("bls,bld->bsd", onehot, xhat_two.reshape(batch, length, width), precision=HIGHEST)
        .reshape(own_segs, width) / counts
    )
    own_pooled = pooled_xhat * f(ffn_gain) + f(ffn_shift)
    pooled = gather_embeddings(own_pooled)
    loss, d_e = contrast(pooled, own_pooled, own_start, positives_all, own_positives)

    g_ffn_gain = jnp.sum(d_e * pooled_xhat, axis=0)
    g_ffn_shift = jnp.sum(d_e, axis=0)
    d_y = jnp.einsum(
        "bls,bsd->bld", onehot, (d_e / counts).reshape(batch, SEG_ROW, width), precision=HIGHEST
    ).reshape(count, width)
    d_two = norm_back(d_y, f(ffn_gain), xhat_two, scale_two)
    d_outer = d_two.astype(BF)
    g_outer = t_dot(active, d_outer).astype(BF)
    part_outer = reduce_scatter(g_outer)
    d_inner = (dot_t(d_outer, outer_weight) * f(slope)).astype(BF)
    g_inner = jnp.concatenate(
        [t_dot(hidden_low, d_inner[:, i * width : (i + 1) * width]) for i in range(ff // width)], axis=0
    ).astype(BF)
    part_inner = reduce_scatter(g_inner)
    d_hidden = d_two + dot_t(d_inner, inner_weight)
    d_one = norm_back(d_hidden, f(attn_gain), xhat_one, scale_one)
    d_attn = d_one.astype(BF)
    g_output = t_dot(o, d_attn)
    d_o = dot_t(d_attn, output_weight).astype(BF)
    d_o4 = heads(d_o)
    d_probs = jnp.einsum("bqhd,bkhd->bhqk", d_o4, v4, preferred_element_type=F32)
    d_v = jnp.einsum("bhqk,bqhd->bkhd", probs_low, d_o4, preferred_element_type=F32)
    d_s = (probs * (d_probs - jnp.sum(d_probs * probs, axis=-1, keepdims=True))).astype(BF)
    d_q = jnp.einsum("bhqk,bkhd->bqhd", d_s, k4, preferred_element_type=F32) * scale
    d_k = jnp.einsum("bhqk,bqhd->bkhd", d_s, q4, preferred_element_type=F32) * scale
    d_q, d_k, d_v = (a.astype(BF).reshape(count, width) for a in (d_q, d_k, d_v))
    g_attn = jnp.concatenate(
        [t_dot(flat, d_q), t_dot(flat, d_k), t_dot(flat, d_v), g_output], axis=0
    ).astype(BF)
    part_attn = reduce_scatter(g_attn)
    column = lambda a: jnp.sum(f(a), axis=0)
    small = jnp.concatenate(
        [
            column(d_q), column(d_v), column(d_attn),
            jnp.sum(d_hidden * xhat_one, axis=0), jnp.sum(d_hidden, axis=0),
            column(d_inner), column(d_outer), g_ffn_gain, g_ffn_shift,
            jnp.broadcast_to(loss, (width,)),
        ]
    ).reshape(-1, 128)
    small = all_sum_small(small).reshape(-1)
    token_grad = (
        d_one + dot_t(d_q, query_weight) + dot_t(d_k, key_weight) + dot_t(d_v, value_weight)
    ).astype(BF)
    grad_tokens = lax.all_to_all(
        token_grad.reshape(batch, length, width), "seq", split_axis=1, concat_axis=0, tiled=True
    ).astype(F32)
    sum_outer = all_gather(part_outer).astype(F32)
    sum_inner = all_gather(part_inner).astype(F32)
    sum_inner = jnp.concatenate(
        [sum_inner[i * width : (i + 1) * width] for i in range(ff // width)], axis=1
    )
    sum_attn = all_gather(part_attn).astype(F32)
    sizes = [width] * 5 + [ff] + [width] * 4
    pieces, at = [], 0
    for size in sizes:
        pieces.append(small[at : at + size])
        at += size
    qb, vb, ob, ag, ash, ib, wb, fg, fs, ls = pieces
    return (
        ls[0] / pooled.shape[0],
        grad_tokens,
        sum_attn[:width],
        qb,
        sum_attn[width : 2 * width],
        sum_attn[2 * width : 3 * width],
        vb,
        sum_attn[3 * width :],
        ob,
        ag,
        ash,
        sum_inner,
        ib,
        sum_outer,
        wb,
        fg,
        fs,
    )


def solution(mesh):
    placed = (
        (P("rows", "seq", None),) + (P(),) * 15 + (P("rows", None), P("rows"))
    )
    return jax.shard_map(
        local,
        mesh=mesh,
        in_specs=placed,
        out_specs=(P(), P("rows", "seq", None)) + (P(),) * 15,
        check_vma=False,
    )
```

time: 1020 us -> 558 us (0.55)
  waiting for transfers between devices: 632 us -> 156 us
  matrix products: 210 us -> 154 us
  starting transfers between devices: 0.33 us -> 55.4 us
  other arithmetic: 35.6 us -> 72.9 us
  blocking collectives: 43 us -> 12.8 us
    psum x2 -> x0, waiting for transfers between devices: 413 us -> none  [the longest x1 381 us: local(): lax.psum((g_query_w, g_query_b, g_key_w, g_value_w, g_value_b, g_output_w...]
    reduce_scatter x3 -> x0, waiting for transfers between devices: 116 us -> none  [the longest x1 63.7 us: local(): lax.psum_scatter(pooled_grad, 'rows', scatter_dimension=0, tiled=True)]
    ppermute x0 -> x35, waiting for transfers between devices: none -> 96.3 us  [exchange(): return lax.ppermute(array, ('seq', 'rows'), pairs)]
    all_gather x3 -> x1, waiting for transfers between devices: 104 us -> 41.4 us  [gather_embeddings(): return lax.all_gather(own, ('rows', 'seq'), axis=0, tiled=True)]
    dot_general x28 -> x30, matrix products: 193 us -> 138 us  [the longest x6 27.2 us: dot_t(): lax.dot_general(a, b, (((1,), (1,)), ((), ())), preferred_element_type=F32)]
    ppermute x0 -> x35, starting transfers between devices: none -> 46.6 us  [exchange(): return lax.ppermute(array, ('seq', 'rows'), pairs)]
    psum x1 -> x0, blocking collectives: 43 us -> none  [local(): lax.psum((g_query_w, g_query_b, g_key_w, g_value_w, g_value_b, g_output_w...]
    convert_element_type x10 -> x30, other arithmetic: 18.6 us -> 42.6 us  [the longest x1 17.4 us: local(): (probs * (d_probs - jnp.sum(d_probs * probs, axis=-1, keepdims=True))).as...]
  transfers between devices with their start and end apart: 8 -> 38, of which waited for: 7 -> 17; matrix products, arithmetic and copies ran while one was open for 11% -> 15% of each run, Pallas kernels for 0% -> 0%
where the time goes in v1:
time: 558 us; the launch traced here: 549 us
  waiting for transfers between devices  156 us (28%)
  matrix products  154 us (28%)
  local copies, waits for them, and re-layouts  79.1 us (14%)
  other arithmetic  72.9 us (13%)
  starting transfers between devices  55.4 us (10%)
  between operations  18.6 us (3%)
  blocking collectives  12.8 us (2%)
    ppermute x35, waiting for transfers between devices, exchange(): return lax.ppermute(array, ('seq', 'rows'), pairs)  96.3 us
    ppermute x35, starting transfers between devices, exchange(): return lax.ppermute(array, ('seq', 'rows'), pairs)  46.6 us
    all_gather x1, waiting for transfers between devices, gather_embeddings(): return lax.all_gather(own, ('rows', 'seq'), axis=0, tiled=True)  41.4 us
    unnamed x161, local copies, waits for them, and re-layouts  30.5 us
    dot_general x6, matrix products, dot_t(): lax.dot_general(a, b, (((1,), (1,)), ((), ())), preferred_element_type=F32)  27.2 us
    dot_general x6, matrix products, dot(): return jnp.dot(a, b, preferred_element_type=F32)  26.5 us
    dot_general x9, matrix products, t_dot(): lax.dot_general(a, b, (((0,), (0,)), ((), ())), preferred_element_type=F32)  23.5 us
    all_to_all x1, waiting for transfers between devices, local(): lax.all_to_all(tokens, 'seq', split_axis=0, concat_axis=1, tiled=True)  18.7 us
  transfers between devices with their start and end apart: 38, of which 17 were waited for; matrix products, arithmetic and copies ran while one was open for 15% of the time, Pallas kernels for 0%

profile of v1, /device:TPU:0, one launch (start us, length us, event | category | flops | bytes accessed | tf_op | source)
XLA Modules:
  0.0 549.2 jit_solution(638088488563738964)
XLA Ops:
  7.3 4.4 all-to-all-start
  13.1 18.7 %all-to-all-done = bf16[8,128,768]{2,1,0:T(8,128)(2,1)S(1)} async-done(((bf16[8,128,768]{2,1,0:T(8,128)(2,1)}), bf16[8,128,768]{2,1,0:T(8,128)(2,1)S(1)}, u32[]{:S(2)}, u32[]{:S(2)}) %all-to-all-start) | async-done | bytes 1572896 | tf_op jit(solution)/shard_map/all_to_all | solution.py:176
  39.5 4.8 add_convert_fusion.5
  46.9 3.8 reshape.229
  50.8 4.3 add_convert_fusion.4
  57.6 3.8 reshape.230
  61.5 15.6 %fusion.120 = (f32[2,12,512]{2,1,0:T(8,128)S(1)}, f32[2,12,512,512]{2,3,1,0:T(8,128)}) fusion(pred[2,512,512]{1,2,0:T(8,128)(4,1)S(1)} %broadcast_compare_fusion, bf16[2,512,12,64]{1,0,3,2:T(2,128)(2,1)S(1)} %reshape.228, bf16[2,512,12,64]{1,0,3,2:T(2,128)(2,1)} %reshape.229), kind=kOutput, calls=%fused_computation.235 | convolution fusion | flops 830472704 | bytes 28884992 | tf_op jit(solution)/shard_map/sub | solution.py:187
  77.1 11.0 %fusion.49 = bf16[2,512,12,64]{1,3,2,0:T(8,128)(2,1)S(1)} fusion(bf16[2,512,12,64]{1,0,3,2:T(2,128)(2,1)} %reshape.230, f32[2,12,512,512]{2,3,1,0:T(8,128)} %get-tuple-element.50, f32[2,12,512]{2,1,0:T(8,128)S(1)} %get-tuple-element.49), kind=kOutput, calls=%fused_computation.93 | convolution fusion | flops 818675712 | bytes 28360704 | tf_op jit(solution)/shard_map/bhqk,bkhd->bqhd/dot_general | solution.py:190
  94.0 8.9 %multiply_convert_fusion.2 = (bf16[1024,3072]{1,0:T(8,128)(2,1)S(1)}, f32[1024,3072]{1,0:T(8,128)}) fusion(f32[3072]{0:T(1024)S(1)} %convert_element_type.298, bf16[1024,768]{1,0:T(8,128)(2,1)S(1)} %fusion.19, bf16[768,3072]{1,0:T(8,128)(2,1)S(1)} %bitcast.170), kind=kOutput, calls=%fused_computation.14 | convolution fusion | flops 4850712576 | bytes 25178112 | tf_op jit(solution)/shard_map/dot_general | solution.py:102
  103.0 5.4 fusion.130
  113.5 12.8 %all-reduce = s32[512]{0:T(512)S(1)} all-reduce(s32[512]{0:T(512)S(1)} %dynamic-update-slice), channel_id=1, replica_groups=mesh['seq'=4,'rows'=8] {'rows'}, use_global_device_ids=true, to_apply=%add | all-reduce | flops 512 | bytes 4096
  126.6 41.4 %all-gather.2.cloned.1.call-done = f32[512,768]{1,0:T(8,128)} async-done(((f32[16,768]{1,0:T(8,128)}), f32[512,768]{1,0:T(8,128)}) %all-gather.2.cloned.1.call-update) | async-done | bytes 1572880 | tf_op jit(solution)/shard_map/all_gather | solution.py:83
  169.7 4.9 fusion.131
  182.3 13.5 %convert_reduce_fusion = (f32[3072]{0:T(1024)}, bf16[1024,3072]{1,0:T(8,128)(2,1)S(1)}) fusion(f32[1024,3072]{1,0:T(8,128)} %get-tuple-element.54, f32[3072]{0:T(1024)S(1)} %convert_element_type.298, bf16[3072,768]{1,0:T(8,128)(2,1)S(1)} %bitcast.168, f32[1024,768]{1,0:T(8,128)S(1)} %get-tuple-element.27), kind=kOutput, calls=%fused_computation.12 | convolution fusion | flops 4879807488 | bytes 26763264 | tf_op jit(solution)/shard_map/dot_general | solution.py:106
  195.7 6.5 %multiply_reduce_fusion.1 = (f32[768]{0:T(1024)}, f32[1024]{0:T(1024)S(1)}, f32[1024]{0:T(1024)S(1)}, f32[768]{0:T(1024)S(1)}, f32[1024,768]{1,0:T(8,128)S(1)}) fusion(f32[1024,768]{1,0:T(8,128)S(1)} %copy-done.6, f32[1024]{0:T(1024)S(1)} %add_rsqrt_fusion.1, f32[1024]{0:T(1024)S(1)} %broadcast_multiply_fusion.4, f32[768]{0:T(1024)S(1)} %convert_element_type.295, ...), kind=kOutput, calls=%fused_computation.43 | convolution fusion | flops 4839698432 | bytes 20472832 | tf_op jit(solution)/shard_map/dot_general | solution.py:106
  211.7 17.8 %multiply_reduce_fusion = (f32[2,12,512]{2,1,0:T(8,128)S(1)}, f32[2,12,512,512]{2,3,1,0:T(8,128)}) fusion(f32[2,12,512,512]{2,3,1,0:T(8,128)} %get-tuple-element.50, f32[2,12,512]{2,1,0:T(8,128)S(1)} %get-tuple-element.49, bf16[2,512,12,64]{1,0,3,2:T(2,128)(2,1)} %reshape.230, bf16[2,512,12,64]{1,0,3,2:T(2,128)(2,1)} %reshape.236), kind=kOutput, calls=%fused_computation.2 | convolution fusion | flops 824168448 | bytes 53575680 | tf_op jit(solution)/shard_map/bqhd,bkhd->bhqk/dot_general | solution.py:231
  229.5 12.2 %convert_reduce_fusion.3 = (f32[12,64]{1,0:T(8,128)}, bf16[2,512,12,64]{1,3,2,0:T(8,128)(2,1)}) fusion(f32[2,12,512,512]{2,3,1,0:T(8,128)} %get-tuple-element.50, f32[2,12,512]{2,1,0:T(8,128)S(1)} %get-tuple-element.49, bf16[2,512,12,64]{1,0,3,2:T(2,128)(2,1)S(1)} %copy-done.29), kind=kOutput, calls=%fused_computation.45 | convolution fusion | flops 820247808 | bytes 28363776 | tf_op jit(solution)/shard_map/bhqk,bqhd->bkhd/dot_general | solution.py:232
  241.7 17.4 %multiply_convert_fusion = bf16[2,12,512,512]{2,3,1,0:T(8,128)(2,1)S(1)} fusion(f32[2,12,512,512]{2,3,1,0:T(8,128)} %get-tuple-element.67, f32[2,12,512]{2,1,0:T(8,128)S(1)} %get-tuple-element.66, f32[2,12,512,512]{2,3,1,0:T(8,128)} %get-tuple-element.50, f32[2,12,512]{2,1,0:T(8,128)S(1)} %get-tuple-element.49), kind=kLoop, calls=%fused_computation.1 | loop fusion | flops 25165824 | bytes 63012864 | tf_op jit(solution)/shard_map/convert_element_type | solution.py:233
  259.1 4.6 copy-done.2
  265.9 8.6 %fusion.53 = bf16[2,512,12,64]{1,3,2,0:T(8,128)(2,1)S(1)} fusion(bf16[2,12,512,512]{2,3,1,0:T(8,128)(2,1)} %copy-done.2, bf16[2,512,12,64]{1,0,3,2:T(2,128)(2,1)S(1)} %copy-done.17), kind=kOutput, calls=%fused_computation.95 | convolution fusion | flops 806879232 | bytes 15728640 | tf_op jit(solution)/shard_map/bhqk,bqhd->bkhd/dot_general | solution.py:235
  274.5 2.9 convolution_convert_fusion.3
  277.5 3.0 fusion.43
  280.5 3.0 fusion.40
  308.5 7.2 %convolution_convert_fusion = bf16[3072,768]{1,0:T(8,128)(2,1)} fusion(bf16[1024,3072]{1,0:T(8,128)(2,1)S(1)} %bitcast.176, f32[1024,768]{1,0:T(8,128)S(1)} %copy-done.19), kind=kOutput, calls=%fused_computation.25 | convolution fusion | flops 4834983936 | bytes 14155776 | tf_op jit(solution)/shard_map/dot_general | solution.py:110
  328.8 3.0 add_convert_fusion.2
  337.1 11.2 %collective-permute-done.6 = bf16[768,768]{1,0:T(8,128)(2,1)S(1)} collective-permute-done((bf16[768,768]{1,0:T(8,128)(2,1)S(1)}, bf16[768,768]{1,0:T(8,128)(2,1)S(1)}, u32[]{:S(2)}, u32[]{:S(2)}) %collective-permute-start.6) | collective-permute-done | bytes 1179680 | tf_op jit(solution)/shard_map/ppermute | solution.py:26
  352.7 14.5 %collective-permute-done.16 = bf16[768,768]{1,0:T(8,128)(2,1)S(1)} collective-permute-done((bf16[768,768]{1,0:T(8,128)(2,1)S(1)}, bf16[768,768]{1,0:T(8,128)(2,1)S(1)}, u32[]{:S(2)}, u32[]{:S(2)}) %collective-permute-start.16) | collective-permute-done | bytes 1179680 | tf_op jit(solution)/shard_map/ppermute | solution.py:26
  369.8 16.3 %collective-permute-done.26 = bf16[768,768]{1,0:T(8,128)(2,1)S(1)} collective-permute-done((bf16[768,768]{1,0:T(8,128)(2,1)S(1)}, bf16[768,768]{1,0:T(8,128)(2,1)S(1)}, u32[]{:S(2)}, u32[]{:S(2)}) %collective-permute-start.26) | collective-permute-done | bytes 1179680 | tf_op jit(solution)/shard_map/ppermute | solution.py:26
  391.3 5.8 %collective-permute-done.9 = bf16[96,768]{1,0:T(8,128)(2,1)S(1)} collective-permute-done((bf16[96,768]{1,0:T(8,128)(2,1)S(1)}, bf16[96,768]{1,0:T(8,128)(2,1)S(1)}, u32[]{:S(2)}, u32[]{:S(2)}) %collective-permute-start.9) | collective-permute-done | bytes 147488 | tf_op jit(solution)/shard_map/ppermute | solution.py:26
  397.4 8.7 %collective-permute-done.10 = bf16[96,768]{1,0:T(8,128)(2,1)S(1)} collective-permute-done((bf16[96,768]{1,0:T(8,128)(2,1)S(1)}, bf16[96,768]{1,0:T(8,128)(2,1)S(1)}, u32[]{:S(2)}, u32[]{:S(2)}) %collective-permute-start.10) | collective-permute-done | bytes 147488 | tf_op jit(solution)/shard_map/ppermute | solution.py:26
  409.0 10.1 %collective-permute-done.11 = bf16[192,768]{1,0:T(8,128)(2,1)S(1)} collective-permute-done((bf16[192,768]{1,0:T(8,128)(2,1)S(1)}, bf16[192,768]{1,0:T(8,128)(2,1)S(1)}, u32[]{:S(2)}, u32[]{:S(2)}) %collective-permute-start.11) | collective-permute-done | bytes 294944 | tf_op jit(solution)/shard_map/ppermute | solution.py:26
  420.4 6.1 %collective-permute-done.28 = bf16[192,768]{1,0:T(8,128)(2,1)S(1)} collective-permute-done((bf16[192,768]{1,0:T(8,128)(2,1)S(1)}, bf16[192,768]{1,0:T(8,128)(2,1)S(1)}, u32[]{:S(2)}, u32[]{:S(2)}) %collective-permute-start.28) | collective-permute-done | bytes 294944 | tf_op jit(solution)/shard_map/ppermute | solution.py:26
  426.6 5.0 collective-permute-done.20
  439.6 5.0 collective-permute-start.22
  446.2 5.2 collective-permute-done.31
  453.9 3.1 collective-permute-start.23
  462.5 4.4 all-to-all-start.1
  474.2 3.7 maximum_select_fusion.4
  477.9 4.5 collective-permute-start.24
  484.3 5.2 collective-permute-done.2
  489.5 3.5 collective-permute-start.3
  497.0 2.9 collective-permute-done.4
  506.7 3.0 maximum_select_fusion.5
  509.8 3.6 collective-permute-start.34
  516.2 3.8 fusion.119
  520.0 4.7 fusion.15
  526.9 5.2 pad_maximum_fusion
  532.2 8.6 %fusion.16 = f32[3072,768]{1,0:T(8,128)} fusion(bf16[1536,768]{1,0:T(8,128)(2,1)} %collective-permute-done.34, bf16[1536,768]{1,0:T(8,128)(2,1)} %maximum_select_fusion.5, pred[]{:T(512)S(6)} %eq.153), kind=kLoop, calls=%fused_computation.33 | loop fusion | flops 23592960 | bytes 14155777 | tf_op jit(solution)/shard_map/convert_element_type | solution.py:257
  (349 shorter events, 147.0 us)
Async XLA Ops:
  7.2 82.9 %copy-start = (bf16[768,768]{1,0:T(8,128)(2,1)S(1)}, bf16[768,768]{1,0:T(8,128)(2,1)}, u32[]{:S(2)}) copy-start(bf16[768,768]{1,0:T(8,128)(2,1)} %param.24) | copy-start | bytes 3538948
  7.3 24.5 %all-to-all-start = ((bf16[8,128,768]{2,1,0:T(8,128)(2,1)}), bf16[8,128,768]{2,1,0:T(8,128)(2,1)S(1)}, u32[]{:S(2)}, u32[]{:S(2)}) async-start(bf16[8,128,768]{2,1,0:T(8,128)(2,1)} %param.18), calls=%async_computation | async-start | bytes 3145728 | tf_op jit(solution)/shard_map/all_to_all | solution.py:176
  11.7 156.4 %all-gather.2.cloned.1.call-start = ((), (), s32[]{:S(2)}) async-start(), calls=%async_computation.2 | async-start | bytes 1622016 | tf_op jit(solution)/shard_map/all_gather | solution.py:83
  39.5 22.0 %copy-start.12 = (bf16[2,512,12,64]{1,0,3,2:T(2,128)(2,1)}, bf16[2,512,12,64]{1,0,3,2:T(2,128)(2,1)S(1)}, u32[]{:S(2)}) copy-start(bf16[2,512,12,64]{1,0,3,2:T(2,128)(2,1)S(1)} %reshape.228) | copy-start | bytes 4718596
  180.1 15.6 %slice-start.10 = ((s8[4718592]{0:T(1024)(128)(4,1)}), s8[4194304]{0:T(1024)(128)(4,1)S(1)}, s32[]{:S(2)}) async-start(s8[4718592]{0:T(1024)(128)(4,1)} %bitcast.171), calls=%async_computation.13 | async-start | bytes 8388608
  182.2 13.5 %copy-start.18 = (f32[1024,768]{1,0:T(8,128)}, f32[1024,768]{1,0:T(8,128)S(1)}, u32[]{:S(2)}) copy-start(f32[1024,768]{1,0:T(8,128)S(1)} %get-tuple-element.27) | copy-start | bytes 9437188
  182.2 13.5 %copy-start.6 = (f32[1024,768]{1,0:T(8,128)S(1)}, f32[1024,768]{1,0:T(8,128)}, u32[]{:S(2)}) copy-start(f32[1024,768]{1,0:T(8,128)} %copy-done.5) | copy-start | bytes 9437188
  182.2 13.5 %slice-start.11 = ((s8[4718592]{0:T(1024)(128)(4,1)}), s8[524288]{0:T(1024)(128)(4,1)S(1)}, s32[]{:S(2)}) async-start(s8[4718592]{0:T(1024)(128)(4,1)} %bitcast.171), calls=%async_computation.14 | async-start | bytes 1048576
  211.7 17.8 %copy-start.29 = (bf16[2,512,12,64]{1,0,3,2:T(2,128)(2,1)S(1)}, bf16[2,512,12,64]{1,0,3,2:T(2,128)(2,1)}, u32[]{:S(2)}) copy-start(bf16[2,512,12,64]{1,0,3,2:T(2,128)(2,1)} %reshape.236) | copy-start | bytes 4718596
  241.7 21.9 %copy-start.13 = (bf16[2,512,12,64]{1,0,3,2:T(2,128)(2,1)S(1)}, bf16[2,512,12,64]{1,0,3,2:T(2,128)(2,1)}, u32[]{:S(2)}) copy-start(bf16[2,512,12,64]{1,0,3,2:T(2,128)(2,1)} %copy-done.12) | copy-start | bytes 4718596
  302.9 25.9 %collective-permute-start.5 = (bf16[1536,768]{1,0:T(8,128)(2,1)}, bf16[1536,768]{1,0:T(8,128)(2,1)}, u32[]{:S(2)}, u32[]{:S(2)}) collective-permute-start(bf16[1536,768]{1,0:T(8,128)(2,1)} %constant_dynamic-slice_fusion.14), channel_id=1, source_target_pairs={{0,8},{1,9},{2,10},{3,11},{4,12},{5,13},{6,14},{7,15},{8,0},{9,1},... | collective-permute-start | bytes 7077896 | tf_op jit(solution)/shard_map/ppermute | solution.py:26
  307.2 26.3 %collective-permute-start.15 = (bf16[1536,768]{1,0:T(8,128)(2,1)}, bf16[1536,768]{1,0:T(8,128)(2,1)S(1)}, u32[]{:S(2)}, u32[]{:S(2)}) collective-permute-start(bf16[1536,768]{1,0:T(8,128)(2,1)} %constant_dynamic-slice_fusion.9), channel_id=1, source_target_pairs={{0,8},{1,9},{2,10},{3,11},{4,12},{5,13},{6,14},{7,15},{8,0},{9,1},... | collective-permute-start | bytes 7077896 | tf_op jit(solution)/shard_map/ppermute | solution.py:26
  317.8 17.0 %collective-permute-start.25 = (bf16[1536,768]{1,0:T(8,128)(2,1)S(1)}, bf16[1536,768]{1,0:T(8,128)(2,1)S(1)}, u32[]{:S(2)}, u32[]{:S(2)}) collective-permute-start(bf16[1536,768]{1,0:T(8,128)(2,1)S(1)} %constant_dynamic-slice_fusion.4), channel_id=1, source_target_pairs={{0,8},{1,9},{2,10},{3,11},{4,12},{5,13},{6,14},{7,15},{8,0},{9,1},... | collective-permute-start | bytes 7077896 | tf_op jit(solution)/shard_map/ppermute | solution.py:26
  331.9 16.3 %collective-permute-start.6 = (bf16[768,768]{1,0:T(8,128)(2,1)S(1)}, bf16[768,768]{1,0:T(8,128)(2,1)S(1)}, u32[]{:S(2)}, u32[]{:S(2)}) collective-permute-start(bf16[768,768]{1,0:T(8,128)(2,1)S(1)} %constant_dynamic-slice_fusion.13), channel_id=1, source_target_pairs={{0,1},{1,0},{2,3},{3,2},{4,5},{5,4},{6,7},{7,6},{8,24},{9,25},{10,... | collective-permute-start | bytes 3538952 | tf_op jit(solution)/shard_map/ppermute | solution.py:26
  334.2 33.0 %collective-permute-start.16 = (bf16[768,768]{1,0:T(8,128)(2,1)S(1)}, bf16[768,768]{1,0:T(8,128)(2,1)S(1)}, u32[]{:S(2)}, u32[]{:S(2)}) collective-permute-start(bf16[768,768]{1,0:T(8,128)(2,1)S(1)} %constant_dynamic-slice_fusion.8), channel_id=1, source_target_pairs={{0,1},{1,0},{2,3},{3,2},{4,5},{5,4},{6,7},{7,6},{8,24},{9,25},{10,... | collective-permute-start | bytes 3538952 | tf_op jit(solution)/shard_map/ppermute | solution.py:26
  335.5 14.6 %copy-start.36 = (f32[768]{0:T(1024)S(1)}, f32[768]{0:T(1024)}, u32[]{:S(2)}) copy-start(f32[768]{0:T(1024)} %get-tuple-element.22) | copy-start | bytes 9220
  335.5 15.8 %copy-start.35 = (f32[768]{0:T(1024)S(1)}, f32[768]{0:T(1024)}, u32[]{:S(2)}) copy-start(f32[768]{0:T(1024)} %get-tuple-element.21) | copy-start | bytes 9220
  335.6 50.6 %collective-permute-start.26 = (bf16[768,768]{1,0:T(8,128)(2,1)S(1)}, bf16[768,768]{1,0:T(8,128)(2,1)S(1)}, u32[]{:S(2)}, u32[]{:S(2)}) collective-permute-start(bf16[768,768]{1,0:T(8,128)(2,1)S(1)} %constant_dynamic-slice_fusion.3), channel_id=1, source_target_pairs={{0,1},{1,0},{2,3},{3,2},{4,5},{5,4},{6,7},{7,6},{8,24},{9,25},{10,... | collective-permute-start | bytes 3538952 | tf_op jit(solution)/shard_map/ppermute | solution.py:26
  348.6 20.5 %collective-permute-start.7 = (bf16[384,768]{1,0:T(8,128)(2,1)S(1)}, bf16[384,768]{1,0:T(8,128)(2,1)S(1)}, u32[]{:S(2)}, u32[]{:S(2)}) collective-permute-start(bf16[384,768]{1,0:T(8,128)(2,1)S(1)} %constant_dynamic-slice_fusion.12), channel_id=1, source_target_pairs={{0,16},{1,17},{2,18},{3,19},{4,20},{5,21},{6,22},{7,23},{8,9},{9,8... | collective-permute-start | bytes 1769480 | tf_op jit(solution)/shard_map/ppermute | solution.py:26
  367.5 21.5 %collective-permute-start.17 = (bf16[384,768]{1,0:T(8,128)(2,1)S(1)}, bf16[384,768]{1,0:T(8,128)(2,1)S(1)}, u32[]{:S(2)}, u32[]{:S(2)}) collective-permute-start(bf16[384,768]{1,0:T(8,128)(2,1)S(1)} %constant_dynamic-slice_fusion.7), channel_id=1, source_target_pairs={{0,16},{1,17},{2,18},{3,19},{4,20},{5,21},{6,22},{7,23},{8,9},{9,8... | collective-permute-start | bytes 1769480 | tf_op jit(solution)/shard_map/ppermute | solution.py:26
  369.2 18.8 %collective-permute-start.8 = (bf16[192,768]{1,0:T(8,128)(2,1)S(1)}, bf16[192,768]{1,0:T(8,128)(2,1)S(1)}, u32[]{:S(2)}, u32[]{:S(2)}) collective-permute-start(bf16[192,768]{1,0:T(8,128)(2,1)S(1)} %constant_dynamic-slice_fusion.11), channel_id=1, source_target_pairs={{0,2},{1,3},{2,0},{3,1},{4,6},{5,7},{6,4},{7,5},{8,10},{9,11},{10,... | collective-permute-start | bytes 884744 | tf_op jit(solution)/shard_map/ppermute | solution.py:26
  386.5 10.7 %collective-permute-start.27 = (bf16[384,768]{1,0:T(8,128)(2,1)S(1)}, bf16[384,768]{1,0:T(8,128)(2,1)S(1)}, u32[]{:S(2)}, u32[]{:S(2)}) collective-permute-start(bf16[384,768]{1,0:T(8,128)(2,1)S(1)} %constant_dynamic-slice_fusion.2), channel_id=1, source_target_pairs={{0,16},{1,17},{2,18},{3,19},{4,20},{5,21},{6,22},{7,23},{8,9},{9,8... | collective-permute-start | bytes 1769480 | tf_op jit(solution)/shard_map/ppermute | solution.py:26
  388.1 9.0 %collective-permute-start.9 = (bf16[96,768]{1,0:T(8,128)(2,1)S(1)}, bf16[96,768]{1,0:T(8,128)(2,1)S(1)}, u32[]{:S(2)}, u32[]{:S(2)}) collective-permute-start(bf16[96,768]{1,0:T(8,128)(2,1)S(1)} %constant_dynamic-slice_fusion.10), channel_id=1, source_target_pairs={{0,4},{1,5},{2,6},{3,7},{4,0},{5,1},{6,2},{7,3},{8,12},{9,13},{10,... | collective-permute-start | bytes 442376 | tf_op jit(solution)/shard_map/ppermute | solution.py:26
  389.2 17.1 %collective-permute-start.18 = (bf16[192,768]{1,0:T(8,128)(2,1)S(1)}, bf16[192,768]{1,0:T(8,128)(2,1)S(1)}, u32[]{:S(2)}, u32[]{:S(2)}) collective-permute-start(bf16[192,768]{1,0:T(8,128)(2,1)S(1)} %constant_dynamic-slice_fusion.6), channel_id=1, source_target_pairs={{0,2},{1,3},{2,0},{3,1},{4,6},{5,7},{6,4},{7,5},{8,10},{9,11},{10,... | collective-permute-start | bytes 884744 | tf_op jit(solution)/shard_map/ppermute | solution.py:26
  397.1 9.0 %collective-permute-start.10 = (bf16[96,768]{1,0:T(8,128)(2,1)S(1)}, bf16[96,768]{1,0:T(8,128)(2,1)S(1)}, u32[]{:S(2)}, u32[]{:S(2)}) collective-permute-start(bf16[96,768]{1,0:T(8,128)(2,1)S(1)} %add_convert_fusion.17), channel_id=1, source_target_pairs={{0,4},{1,5},{2,6},{3,7},{4,0},{5,1},{6,2},{7,3},{8,12},{9,13},{10,... | collective-permute-start | bytes 442376 | tf_op jit(solution)/shard_map/ppermute | solution.py:26
  406.2 13.0 %collective-permute-start.11 = (bf16[192,768]{1,0:T(8,128)(2,1)S(1)}, bf16[192,768]{1,0:T(8,128)(2,1)S(1)}, u32[]{:S(2)}, u32[]{:S(2)}) collective-permute-start(bf16[192,768]{1,0:T(8,128)(2,1)S(1)} %maximum_select_fusion.12), channel_id=1, source_target_pairs={{0,2},{1,3},{2,0},{3,1},{4,6},{5,7},{6,4},{7,5},{8,10},{9,11},{10,... | collective-permute-start | bytes 884744 | tf_op jit(solution)/shard_map/ppermute | solution.py:26
  406.4 13.4 %collective-permute-start.19 = (bf16[96,768]{1,0:T(8,128)(2,1)S(1)}, bf16[96,768]{1,0:T(8,128)(2,1)S(1)}, u32[]{:S(2)}, u32[]{:S(2)}) collective-permute-start(bf16[96,768]{1,0:T(8,128)(2,1)S(1)} %constant_dynamic-slice_fusion.5), channel_id=1, source_target_pairs={{0,4},{1,5},{2,6},{3,7},{4,0},{5,1},{6,2},{7,3},{8,12},{9,13},{10,... | collective-permute-start | bytes 442376 | tf_op jit(solution)/shard_map/ppermute | solution.py:26
  408.9 17.5 %collective-permute-start.28 = (bf16[192,768]{1,0:T(8,128)(2,1)S(1)}, bf16[192,768]{1,0:T(8,128)(2,1)S(1)}, u32[]{:S(2)}, u32[]{:S(2)}) collective-permute-start(bf16[192,768]{1,0:T(8,128)(2,1)S(1)} %constant_dynamic-slice_fusion.1), channel_id=1, source_target_pairs={{0,2},{1,3},{2,0},{3,1},{4,6},{5,7},{6,4},{7,5},{8,10},{9,11},{10,... | collective-permute-start | bytes 884744 | tf_op jit(solution)/shard_map/ppermute | solution.py:26
  419.3 12.5 %collective-permute-start.12 = (bf16[384,768]{1,0:T(8,128)(2,1)S(1)}, bf16[384,768]{1,0:T(8,128)(2,1)S(1)}, u32[]{:S(2)}, u32[]{:S(2)}) collective-permute-start(bf16[384,768]{1,0:T(8,128)(2,1)S(1)} %maximum_select_fusion.9), channel_id=1, source_target_pairs={{0,16},{1,17},{2,18},{3,19},{4,20},{5,21},{6,22},{7,23},{8,9},{9,8... | collective-permute-start | bytes 1769480 | tf_op jit(solution)/shard_map/ppermute | solution.py:26
  419.9 11.8 %collective-permute-start.20 = (bf16[96,768]{1,0:T(8,128)(2,1)S(1)}, bf16[96,768]{1,0:T(8,128)(2,1)S(1)}, u32[]{:S(2)}, u32[]{:S(2)}) collective-permute-start(bf16[96,768]{1,0:T(8,128)(2,1)S(1)} %add_convert_fusion.16), channel_id=1, source_target_pairs={{0,4},{1,5},{2,6},{3,7},{4,0},{5,1},{6,2},{7,3},{8,12},{9,13},{10,... | collective-permute-start | bytes 442376 | tf_op jit(solution)/shard_map/ppermute | solution.py:26
  426.5 8.3 %collective-permute-start.29 = (bf16[96,768]{1,0:T(8,128)(2,1)S(1)}, bf16[96,768]{1,0:T(8,128)(2,1)S(1)}, u32[]{:S(2)}, u32[]{:S(2)}) collective-permute-start(bf16[96,768]{1,0:T(8,128)(2,1)S(1)} %constant_dynamic-slice_fusion), channel_id=1, source_target_pairs={{0,4},{1,5},{2,6},{3,7},{4,0},{5,1},{6,2},{7,3},{8,12},{9,13},{10,... | collective-permute-start | bytes 442376 | tf_op jit(solution)/shard_map/ppermute | solution.py:26
  431.7 7.7 %collective-permute-start.21 = (bf16[192,768]{1,0:T(8,128)(2,1)S(1)}, bf16[192,768]{1,0:T(8,128)(2,1)S(1)}, u32[]{:S(2)}, u32[]{:S(2)}) collective-permute-start(bf16[192,768]{1,0:T(8,128)(2,1)S(1)} %maximum_select_fusion.13), channel_id=1, source_target_pairs={{0,2},{1,3},{2,0},{3,1},{4,6},{5,7},{6,4},{7,5},{8,10},{9,11},{10,... | collective-permute-start | bytes 884744 | tf_op jit(solution)/shard_map/ppermute | solution.py:26
  432.3 24.7 %collective-permute-start.13 = (bf16[768,768]{1,0:T(8,128)(2,1)S(1)}, bf16[768,768]{1,0:T(8,128)(2,1)S(1)}, u32[]{:S(2)}, u32[]{:S(2)}) collective-permute-start(bf16[768,768]{1,0:T(8,128)(2,1)S(1)} %maximum_select_fusion.6), channel_id=1, source_target_pairs={{0,1},{1,0},{2,3},{3,2},{4,5},{5,4},{6,7},{7,6},{8,24},{9,25},{10,... | collective-permute-start | bytes 3538952 | tf_op jit(solution)/shard_map/ppermute | solution.py:26
  434.8 9.7 %collective-permute-start.30 = (bf16[96,768]{1,0:T(8,128)(2,1)S(1)}, bf16[96,768]{1,0:T(8,128)(2,1)S(1)}, u32[]{:S(2)}, u32[]{:S(2)}) collective-permute-start(bf16[96,768]{1,0:T(8,128)(2,1)S(1)} %add_convert_fusion.15), channel_id=1, source_target_pairs={{0,4},{1,5},{2,6},{3,7},{4,0},{5,1},{6,2},{7,3},{8,12},{9,13},{10,... | collective-permute-start | bytes 442376 | tf_op jit(solution)/shard_map/ppermute | solution.py:26
  438.8 28.1 %collective-permute-start = (f32[78,128]{1,0:T(8,128)}, f32[78,128]{1,0:T(8,128)}, u32[]{:S(2)}, u32[]{:S(2)}) collective-permute-start(f32[78,128]{1,0:T(8,128)} %bitcast.12), channel_id=1, source_target_pairs={{0,8},{1,9},{2,10},{3,11},{4,12},{5,13},{6,14},{7,15},{8,0},{9,1},... | collective-permute-start | bytes 119816 | tf_op jit(solution)/shard_map/ppermute | solution.py:26
  439.6 12.8 %collective-permute-start.22 = (bf16[384,768]{1,0:T(8,128)(2,1)S(1)}, bf16[384,768]{1,0:T(8,128)(2,1)S(1)}, u32[]{:S(2)}, u32[]{:S(2)}) collective-permute-start(bf16[384,768]{1,0:T(8,128)(2,1)S(1)} %maximum_select_fusion.10), channel_id=1, source_target_pairs={{0,16},{1,17},{2,18},{3,19},{4,20},{5,21},{6,22},{7,23},{8,9},{9,8... | collective-permute-start | bytes 1769480 | tf_op jit(solution)/shard_map/ppermute | solution.py:26
  444.6 6.8 %collective-permute-start.31 = (bf16[192,768]{1,0:T(8,128)(2,1)S(1)}, bf16[192,768]{1,0:T(8,128)(2,1)S(1)}, u32[]{:S(2)}, u32[]{:S(2)}) collective-permute-start(bf16[192,768]{1,0:T(8,128)(2,1)S(1)} %maximum_select_fusion.14), channel_id=1, source_target_pairs={{0,2},{1,3},{2,0},{3,1},{4,6},{5,7},{6,4},{7,5},{8,10},{9,11},{10,... | collective-permute-start | bytes 884744 | tf_op jit(solution)/shard_map/ppermute | solution.py:26
  452.4 17.3 %collective-permute-start.32 = (bf16[384,768]{1,0:T(8,128)(2,1)}, bf16[384,768]{1,0:T(8,128)(2,1)}, u32[]{:S(2)}, u32[]{:S(2)}) collective-permute-start(bf16[384,768]{1,0:T(8,128)(2,1)} %maximum_select_fusion.11), channel_id=1, source_target_pairs={{0,16},{1,17},{2,18},{3,19},{4,20},{5,21},{6,22},{7,23},{8,9},{9,8... | collective-permute-start | bytes 1769480 | tf_op jit(solution)/shard_map/ppermute | solution.py:26
  453.9 20.3 %collective-permute-start.23 = (bf16[768,768]{1,0:T(8,128)(2,1)}, bf16[768,768]{1,0:T(8,128)(2,1)}, u32[]{:S(2)}, u32[]{:S(2)}) collective-permute-start(bf16[768,768]{1,0:T(8,128)(2,1)} %maximum_select_fusion.7), channel_id=1, source_target_pairs={{0,1},{1,0},{2,3},{3,2},{4,5},{5,4},{6,7},{7,6},{8,24},{9,25},{10,... | collective-permute-start | bytes 3538952 | tf_op jit(solution)/shard_map/ppermute | solution.py:26
  457.9 55.4 %collective-permute-start.14 = (bf16[1536,768]{1,0:T(8,128)(2,1)S(1)}, bf16[1536,768]{1,0:T(8,128)(2,1)}, u32[]{:S(2)}, u32[]{:S(2)}) collective-permute-start(bf16[1536,768]{1,0:T(8,128)(2,1)S(1)} %maximum_select_fusion.3), channel_id=1, source_target_pairs={{0,8},{1,9},{2,10},{3,11},{4,12},{5,13},{6,14},{7,15},{8,0},{9,1},... | collective-permute-start | bytes 7077896 | tf_op jit(solution)/shard_map/ppermute | solution.py:26
  462.5 39.8 %all-to-all-start.1 = ((bf16[2,512,768]{2,0,1:T(2,128)(2,1)}), bf16[2,512,768]{2,0,1:T(2,128)(2,1)}, u32[]{:S(2)}, u32[]{:S(2)}) async-start(bf16[2,512,768]{2,0,1:T(2,128)(2,1)} %copy.92), calls=%async_computation.1 | async-start | bytes 3145728 | tf_op jit(solution)/shard_map/all_to_all | solution.py:254
  467.7 14.7 %collective-permute-start.1 = (f32[78,128]{1,0:T(8,128)S(1)}, f32[78,128]{1,0:T(8,128)S(1)}, u32[]{:S(2)}, u32[]{:S(2)}) collective-permute-start(f32[78,128]{1,0:T(8,128)S(1)} %bitcast_add_fusion), channel_id=1, source_target_pairs={{0,1},{1,0},{2,3},{3,2},{4,5},{5,4},{6,7},{7,6},{8,24},{9,25},{10,... | collective-permute-start | bytes 119816 | tf_op jit(solution)/shard_map/ppermute | solution.py:26
  471.5 35.2 %collective-permute-start.33 = (bf16[768,768]{1,0:T(8,128)(2,1)S(1)}, bf16[768,768]{1,0:T(8,128)(2,1)}, u32[]{:S(2)}, u32[]{:S(2)}) collective-permute-start(bf16[768,768]{1,0:T(8,128)(2,1)S(1)} %maximum_select_fusion.8), channel_id=1, source_target_pairs={{0,1},{1,0},{2,3},{3,2},{4,5},{5,4},{6,7},{7,6},{8,24},{9,25},{10,... | collective-permute-start | bytes 3538952 | tf_op jit(solution)/shard_map/ppermute | solution.py:26
  477.9 42.2 %collective-permute-start.24 = (bf16[1536,768]{1,0:T(8,128)(2,1)}, bf16[1536,768]{1,0:T(8,128)(2,1)}, u32[]{:S(2)}, u32[]{:S(2)}) collective-permute-start(bf16[1536,768]{1,0:T(8,128)(2,1)} %maximum_select_fusion.4), channel_id=1, source_target_pairs={{0,8},{1,9},{2,10},{3,11},{4,12},{5,13},{6,14},{7,15},{8,0},{9,1},... | collective-permute-start | bytes 7077896 | tf_op jit(solution)/shard_map/ppermute | solution.py:26
  483.2 6.3 %collective-permute-start.2 = (f32[78,128]{1,0:T(8,128)S(1)}, f32[78,128]{1,0:T(8,128)S(1)}, u32[]{:S(2)}, u32[]{:S(2)}) collective-permute-start(f32[78,128]{1,0:T(8,128)S(1)} %fusion.171), channel_id=1, source_target_pairs={{0,16},{1,17},{2,18},{3,19},{4,20},{5,21},{6,22},{7,23},{8,9},{9,8... | collective-permute-start | bytes 119816 | tf_op jit(solution)/shard_map/ppermute | solution.py:26
  489.5 5.4 collective-permute-start.3
  494.9 5.0 collective-permute-start.4
  509.8 22.4 %collective-permute-start.34 = (bf16[1536,768]{1,0:T(8,128)(2,1)}, bf16[1536,768]{1,0:T(8,128)(2,1)}, u32[]{:S(2)}, u32[]{:S(2)}) collective-permute-start(bf16[1536,768]{1,0:T(8,128)(2,1)} %maximum_select_fusion.5), channel_id=1, source_target_pairs={{0,8},{1,9},{2,10},{3,11},{4,12},{5,13},{6,14},{7,15},{8,0},{9,1},... | collective-permute-start | bytes 7077896 | tf_op jit(solution)/shard_map/ppermute | solution.py:26
  (62 other events, 331.0 us)
Sparse Core Ops, SparseCore 0:
  111.9 56.0 all-gather.1

commit v2 on v1

v2 whole, which is shorter than its diff:
```python
import functools

import jax
import jax.numpy as jnp
from jax import lax
from jax.experimental import pallas as pl
from jax.experimental.pallas import tpu as pltpu
from jax.sharding import PartitionSpec as P

HEADS = 12
SEG_ROW = 8
HIGHEST = lax.Precision.HIGHEST
NORM_EPS = 1e-12
POOL_EPS = 1e-06
INV_TEMPER = 100.0
MASKED = -1000000000.0
INV_ROOT_TWO_PI = 0.3989422804014327
INV_ROOT_TWO = 0.7071067811865476
BF = jnp.bfloat16
F32 = jnp.float32
MESH = pl.DeviceIdType.MESH


def dot(a, b):
    return jnp.dot(a, b, preferred_element_type=F32)


def dot_t(a, b, precision=None):
    return lax.dot_general(
        a, b, (((1,), (1,)), ((), ())), preferred_element_type=F32, precision=precision
    )


def t_dot(a, b):
    return lax.dot_general(a, b, (((0,), (0,)), ((), ())), preferred_element_type=F32)


def normalize(resid):
    center = resid - jnp.mean(resid, axis=-1, keepdims=True)
    spread = jnp.mean(center * center, axis=-1, keepdims=True)
    scale = lax.rsqrt(spread + NORM_EPS)
    return center * scale, scale


def norm_back(grad, gain, xhat, scale):
    q = grad * gain
    return scale * (
        q - jnp.mean(q, axis=-1, keepdims=True) - xhat * jnp.mean(q * xhat, axis=-1, keepdims=True)
    )


def split3(a):
    hi = a.astype(BF)
    rest = a - hi.astype(F32)
    mid = rest.astype(BF)
    return hi, mid, (rest - mid.astype(F32)).astype(BF)


def call(kernel, grid, in_specs, out_specs, out_shape, scratch, flops, moved, vmem=48):
    return pl.pallas_call(
        kernel,
        grid=grid,
        in_specs=in_specs,
        out_specs=out_specs,
        out_shape=out_shape,
        scratch_shapes=scratch,
        cost_estimate=pl.CostEstimate(flops=flops, bytes_accessed=moved, transcendentals=0),
        compiler_params=pltpu.CompilerParams(vmem_limit_bytes=vmem << 20),
    )


def shape_of(dims, dtype):
    return jax.ShapeDtypeStruct(dims, dtype)


PAIR = 128
QUAD = 256


def attend_kernel(
    x_ref, wq_ref, bq_ref, wk_ref, wv_ref, bv_ref, wo_ref, bo_ref, qa_ref, kb_ref,
    q_ref, k_ref, v_ref, o_ref, pt_ref, r_ref,
):
    x = x_ref[0]
    hd = PAIR // 2
    q = (dot(x, wq_ref[...]) + bq_ref[...]).astype(BF) * jnp.asarray(hd ** (-0.5), BF)
    k = dot(x, wk_ref[...]).astype(BF)
    v = (dot(x, wv_ref[...]) + bv_ref[...]).astype(BF)
    q_ref[0], k_ref[0], v_ref[0] = q, k, v
    lane = lax.broadcasted_iota(jnp.int32, (x.shape[0], PAIR), 1)
    outs = []
    for pair in range(QUAD // PAIR):
        at = slice(pair * PAIR, (pair + 1) * PAIR)
        keys = jnp.concatenate([k[:, at], kb_ref[0]], axis=1)
        vt = v[:, at].T
        parts = []
        for h in range(2):
            mine = (lane >= hd) if h else (lane < hd)
            queries = jnp.concatenate([jnp.where(mine, q[:, at], 0), qa_ref[0]], axis=1)
            st = dot_t(keys, queries)
            expo = jnp.exp(st - jnp.max(st, axis=0, keepdims=True))
            pt = (expo * (1.0 / jnp.sum(expo, axis=0, keepdims=True))).astype(BF)
            pt_ref[0, 2 * pair + h] = pt
            parts.append(dot(vt[h * hd : (h + 1) * hd], pt))
        outs.append(jnp.concatenate(parts, axis=0).T)
    o = jnp.concatenate(outs, axis=1).astype(BF)
    o_ref[0] = o
    part = dot(o, wo_ref[...])

    @pl.when(pl.program_id(1) == 0)
    def _():
        r_ref[0] = x.astype(F32) + bo_ref[...] + part

    @pl.when(pl.program_id(1) > 0)
    def _():
        r_ref[0] += part


def attend(x, wq, bq, wk, wv, bv, wo, bo, qa, kb):
    batch, length, width = x.shape
    row = pl.BlockSpec((1, length, width), lambda b, j: (b, 0, 0))
    cols = pl.BlockSpec((width, QUAD), lambda b, j: (0, j))
    bias = pl.BlockSpec((1, QUAD), lambda b, j: (0, j))
    quad = pl.BlockSpec((1, length, QUAD), lambda b, j: (b, 0, j))
    aug = pl.BlockSpec((1, length, PAIR), lambda b, j: (b, 0, 0))
    heads = QUAD // (width // HEADS)
    act = shape_of(x.shape, BF)
    return call(
        attend_kernel,
        (batch, width // QUAD),
        [row, cols, bias, cols, cols, bias,
         pl.BlockSpec((QUAD, width), lambda b, j: (j, 0)),
         pl.BlockSpec((1, width), lambda b, j: (0, 0)), aug, aug],
        [quad, quad, quad, quad,
         pl.BlockSpec((1, heads, length, length), lambda b, j: (b, j, 0, 0)), row],
        [act, act, act, act, shape_of((batch, HEADS, length, length), BF), shape_of(x.shape, F32)],
        [],
        batch * length * width * (8 * width + 8 * length),
        batch * length * (14 * width + 2 * HEADS * length) + 8 * width * width,
    )(x, wq, bq, wk, wv, bv, wo, bo, qa, kb)


def attend_back_kernel(
    q_ref, k_ref, v_ref, o_ref, do_ref, pt_ref, dq_ref, dk_ref, dv_ref, sum_ref,
):
    hd = PAIR // 2
    length = q_ref.shape[1]
    lane = lax.broadcasted_iota(jnp.int32, (length, PAIR), 1)
    lane8 = lax.broadcasted_iota(jnp.int32, (8, PAIR), 1)
    dqs, dvs = [], []
    for pair in range(QUAD // PAIR):
        at = slice(pair * PAIR, (pair + 1) * PAIR)
        q, k, v, o, do = (ref[0, :, at] for ref in (q_ref, k_ref, v_ref, o_ref, do_ref))
        kt = k.T
        prod = o.astype(F32) * do.astype(F32)
        high = prod.astype(BF)
        low = (prod - high.astype(F32)).astype(BF)
        dk = dv = None
        dqt = []
        for h in range(2):
            mine = (lane >= hd) if h else (lane < hd)
            ones = jnp.where((lane8 >= hd) if h else (lane8 < hd), 1.0, 0.0).astype(BF)
            do_h = jnp.where(mine, do, 0)
            q_h = jnp.where(mine, q, 0)
            mixed = (dot_t(ones, high) + dot_t(ones, low))[0:1]
            pt = pt_ref[0, 2 * pair + h]
            ds = (pt.astype(F32) * (dot_t(v, do_h) - mixed)).astype(BF)
            dv_h, dk_h = dot(pt, do_h), dot(ds, q_h)
            dv = dv_h if dv is None else dv + dv_h
            dk = dk_h if dk is None else dk + dk_h
            dqt.append(dot(kt[h * hd : (h + 1) * hd], ds))
        dq = (jnp.concatenate(dqt, axis=0).T * (hd ** (-0.5))).astype(BF)
        dv = dv.astype(BF)
        dq_ref[0, :, at], dk_ref[0, :, at], dv_ref[0, :, at] = dq, dk.astype(BF), dv
        sum_ref[0, 0:1, at] = jnp.sum(dq.astype(F32), axis=0, keepdims=True)
        sum_ref[0, 1:2, at] = jnp.sum(dv.astype(F32), axis=0, keepdims=True)


def attend_back(q, k, v, o, do, pt):
    batch, length, width = q.shape
    quad = pl.BlockSpec((1, length, QUAD), lambda b, j: (b, 0, j))
    heads = QUAD // (width // HEADS)
    act = shape_of(q.shape, BF)
    return call(
        attend_back_kernel,
        (batch, width // QUAD),
        [quad] * 5 + [pl.BlockSpec((1, heads, length, length), lambda b, j: (b, j, 0, 0))],
        [quad, quad, quad, pl.BlockSpec((1, 8, QUAD), lambda b, j: (b, 0, j))],
        [act, act, act, shape_of((batch, 8, width), F32)],
        [],
        batch * length * length * width * 16,
        batch * length * (16 * width + 2 * HEADS * length),
    )(q, k, v, o, do, pt)


def gelu_both(u):
    t = 1.0 / (1.0 + (0.3275911 * INV_ROOT_TWO) * jnp.abs(u))
    poly = t * (
        0.127414796 + t * (-0.142248368 + t * (0.7107068705 + t * (-0.7265760135 + t * 0.5307027145)))
    )
    bell = jnp.exp(-0.5 * u * u)
    tail = poly * bell
    cdf = jnp.where(u < 0.0, tail, 1.0 - tail)
    return u * cdf, cdf + (INV_ROOT_TWO_PI * u) * bell


def feed_kernel(
    r_ref, g_ref, b_ref, wi_ref, bi_ref, wo_ref, bo_ref, ids_ref,
    h_ref, act_ref, slope_ref, r2_ref, pool_ref, hidden,
):
    step = pl.program_id(1)

    @pl.when(step == 0)
    def _():
        xhat, _ = normalize(r_ref[0])
        h = xhat * g_ref[...] + b_ref[...]
        hidden[...] = h
        h_ref[0] = h.astype(BF)

    u = dot(h_ref[0], wi_ref[...]) + bi_ref[...]
    act, slope = gelu_both(u)
    act = act.astype(BF)
    act_ref[0] = act
    slope_ref[0] = slope.astype(BF)
    hidden[...] += dot(act, wo_ref[...])

    @pl.when(step == pl.num_programs(1) - 1)
    def _():
        r2 = hidden[...] + bo_ref[...]
        r2_ref[0] = r2
        xhat, _ = normalize(r2)
        hot = lax.broadcasted_iota(jnp.int32, (SEG_ROW, r2.shape[0]), 0) == ids_ref[0]
        counts = jnp.sum(hot.astype(F32), axis=1, keepdims=True)
        hot = hot.astype(F32).astype(BF)
        total = sum(dot(hot, piece) for piece in split3(xhat))
        pool_ref[0] = total / counts


def feed(r, gain, shift, wi, bi, wo, bo, ids):
    batch, length, width = r.shape
    ff = wi.shape[1]
    row = pl.BlockSpec((1, length, width), lambda b, c: (b, 0, 0))
    vec = pl.BlockSpec((1, width), lambda b, c: (0, 0))
    chunk = pl.BlockSpec((1, length, width), lambda b, c: (b, 0, c))
    wide = shape_of((batch, length, ff), BF)
    return call(
        feed_kernel,
        (batch, ff // width),
        [row, vec, vec, pl.BlockSpec((width, width), lambda b, c: (0, c)),
         pl.BlockSpec((1, width), lambda b, c: (0, c)),
         pl.BlockSpec((width, width), lambda b, c: (c, 0)), vec,
         pl.BlockSpec((1, 1, length), lambda b, c: (b, 0, 0))],
        [row, chunk, chunk, row, pl.BlockSpec((1, SEG_ROW, width), lambda b, c: (b, 0, 0))],
        [shape_of(r.shape, BF), wide, wide, shape_of(r.shape, F32), shape_of((batch, SEG_ROW, width), F32)],
        [pltpu.VMEM((length, width), F32)],
        4 * batch * length * width * ff,
        batch * length * (10 * width + 4 * ff) + 4 * batch * width * ff,
    )(r, gain, shift, wi, bi, wo, bo, ids)


def flip(v, step):
    return v + step * (1 - 2 * (v // step % 2))


def links(rows):
    seq, row = lax.axis_index("seq"), lax.axis_index("rows")
    core, y, x = seq % 2, seq // 2 % 2, row % 2
    other = 1 - core
    found = [
        ((flip(seq, 1), row), core),
        ((seq + core * 2 * (1 - 2 * y), row + other * (1 - 2 * x)), core * y + other * x),
        ((seq + other * 2 * (1 - 2 * y), row + core * (1 - 2 * x)), other * y + core * x),
    ]
    step = 2
    while step < rows:
        found.append(((seq, flip(row, step)), row // step % 2))
        step *= 2
    return found


def greet(devices):
    barrier = pltpu.get_barrier_semaphore()
    for device in devices:
        pl.semaphore_signal(barrier, inc=1, device_id=device, device_id_type=MESH)
    pl.semaphore_wait(barrier, len(devices))


def remote(source, target, send, receive, device):
    return pltpu.make_async_remote_copy(
        src_ref=source, dst_ref=target, send_sem=send, recv_sem=receive,
        device_id=device, device_id_type=MESH,
    )


def contrast_kernel(
    rows, xpool_ref, gain_ref, shift_ref, tag_ref, counts_ref,
    de_ref, vec_ref, all_ref, lse_ref, send, receive,
):
    own, width = xpool_ref.shape
    total = all_ref.shape[0]
    near = links(rows)
    hops = near[3:][::-1] + near[1:3] + near[:1]
    greet([device for device, _ in hops])
    e_own = xpool_ref[...] * gain_ref[...] + shift_ref[...]
    all_ref[0:own, 0:width] = e_own
    all_ref[0:own, width:] = tag_ref[...]
    have = own
    for i, (device, _) in enumerate(hops):
        copy = remote(
            all_ref.at[0:have], all_ref.at[have : 2 * have], send.at[i], receive.at[i], device
        )
        copy.start()
        copy.wait()
        have *= 2

    def unit(e):
        rho = lax.rsqrt(jnp.sum(e * e, axis=1, keepdims=True) + POOL_EPS)
        return e * rho, rho

    n_all, _ = unit(all_ref[:, 0:width])
    pick = lax.broadcasted_iota(jnp.int32, (8, PAIR), 0) == lax.broadcasted_iota(jnp.int32, (8, PAIR), 1)
    tags = dot_t(pick.astype(F32), all_ref[:, width:], HIGHEST)
    pos_all, id_all = tags[0:1], tags[1:2]
    block = min(total, 512)
    for b in range(total // block):
        n_b, _ = unit(all_ref[b * block : (b + 1) * block, 0:width])
        c = dot_t(n_all, n_b, HIGHEST) * INV_TEMPER
        i = lax.broadcasted_iota(jnp.int32, c.shape, 0)
        j = lax.broadcasted_iota(jnp.int32, c.shape, 1) + b * block
        c = jnp.where(i == j, MASKED, c)
        top = jnp.max(c, axis=0, keepdims=True)
        lse_ref[:, b * block : (b + 1) * block] = (
            jnp.log(jnp.sum(jnp.exp(c - top), axis=0, keepdims=True)) + top
        )
    n_own, rho = unit(e_own)
    pos_own, id_own = tag_ref[:, 0:1], tag_ref[:, 1:2]
    c = dot_t(n_own, n_all, HIGHEST) * INV_TEMPER
    c = jnp.where(id_own == id_all, MASKED, c)
    top = jnp.max(c, axis=1, keepdims=True)
    lse_own = jnp.log(jnp.sum(jnp.exp(c - top), axis=1, keepdims=True)) + top
    chosen = id_all == pos_own
    picked = jnp.sum(jnp.where(chosen, c, 0.0), axis=1, keepdims=True)
    weight = (
        jnp.exp(c - lse_own)
        + jnp.exp(c - lse_ref[...])
        - jnp.where(chosen, 1.0, 0.0)
        - jnp.where(id_own == pos_all, 1.0, 0.0)
    )
    d_n = INV_TEMPER * jnp.dot(weight, n_all, precision=HIGHEST, preferred_element_type=F32)
    along = jnp.sum(e_own * d_n, axis=1, keepdims=True)
    d_e = rho * d_n - (rho * rho * rho) * e_own * along
    de_ref[...] = d_e / counts_ref[...]
    vec_ref[0:1] = jnp.sum(d_e * xpool_ref[...], axis=0, keepdims=True)
    vec_ref[1:2] = jnp.sum(d_e, axis=0, keepdims=True)
    vec_ref[2:3] = jnp.broadcast_to(jnp.sum(lse_own - picked), (1, vec_ref.shape[1]))
    vec_ref[3:8] = jnp.zeros((5, vec_ref.shape[1]), F32)


def contrast(xpool, gain, shift, tags, counts, devices, rows):
    own, width = xpool.shape
    total = own * devices
    vmem = pl.BlockSpec(memory_space=pltpu.VMEM)
    stages = len(bin(devices)) - 3
    return pl.pallas_call(
        functools.partial(contrast_kernel, rows),
        in_specs=[vmem] * 5,
        out_specs=[vmem, vmem],
        out_shape=[shape_of((own, width), F32), shape_of((8, width), F32)],
        scratch_shapes=[
            pltpu.VMEM((total, width + PAIR), F32),
            pltpu.VMEM((1, total), F32),
            pltpu.SemaphoreType.DMA((stages,)),
            pltpu.SemaphoreType.DMA((stages,)),
        ],
        cost_estimate=pl.CostEstimate(
            flops=12 * total * total * width, bytes_accessed=4 * total * width, transcendentals=0
        ),
        compiler_params=pltpu.CompilerParams(
            vmem_limit_bytes=48 << 20, collective_id=0, has_side_effects=True
        ),
    )(xpool, gain, shift, tags, counts)


class Chain:
    def __init__(self, order, first, number, rows_chunk, start, period, grads, sums, send, receive, came):
        self.order, self.first, self.number = order, first, number
        self.start, self.period = start, period
        self.grads, self.sums, self.send, self.receive, self.came = grads, sums, send, receive, came
        sizes, height, wide = [], rows_chunk, grads.shape[1]
        for _ in order:
            if height % 32 == 0:
                height //= 2
            else:
                wide //= 2
            sizes.append((height, wide))
        self.sizes, self.rows_chunk = sizes, rows_chunk
        self.last = start + (number - 1) * period + 2 * len(order)

    def places(self, chunk):
        row, column = chunk * self.rows_chunk, 0
        before = self.rows_chunk
        found = []
        for (height, wide), (_, bit) in zip(self.sizes, self.order):
            if height < before:
                kept = (row + bit * height, column)
                sent = (row + (1 - bit) * height, column)
            else:
                kept = (row, column + bit * wide)
                sent = (row, column + (1 - bit) * wide)
            found.append((kept, sent))
            (row, column), before = kept, height
        return found

    def at(self, ref, place, size):
        row, column = place
        if size[1] == ref.shape[1]:
            return ref.at[pl.ds(pl.multiple_of(row, 16), size[0])]
        return ref.at[
            pl.ds(pl.multiple_of(row, 16), size[0]), pl.ds(pl.multiple_of(column, PAIR), size[1])
        ]

    def copy(self, chunk, places, stage):
        n = len(self.order)
        i = stage if stage < n else 2 * n - 1 - stage
        kept, sent = places[i]
        size, device = self.sizes[i], self.order[i][0]
        sems = self.send.at[stage, chunk], self.receive.at[stage, chunk]
        if stage < n:
            slot = self.came[i].at[chunk - self.first]
            return remote(self.at(self.grads, sent, size), slot, *sems, device)
        part = self.at(self.sums, kept, size)
        return remote(part, part, *sems, device)

    def step(self, t):
        for stage in range(2 * len(self.order), -1, -1):
            since = t - stage - self.start
            index = since // self.period
            pl.when((since >= 0) & (since % self.period == 0) & (index < self.number))(
                functools.partial(self.advance, stage, index + self.first)
            )

    def advance(self, stage, chunk):
        n = len(self.order)
        places = self.places(chunk)
        if stage > 0:
            self.copy(chunk, places, stage - 1).wait()
        if 0 < stage <= n:
            i = stage - 1
            height, wide = self.sizes[i]
            tile = min(height, 32)
            (row, column), _ = places[i]
            target = self.grads if stage < n else self.sums

            def add(k, carry):
                place, size = (row + k * tile, column), (tile, wide)
                mine = self.at(self.grads, place, size)
                theirs = self.came[i].at[chunk - self.first, pl.ds(pl.multiple_of(k * tile, 16), tile)]
                total = mine[...].astype(F32) + theirs[...].astype(F32)
                self.at(target, place, size)[...] = total.astype(BF)
                return carry

            lax.fori_loop(0, height // tile, add, 0)
        if stage < 2 * n:
            self.copy(chunk, places, stage).start()


def sum_kernel(plan, rows, *refs):
    (grads, tokens, small), (sums, token_out, small_out) = refs[:3], refs[3:6]
    send, receive, s_send, s_receive, t_send, t_receive, own_sem, small_came = refs[6:14]
    came = refs[14:]
    near = links(rows)
    n = len(near)
    seq, row = lax.axis_index("seq"), lax.axis_index("rows")
    seqs = tokens.shape[1] // token_out.shape[1]
    greet([device for device, _ in near] + [(flip(flip(seq, 1), 2), row)])

    batch, part = tokens.shape[0], token_out.shape[1]
    def piece(i):
        to = lax.rem(seq + i, seqs)
        return remote(
            tokens.at[:, pl.ds(pl.multiple_of(to * part, 16), part)],
            token_out.at[pl.ds(seq * batch, batch)],
            t_send.at[i], t_receive.at[i], (to, row),
        )
    for i in range(1, seqs):
        piece(i).start()
    own = pltpu.make_async_copy(
        tokens.at[:, pl.ds(pl.multiple_of(seq * part, 16), part)],
        token_out.at[pl.ds(seq * batch, batch)], own_sem,
    )
    own.start()

    small_out[...] = small[...]
    orders = {"ab": near, "z": near[:1] + near[3:] + near[1:3]}
    chains, at = [], 0
    for name, first, number, rows_chunk, start, period in plan:
        chains.append(
            Chain(orders[name], first, number, rows_chunk, start, period,
                  grads, sums, send, receive, came[at : at + n])
        )
        at += n

    def small_copy(i):
        source = small_out if i == 0 else small_came.at[n + i - 1]
        return remote(source, small_came.at[i], s_send.at[i], s_receive.at[i], near[i][0])

    def step(t, carry):
        for chain in chains:
            chain.step(t)
        for i in range(n + 1):
            @pl.when(t == i)
            def _(i=i):
                if i > 0:
                    small_copy(i - 1).wait()
                    before = small_out if i == 1 else small_came.at[n + i - 2]
                    after = small_out if i == n else small_came.at[n + i - 1]
                    after[...] = before[...] + small_came[i - 1]
                if i < n:
                    small_copy(i).start()
        return carry

    lax.fori_loop(0, max(max(chain.last for chain in chains), n) + 1, step, 0)
    own.wait()
    for i in range(1, seqs):
        piece(i).wait()


def sum_all(grads, tokens, small, devices, rows, seqs):
    n = len(bin(devices)) - 3
    chunk = 1024
    plan = [("ab", 0, 9, chunk, 0, 1)]
    batch, length, width = tokens.shape
    total = grads.shape[0]
    vmem = pl.BlockSpec(memory_space=pltpu.VMEM)
    came = []
    for _, _, number, height, _, _ in plan:
        wide = width
        for _ in range(n):
            if height % 32 == 0:
                height //= 2
            else:
                wide //= 2
            came.append(pltpu.VMEM((number, height, wide), BF))
    chunks = sum(p[2] for p in plan)
    return pl.pallas_call(
        functools.partial(sum_kernel, plan, rows),
        in_specs=[vmem] * 3,
        out_specs=[vmem] * 3,
        out_shape=[
            shape_of(grads.shape, BF),
            shape_of((batch * seqs, length // seqs, width), BF),
            shape_of(small.shape, F32),
        ],
        scratch_shapes=[
            pltpu.SemaphoreType.DMA((2 * n, chunks)),
            pltpu.SemaphoreType.DMA((2 * n, chunks)),
            pltpu.SemaphoreType.DMA((n,)),
            pltpu.SemaphoreType.DMA((n,)),
            pltpu.SemaphoreType.DMA((seqs,)),
            pltpu.SemaphoreType.DMA((seqs,)),
            pltpu.SemaphoreType.DMA,
            pltpu.VMEM((2 * n,) + small.shape, F32),
        ] + came,
        cost_estimate=pl.CostEstimate(flops=total * width * 4, bytes_accessed=total * width * 8, transcendentals=0),
        compiler_params=pltpu.CompilerParams(
            vmem_limit_bytes=60 << 20, collective_id=1, has_side_effects=True
        ),
    )(grads, tokens, small)


def pool_back_kernel(r2_ref, gain_ref, ids_ref, de_ref, dr_ref, df_ref, sum_ref):
    length, width = r2_ref.shape[1:]
    xhat, scale = normalize(r2_ref[0])
    lane = lax.broadcasted_iota(jnp.int32, (length, PAIR), 1)
    hot = (lane % SEG_ROW == ids_ref[0]) & (lane < 3 * SEG_ROW)
    hot = jnp.where(hot, 1.0, 0.0).astype(BF)
    pieces = list(split3(de_ref[0])) + [jnp.zeros((PAIR - 3 * SEG_ROW, width), BF)]
    d_y = dot(hot, jnp.concatenate(pieces, axis=0))
    d_r = norm_back(d_y, gain_ref[...], xhat, scale)
    dr_ref[0] = d_r
    d_f = d_r.astype(BF)
    df_ref[0] = d_f
    sum_ref[0, 0:1] = jnp.sum(d_f.astype(F32), axis=0, keepdims=True)


def pool_back(r2, gain, ids_col, de):
    batch, length, width = r2.shape
    row = pl.BlockSpec((1, length, width), lambda b: (b, 0, 0))
    eight = pl.BlockSpec((1, 8, width), lambda b: (b, 0, 0))
    return call(
        pool_back_kernel,
        (batch,),
        [row, pl.BlockSpec((1, width), lambda b: (0, 0)),
         pl.BlockSpec((1, length, 1), lambda b: (b, 0, 0)),
         pl.BlockSpec((1, SEG_ROW, width), lambda b: (b, 0, 0))],
        [row, row, eight],
        [shape_of(r2.shape, F32), shape_of(r2.shape, BF), shape_of((batch, 8, width), F32)],
        [],
        batch * length * width * 300,
        batch * length * width * 10,
    )(r2, gain, ids_col, de)


def feed_back_kernel(
    df_ref, dr2_ref, slope_ref, wo_ref, wi_ref, r_ref, gain_ref, wa_ref,
    du_ref, dr_ref, da_ref, do_ref, sum_ref, usum_ref, total,
):
    step = pl.program_id(1)
    d_u = (dot_t(df_ref[0], wo_ref[...]) * slope_ref[0].astype(F32)).astype(BF)
    du_ref[0] = d_u
    usum_ref[0, 0:1] = jnp.sum(d_u.astype(F32), axis=0, keepdims=True)
    part = dot_t(d_u, wi_ref[...])

    @pl.when(step == 0)
    def _():
        total[...] = dr2_ref[0] + part

    @pl.when(step > 0)
    def _():
        total[...] += part

    @pl.when(step == pl.num_programs(1) - 1)
    def _():
        d_h = total[...]
        xhat, scale = normalize(r_ref[0])
        d_r = norm_back(d_h, gain_ref[...], xhat, scale)
        dr_ref[0] = d_r
        d_a = d_r.astype(BF)
        da_ref[0] = d_a
        do_ref[0] = dot_t(d_a, wa_ref[...]).astype(BF)
        sum_ref[0, 0:1] = jnp.sum(d_a.astype(F32), axis=0, keepdims=True)
        sum_ref[0, 1:2] = jnp.sum(d_h * xhat, axis=0, keepdims=True)
        sum_ref[0, 2:3] = jnp.sum(d_h, axis=0, keepdims=True)


def feed_back(df, dr2, slope, wo, wi, r, gain, wa):
    batch, length, width = r.shape
    ff = wi.shape[1]
    row = pl.BlockSpec((1, length, width), lambda b, c: (b, 0, 0))
    chunk = pl.BlockSpec((1, length, width), lambda b, c: (b, 0, c))
    return call(
        feed_back_kernel,
        (batch, ff // width),
        [row, row, chunk, pl.BlockSpec((width, width), lambda b, c: (c, 0)),
         pl.BlockSpec((width, width), lambda b, c: (0, c)), row,
         pl.BlockSpec((1, width), lambda b, c: (0, 0)),
         pl.BlockSpec((width, width), lambda b, c: (0, 0))],
        [chunk, row, row, row, pl.BlockSpec((1, 8, width), lambda b, c: (b, 0, 0)),
         pl.BlockSpec((1, 8, width), lambda b, c: (b, 0, c))],
        [shape_of((batch, length, ff), BF), shape_of(r.shape, F32), shape_of(r.shape, BF),
         shape_of(r.shape, BF), shape_of((batch, 8, width), F32), shape_of((batch, 8, ff), F32)],
        [pltpu.VMEM((length, width), F32)],
        batch * length * width * (4 * ff + 2 * width),
        batch * length * (20 * width + 4 * ff) + 4 * batch * width * ff,
    )(df, dr2, slope, wo, wi, r, gain, wa)


def local(
    tokens,
    query_weight,
    query_bias,
    key_weight,
    value_weight,
    value_bias,
    output_weight,
    output_bias,
    attn_gain,
    attn_shift,
    inner_weight,
    inner_bias,
    outer_weight,
    outer_bias,
    ffn_gain,
    ffn_shift,
    segment_ids,
    positives,
):
    group_rows, local_len, width = tokens.shape
    ff = inner_weight.shape[1]
    seqs = lax.axis_size("seq")
    seq, row_place = lax.axis_index("seq"), lax.axis_index("rows")
    batch, length = group_rows // seqs, local_len * seqs
    count = batch * length
    ids = lax.dynamic_slice_in_dim(segment_ids, seq * batch, batch, 0)
    own_segs = batch * SEG_ROW
    own_positives = lax.dynamic_slice_in_dim(positives, seq * own_segs, own_segs, 0)
    own_ids = row_place * positives.shape[0] + seq * own_segs + jnp.arange(own_segs, dtype=jnp.int32)
    tags = jnp.stack([own_positives, own_ids] + [jnp.zeros_like(own_ids)] * (PAIR - 2), axis=1).astype(F32)
    hot = ids[:, :, None] == jnp.arange(PAIR, dtype=jnp.int32)
    real = jnp.arange(PAIR, dtype=jnp.int32) < SEG_ROW
    apart_q = jnp.where(hot, -(2.0**30), 0.0).astype(BF)
    apart_k = jnp.where(hot | ~real, 0.0, 1.0).astype(BF)
    counts = jnp.sum(hot.astype(F32), axis=1)[:, :SEG_ROW].reshape(own_segs, 1)
    vec = lambda v: v.astype(F32).reshape(1, -1)
    flat2 = lambda a: a.reshape(count, a.shape[-1])

    x = lax.all_to_all(tokens, "seq", split_axis=0, concat_axis=1, tiled=True)
    q, k, v, o, pt, r_one = attend(
        x, query_weight, vec(query_bias), key_weight, value_weight, vec(value_bias),
        output_weight, vec(output_bias), apart_q, apart_k,
    )
    hidden, active, slope, r_two, xpool = feed(
        r_one, vec(attn_gain), vec(attn_shift), inner_weight, vec(inner_bias), outer_weight,
        vec(outer_bias), ids.reshape(batch, 1, length),
    )
    xpool = xpool.reshape(own_segs, width)
    rows = lax.axis_size("rows")
    devices = rows * seqs
    d_e, loss_vec = contrast(xpool, vec(ffn_gain), vec(ffn_shift), tags, counts, devices, rows)
    d_two, d_outer, outer_sum = pool_back(
        r_two, vec(ffn_gain), ids.reshape(batch, length, 1), d_e.reshape(batch, SEG_ROW, width)
    )
    g_outer = t_dot(flat2(active), flat2(d_outer)).astype(BF)
    d_inner, d_one, d_attn, d_o, row_sums, inner_sum = feed_back(
        d_outer, d_two, slope, outer_weight, inner_weight, r_one, vec(attn_gain), output_weight
    )
    d_inner2 = flat2(d_inner)
    g_inner = jnp.concatenate(
        [t_dot(flat2(hidden), d_inner2[:, i * width : (i + 1) * width]).astype(BF) for i in range(ff // width)],
        axis=0,
    )
    d_q, d_k, d_v, head_sums = attend_back(q, k, v, o, d_o, pt)
    d_q, d_k, d_v = flat2(d_q), flat2(d_k), flat2(d_v)
    flat = flat2(x)
    g_attn = jnp.concatenate(
        [t_dot(flat, d_q).astype(BF), t_dot(flat, d_k).astype(BF), t_dot(flat, d_v).astype(BF),
         t_dot(flat2(o), flat2(d_attn)).astype(BF)], axis=0
    )
    row_sums, head_sums = jnp.sum(row_sums, axis=0), jnp.sum(head_sums, axis=0)
    small = jnp.concatenate(
        [
            head_sums[0], head_sums[1], row_sums[0], row_sums[1], row_sums[2],
            jnp.sum(inner_sum[:, 0], axis=0), jnp.sum(outer_sum[:, 0], axis=0),
            loss_vec[0], loss_vec[1], loss_vec[2],
        ]
    ).reshape(-1, 128)
    small = jnp.pad(small, ((0, -small.shape[0] % 8), (0, 0)))
    token_grad = (
        flat2(d_one) + dot_t(d_q, query_weight) + dot_t(d_k, key_weight) + dot_t(d_v, value_weight)
    ).astype(BF)
    sums, grad_tokens, small = sum_all(
        jnp.concatenate([g_outer, g_inner, g_attn], axis=0),
        token_grad.reshape(batch, length, width), small, devices, rows, seqs,
    )
    grad_tokens = grad_tokens.astype(F32)
    small = small.reshape(-1)
    sum_outer = sums[:ff].astype(F32)
    sum_inner = jnp.concatenate(
        [sums[ff + i * width : ff + (i + 1) * width] for i in range(ff // width)], axis=1
    ).astype(F32)
    sum_attn = sums[2 * ff :].astype(F32)
    sizes = [width] * 5 + [ff] + [width] * 4
    pieces, at = [], 0
    for size in sizes:
        pieces.append(small[at : at + size])
        at += size
    qb, vb, ob, ag, ash, ib, wb, fg, fs, ls = pieces
    return (
        ls[0] / (own_segs * devices),
        grad_tokens,
        sum_attn[:width],
        qb,
        sum_attn[width : 2 * width],
        sum_attn[2 * width : 3 * width],
        vb,
        sum_attn[3 * width :],
        ob,
        ag,
        ash,
        sum_inner,
        ib,
        sum_outer,
        wb,
        fg,
        fs,
    )


def solution(mesh):
    placed = (
        (P("rows", "seq", None),) + (P(),) * 15 + (P("rows", None), P("rows"))
    )
    return jax.shard_map(
        local,
        mesh=mesh,
        in_specs=placed,
        out_specs=(P(), P("rows", "seq", None)) + (P(),) * 15,
        check_vma=False,
    )
```

time: 558 us -> 413 us (0.74)
  Pallas kernels: 0 us -> 299 us
  waiting for transfers between devices: 156 us -> 19.6 us
  matrix products: 154 us -> 28.7 us
  other arithmetic: 72.9 us -> 20.1 us
  starting transfers between devices: 55.4 us -> 4.49 us
  local copies, waits for them, and re-layouts: 79.1 us -> 30.1 us
  between operations: 18.6 us -> 3.7 us
  blocking collectives: 12.8 us -> 0 us
    pallas_call x0 -> x7, Pallas kernels: none -> 299 us  [the longest x1 167 us: sum_all(): pl.pallas_call(functools.partial(sum_kernel, plan, rows), in_specs=[vmem]...]
    dot_general x21 -> x3, matrix products: 115 us -> 8.11 us  [dot_t(): lax.dot_general(a, b, (((1,), (1,)), ((), ())), preferred_element_type=F3...]
    ppermute x35 -> x0, waiting for transfers between devices: 96.3 us -> none  [exchange(): return lax.ppermute(array, ('seq', 'rows'), pairs)]
    ppermute x35 -> x0, starting transfers between devices: 46.6 us -> none  [exchange(): return lax.ppermute(array, ('seq', 'rows'), pairs)]
    all_gather x1 -> x0, waiting for transfers between devices: 41.4 us -> none  [gather_embeddings(): return lax.all_gather(own, ('rows', 'seq'), axis=0, tiled=True)]
    convert_element_type x30 -> x4, other arithmetic: 42.6 us -> 19.8 us  [the longest x1 12.1 us: local(): sum_outer = sums[:ff].astype(F32)]
    unnamed x161 -> x83, local copies, waits for them, and re-layouts: 30.5 us -> 11.4 us
    convert_element_type x9 -> x0, local copies, waits for them, and re-layouts: 17.1 us -> none  [the longest x3 5.03 us: local(): a.astype(BF).reshape(count, width)]
  transfers between devices with their start and end apart: 38 -> 1, of which waited for: 17 -> 1; matrix products, arithmetic and copies ran while one was open for 15% -> 0% of each run, Pallas kernels for 0% -> 0%
where the time goes in v2:
time: 413 us; the launch traced here: 405 us
  Pallas kernels  299 us (72%)
  local copies, waits for them, and re-layouts  30.1 us (7%)
  matrix products  28.7 us (7%)
  other arithmetic  20.1 us (5%)
  waiting for transfers between devices  19.6 us (5%)
  starting transfers between devices  4.49 us (1%)
    pallas_call x1, Pallas kernels, sum_all(): pl.pallas_call(functools.partial(sum_kernel, plan, rows), in_specs=[vmem]...  167 us
    pallas_call x1, Pallas kernels, contrast(): pl.pallas_call(functools.partial(contrast_kernel, rows), in_specs=[vmem]...  32.3 us
    pallas_call x1, Pallas kernels, feed(): call(feed_kernel, (batch, ff // width), [row, vec, vec, pl.BlockSpec((wid...  26.2 us
    pallas_call x1, Pallas kernels, attend(): call(attend_kernel, (batch, width // QUAD), [row, cols, bias, cols, cols,...  25.5 us
    pallas_call x1, Pallas kernels, feed_back(): call(feed_back_kernel, (batch, ff // width), [row, row, chunk, pl.BlockSp...  24.2 us
    dot_general x9, matrix products, t_dot(): lax.dot_general(a, b, (((0,), (0,)), ((), ())), preferred_element_type=F32)  20.6 us
    all_to_all x1, waiting for transfers between devices, local(): x = lax.all_to_all(tokens, 'seq', split_axis=0, concat_axis=1, tiled=True)  19.6 us
    pallas_call x1, Pallas kernels, attend_back(): call(attend_back_kernel, (batch, width // QUAD), [quad] * 5 + [pl.BlockSp...  19.3 us
  transfers between devices with their start and end apart: 1, of which 1 were waited for; matrix products, arithmetic and copies ran while one was open for 0% of the time, Pallas kernels for 0%

profile of v2, /device:TPU:0, one launch (start us, length us, event | category | flops | bytes accessed | tf_op | source)
XLA Modules:
  0.0 405.4 jit_solution(6650064899358234257)
XLA Ops:
  0.7 0.0 copy-start
  0.8 4.5 %all-to-all-start = ((bf16[8,128,768]{2,1,0:T(8,128)(2,1)}), bf16[8,128,768]{2,1,0:T(8,128)(2,1)}, u32[]{:S(2)}, u32[]{:S(2)}) async-start(bf16[8,128,768]{2,1,0:T(8,128)(2,1)} %param.18), calls=%async_computation | async-start | bytes 3145728 | tf_op jit(solution)/shard_map/all_to_all | solution.py:697
  5.5 0.1 dynamic-slice_bitcast_fusion
  5.6 0.1 copy.41
  5.8 0.1 stack.32
  5.9 0.2 copy.43.ids_ref
  6.1 0.2 convert_reduce_fusion
  6.4 0.1 reshape.206.counts_ref
  6.5 19.6 %all-to-all-done = bf16[8,128,768]{2,1,0:T(8,128)(2,1)} async-done(((bf16[8,128,768]{2,1,0:T(8,128)(2,1)}), bf16[8,128,768]{2,1,0:T(8,128)(2,1)}, u32[]{:S(2)}, u32[]{:S(2)}) %all-to-all-start) | async-done | bytes 1572896 | tf_op jit(solution)/shard_map/all_to_all | solution.py:697
  26.1 2.8 copy.40
  28.9 1.3 copy-done.9
  30.1 25.5 %shard_map.305 = (bf16[2,512,768]{2,1,0:T(8,128)(2,1)}, bf16[2,512,768]{2,1,0:T(8,128)(2,1)}, bf16[2,512,768]{2,1,0:T(8,128)(2,1)}, bf16[2,512,768]{2,1,0:T(8,12...) custom-call(bf16[2,512,768]{2,1,0:T(8,128)(2,1)} %bitcast.104, bf16[768,768]{1,0:T(8,128)(2,1)S(1)} %copy-done.9, ...), custom_call_target="tpu_custom_call" | custom-call | flops 8053063680 | bytes 28311552 | tf_op jit(solution)/shard_map/pallas_call | solution.py:128
  55.6 26.2 %shard_map.306 = (bf16[2,512,768]{2,1,0:T(8,128)(2,1)S(1)}, bf16[2,512,3072]{2,1,0:T(8,128)(2,1)}, bf16[2,512,3072]{2,1,0:T(8,128)(2,1)}, f32[2,512,768]{2,1,0:T(8,128)S(1)}, f32[2,8,768]{2,1,0:T(8,128)S(1)}) custom-call(f32[2,512,768]{2,1,0:T(8,128)} %get-tuple-element.46.r_ref, f32[1,768]{1,0:T(1,128)S(1)} %reshape.193.g_ref.gain_ref, ...), custom_call_target="tpu_custom_call" | custom-call | flops 9663676416 | bytes 39321600 | tf_op jit(solution)/shard_map/pallas_call | solution.py:246
  81.8 1.2 copy-done.11
  83.0 32.3 %shard_map.307 = (f32[16,768]{1,0:T(8,128)S(1)}, f32[8,768]{1,0:T(8,128)S(1)}) custom-call(f32[16,768]{1,0:T(8,128)S(1)} %bitcast.102, f32[1,768]{1,0:T(1,128)S(1)} %reshape.201.gain_ref, f32[1,768]{1,0:T(1,128)S(1)} %reshape.203.shift_ref, f32[16,128]{1,0:T(8,128)S(1)} %convert_element_type.78.tag_ref, f32[16,1]{1,0:T(8,128)S(1)} %reshape.206.counts_ref), custom_call_target="tpu_custom_call" | custom-call | flops 2415919104 | bytes 1572864 | tf_op jit(solution)/shard_map/pallas_call | solution.py:364
  115.3 3.7 shard_map.308
  119.0 1.7 copy-done.4
  120.7 24.2 %shard_map.309 = (bf16[2,512,3072]{2,1,0:T(8,128)(2,1)}, f32[2,512,768]{2,1,0:T(8,128)}, bf16[2,512,768]{2,1,0:T(8,128)(2,1)S(1)}, bf16[2,512,768]{2,1,0:T(8,128...) custom-call(bf16[2,512,768]{2,1,0:T(8,128)(2,1)S(1)} %get-tuple-element.51.df_ref, ...), custom_call_target="tpu_custom_call" | custom-call | flops 10871635968 | bytes 47185920 | tf_op jit(solution)/shard_map/pallas_call | solution.py:641
  144.9 1.1 copy-done.17
  146.0 1.1 copy-done.18
  147.2 19.3 %shard_map.310 = (bf16[2,512,768]{2,1,0:T(8,128)(2,1)S(1)}, bf16[2,512,768]{2,1,0:T(8,128)(2,1)S(1)}, bf16[2,512,768]{2,1,0:T(8,128)(2,1)S(1)}, f32[2,8,768]{2,1,0:T(8,128)S(1)}) custom-call(bf16[2,512,768]{2,1,0:T(8,128)(2,1)} %get-tuple-element.56.q_ref, bf16[2,512,768]{2,1,0:T(8,128)(2,1)} %get-tuple-element.57.k_ref, ...), custom_call_target="tpu_custom_call" | custom-call | flops 6442450944 | bytes 25165824 | tf_op jit(solution)/shard_map/pallas_call | solution.py:184
  166.6 1.1 copy-done.13
  167.7 1.1 copy-done.15
  169.1 0.6 pad.4.refs_2_
  169.7 3.3 fusion.47
  173.1 1.4 fusion.46
  174.5 9.0 %fusion = bf16[9216,768]{1,0:T(8,128)(2,1)S(1)} fusion(bf16[2,512,3072]{2,1,0:T(8,128)(2,1)} %get-tuple-element.47, bf16[2,512,768]{2,1,0:T(8,128)(2,1)S(1)} %copy-done.6), kind=kOutput, calls=%fused_computation.1 | convolution fusion | flops 4834197504 | bytes 12582912 | tf_op jit(solution)/shard_map/dot_general | solution.py:35
  183.6 1.4 fusion.15
  185.0 1.4 fusion.21
  186.5 1.4 fusion.27
  187.9 1.4 fusion.33
  189.4 1.4 fusion.38
  190.8 1.5 fusion.40
  192.4 1.4 fusion.42
  193.8 0.4 copy-done.34
  194.2 1.5 fusion.36.refs_0_
  195.7 0.4 copy-done.22
  196.1 3.4 fusion.3
  199.5 1.7 copy-done.20
  201.2 167.5 %shard_map.311 = (bf16[9216,768]{1,0:T(8,128)(2,1)}, bf16[8,128,768]{2,1,0:T(8,128)(2,1)}, f32[80,128]{1,0:T(8,128)}) custom-call(bf16[9216,768]{1,0:T(8,128)(2,1)} %copy-done.20, bf16[2,512,768]{2,1,0:T(8,128)(2,1)} %bitcast.103, f32[80,128]{1,0:T(8,128)} %pad.4.refs_2_), custom_call_target="tpu_custom_call" | custom-call | flops 28311552 | bytes 56623104 | tf_op jit(solution)/shard_map/pallas_call | solution.py:545
  368.7 1.3 slice_bitcast_fusion
  370.0 1.4 slice_bitcast_fusion.1
  371.4 3.7 fusion.44
  375.1 12.1 %slice_convert_fusion = (f32[3072,768]{1,0:T(8,128)}, f32[3072,768]{1,0:T(8,128)}) fusion(bf16[9216,768]{1,0:T(8,128)(2,1)} %get-tuple-element.74), kind=kLoop, calls=%fused_computation.3 | loop fusion | flops 4718592 | bytes 28311552 | tf_op jit(solution)/shard_map/convert_element_type | solution.py:747
  387.2 0.5 slice.155
  387.7 3.4 convert_element_type.93
  391.1 7.7 %fusion.45 = (f32[768,768]{1,0:T(8,128)}, f32[768,768]{1,0:T(8,128)}, f32[768,768]{1,0:T(8,128)}, f32[768,768]{1,0:T(8,128)}) fusion(f32[3072,768]{1,0:T(8,128)} %get-tuple-element.84), kind=kLoop, calls=%fused_computation.76 | loop fusion | bytes 18874368 | tf_op jit(solution)/shard_map/slice | solution.py:766
  399.4 4.3 %maximum_convert_fusion = f32[768,3072]{1,0:T(8,128)} fusion(bf16[768,768]{1,0:T(8,128)(2,1)S(1)} %get-tuple-element.86, bf16[768,768]{1,0:T(8,128)(2,1)S(1)} %get-tuple-element.87, bf16[768,768]{1,0:T(8,128)(2,1)S(1)} %copy-done.21, bf16[768,768]{1,0:T(8,128)(2,1)S(1)} %get-tuple-element.85), kind=kLoop, calls=%fused_computation.2 | loop fusion | flops 18874368 | bytes 14155776 | tf_op jit(solution)/shard_map/convert_element_type | solution.py:750
  (103 shorter events, 0.4 us)
Async XLA Ops:
  0.7 4.8 %copy-start = (s32[8,512]{1,0:T(8,128)S(1)}, s32[8,512]{1,0:T(8,128)}, u32[]{:S(2)}) copy-start(s32[8,512]{1,0:T(8,128)} %param.34) | copy-start | bytes 49156
  0.7 4.6 %copy-start.25 = (bf16[768]{0:T(1024)(128)(2,1)S(1)}, bf16[768]{0:T(1024)(128)(2,1)}, u32[]{:S(2)}) copy-start(bf16[768]{0:T(1024)(128)(2,1)} %param.26) | copy-start | bytes 4612
  0.7 4.6 %copy-start.26 = (bf16[768]{0:T(1024)(128)(2,1)S(1)}, bf16[768]{0:T(1024)(128)(2,1)}, u32[]{:S(2)}) copy-start(bf16[768]{0:T(1024)(128)(2,1)} %param.32) | copy-start | bytes 4612
  0.7 4.6 %copy-start.27 = (bf16[768]{0:T(1024)(128)(2,1)S(1)}, bf16[768]{0:T(1024)(128)(2,1)}, u32[]{:S(2)}) copy-start(bf16[768]{0:T(1024)(128)(2,1)} %param.20) | copy-start | bytes 4612
  0.7 4.7 %copy-start.28 = (bf16[768]{0:T(1024)(128)(2,1)S(1)}, bf16[768]{0:T(1024)(128)(2,1)}, u32[]{:S(2)}) copy-start(bf16[768]{0:T(1024)(128)(2,1)} %param.23) | copy-start | bytes 4612
  0.7 4.7 %copy-start.29 = (bf16[768]{0:T(1024)(128)(2,1)S(1)}, bf16[768]{0:T(1024)(128)(2,1)}, u32[]{:S(2)}) copy-start(bf16[768]{0:T(1024)(128)(2,1)} %param.25) | copy-start | bytes 4612
  0.7 4.7 %copy-start.30 = (bf16[768]{0:T(1024)(128)(2,1)S(1)}, bf16[768]{0:T(1024)(128)(2,1)}, u32[]{:S(2)}) copy-start(bf16[768]{0:T(1024)(128)(2,1)} %param.27) | copy-start | bytes 4612
  0.7 4.7 %copy-start.31 = (bf16[768]{0:T(1024)(128)(2,1)S(1)}, bf16[768]{0:T(1024)(128)(2,1)}, u32[]{:S(2)}) copy-start(bf16[768]{0:T(1024)(128)(2,1)} %param.31) | copy-start | bytes 4612
  0.7 4.7 %copy-start.32 = (bf16[768]{0:T(1024)(128)(2,1)S(1)}, bf16[768]{0:T(1024)(128)(2,1)}, u32[]{:S(2)}) copy-start(bf16[768]{0:T(1024)(128)(2,1)} %param.33) | copy-start | bytes 4612
  0.8 4.8 %copy-start.33 = (s32[64]{0:T(128)S(1)}, s32[64]{0:T(128)}, u32[]{:S(2)}) copy-start(s32[64]{0:T(128)} %param.35) | copy-start | bytes 772
  0.8 5.1 %copy-start.24 = (bf16[3072]{0:T(1024)(128)(2,1)S(1)}, bf16[3072]{0:T(1024)(128)(2,1)}, u32[]{:S(2)}) copy-start(bf16[3072]{0:T(1024)(128)(2,1)} %param.29) | copy-start | bytes 18436
  0.8 25.3 %all-to-all-start = ((bf16[8,128,768]{2,1,0:T(8,128)(2,1)}), bf16[8,128,768]{2,1,0:T(8,128)(2,1)}, u32[]{:S(2)}, u32[]{:S(2)}) async-start(bf16[8,128,768]{2,1,0:T(8,128)(2,1)} %param.18), calls=%async_computation | async-start | bytes 3145728 | tf_op jit(solution)/shard_map/all_to_all | solution.py:697
  6.1 22.7 %copy-start.8 = (bf16[768,768]{1,0:T(8,128)(2,1)S(1)}, bf16[768,768]{1,0:T(8,128)(2,1)}, u32[]{:S(2)}) copy-start(bf16[768,768]{1,0:T(8,128)(2,1)} %wk_ref.1) | copy-start | bytes 3538948
  26.0 2.8 copy-start.3
  26.1 2.8 copy-start.7
  28.9 1.3 copy-start.9
  81.8 1.2 copy-start.11
  83.0 32.3 %copy-start.2 = (f32[2,512,768]{2,1,0:T(8,128)}, f32[2,512,768]{2,1,0:T(8,128)S(1)}, u32[]{:S(2)}) copy-start(f32[2,512,768]{2,1,0:T(8,128)S(1)} %get-tuple-element.48.r2_ref) | copy-start | bytes 9437188
  119.0 1.7 copy-start.4
  120.7 24.2 %copy-start.5 = (bf16[2,512,768]{2,1,0:T(8,128)(2,1)}, bf16[2,512,768]{2,1,0:T(8,128)(2,1)S(1)}, u32[]{:S(2)}) copy-start(bf16[2,512,768]{2,1,0:T(8,128)(2,1)S(1)} %get-tuple-element.51.df_ref) | copy-start | bytes 4718596
  144.9 1.1 copy-start.17
  146.0 1.1 copy-start.18
  166.6 1.1 copy-start.13
  167.7 1.1 copy-start.15
  169.7 3.3 copy-start.10
  169.7 3.3 copy-start.16
  173.0 1.5 copy-start.6
  173.0 10.5 %slice-start = ((s8[6291456]{0:T(1024)(128)(4,1)}), s8[4194304]{0:T(1024)(128)(4,1)S(1)}, s32[]{:S(2)}) async-start(s8[6291456]{0:T(1024)(128)(4,1)} %bitcast.110), calls=%async_computation.1 | async-start | bytes 8388608
  174.5 9.0 %copy-start.12 = (bf16[2,512,768]{2,1,0:T(8,128)(2,1)S(1)}, bf16[2,512,768]{2,1,0:T(8,128)(2,1)}, u32[]{:S(2)}) copy-start(bf16[2,512,768]{2,1,0:T(8,128)(2,1)} %copy-done.11) | copy-start | bytes 4718596
  174.5 9.0 %slice-start.1 = ((s8[6291456]{0:T(1024)(128)(4,1)}), s8[2097152]{0:T(1024)(128)(4,1)S(1)}, s32[]{:S(2)}) async-start(s8[6291456]{0:T(1024)(128)(4,1)} %bitcast.110), calls=%async_computation.2 | async-start | bytes 4194304
  187.9 1.5 copy-start.23
  189.4 1.5 copy-start.14
  192.3 1.5 copy-start.19
  192.3 1.9 copy-start.34
  194.2 1.9 copy-start.22
  195.7 5.5 %copy-start.20 = (bf16[9216,768]{1,0:T(8,128)(2,1)}, bf16[9216,768]{1,0:T(8,128)(2,1)S(1)}, u32[]{:S(2)}) copy-start(bf16[9216,768]{1,0:T(8,128)(2,1)S(1)} %fusion.36.refs_0_) | copy-start | bytes 42467332
  391.1 8.3 %copy-start.21 = (bf16[768,768]{1,0:T(8,128)(2,1)S(1)}, bf16[768,768]{1,0:T(8,128)(2,1)}, u32[]{:S(2)}) copy-start(bf16[768,768]{1,0:T(8,128)(2,1)} %get-tuple-element.88) | copy-start | bytes 3538948
  399.4 4.4 %copy-start.1 = (s32[8,512]{1,0:T(8,128)S(1)}, s32[8,512]{1,0:T(8,128)}, u32[]{:S(2)}) copy-start(s32[8,512]{1,0:T(8,128)} %param.34) | copy-start | bytes 49156

commit v3 on v2

--- a/solution.py
+++ b/solution.py
@@ -140,59 +140,6 @@
     )(x, wq, bq, wk, wv, bv, wo, bo, qa, kb)
 
 
-def attend_back_kernel(
-    q_ref, k_ref, v_ref, o_ref, do_ref, pt_ref, dq_ref, dk_ref, dv_ref, sum_ref,
-):
-    hd = PAIR // 2
-    length = q_ref.shape[1]
-    lane = lax.broadcasted_iota(jnp.int32, (length, PAIR), 1)
-    lane8 = lax.broadcasted_iota(jnp.int32, (8, PAIR), 1)
-    dqs, dvs = [], []
-    for pair in range(QUAD // PAIR):
-        at = slice(pair * PAIR, (pair + 1) * PAIR)
-        q, k, v, o, do = (ref[0, :, at] for ref in (q_ref, k_ref, v_ref, o_ref, do_ref))
-        kt = k.T
-        prod = o.astype(F32) * do.astype(F32)
-        high = prod.astype(BF)
-        low = (prod - high.astype(F32)).astype(BF)
-        dk = dv = None
-        dqt = []
-        for h in range(2):
-            mine = (lane >= hd) if h else (lane < hd)
-            ones = jnp.where((lane8 >= hd) if h else (lane8 < hd), 1.0, 0.0).astype(BF)
-            do_h = jnp.where(mine, do, 0)
-            q_h = jnp.where(mine, q, 0)
-            mixed = (dot_t(ones, high) + dot_t(ones, low))[0:1]
-            pt = pt_ref[0, 2 * pair + h]
-            ds = (pt.astype(F32) * (dot_t(v, do_h) - mixed)).astype(BF)
-            dv_h, dk_h = dot(pt, do_h), dot(ds, q_h)
-            dv = dv_h if dv is None else dv + dv_h
-            dk = dk_h if dk is None else dk + dk_h
-            dqt.append(dot(kt[h * hd : (h + 1) * hd], ds))
-        dq = (jnp.concatenate(dqt, axis=0).T * (hd ** (-0.5))).astype(BF)
-        dv = dv.astype(BF)
-        dq_ref[0, :, at], dk_ref[0, :, at], dv_ref[0, :, at] = dq, dk.astype(BF), dv
-        sum_ref[0, 0:1, at] = jnp.sum(dq.astype(F32), axis=0, keepdims=True)
-        sum_ref[0, 1:2, at] = jnp.sum(dv.astype(F32), axis=0, keepdims=True)
-
-
-def attend_back(q, k, v, o, do, pt):
-    batch, length, width = q.shape
-    quad = pl.BlockSpec((1, length, QUAD), lambda b, j: (b, 0, j))
-    heads = QUAD // (width // HEADS)
-    act = shape_of(q.shape, BF)
-    return call(
-        attend_back_kernel,
-        (batch, width // QUAD),
-        [quad] * 5 + [pl.BlockSpec((1, heads, length, length), lambda b, j: (b, j, 0, 0))],
-        [quad, quad, quad, pl.BlockSpec((1, 8, QUAD), lambda b, j: (b, 0, j))],
-        [act, act, act, shape_of((batch, 8, width), F32)],
-        [],
-        batch * length * length * width * 16,
-        batch * length * (16 * width + 2 * HEADS * length),
-    )(q, k, v, o, do, pt)
-
-
 def gelu_both(u):
     t = 1.0 / (1.0 + (0.3275911 * INV_ROOT_TWO) * jnp.abs(u))
     poly = t * (
@@ -381,24 +328,57 @@
     )(xpool, gain, shift, tags, counts)
 
 
+CHUNK = 1024
+
+
+def halves(steps, dims):
+    sizes, (height, wide) = [], dims
+    for _ in range(steps):
+        if height % 32 == 0:
+            height //= 2
+        else:
+            wide //= 2
+        sizes.append((height, wide))
+    return sizes
+
+
+def plan(outer, inner, quads, batch):
+    ready = outer + inner + 2 * batch
+    return [
+        ("ab", 0, 0, outer, 1, 1, (1, 3, 2, 1)),
+        ("ab", 1, 0, inner, outer + 1, 1, (1, 3, 2, 1)),
+        ("ab", 2, 0, quads, ready, 2 * batch, (1, 2, 2, 1)),
+    ]
+
+
+def orders(rows):
+    near = links(rows)
+    seq, row = lax.axis_index("seq"), lax.axis_index("rows")
+    along = [((seq, flip(row, 1)), row % 2), ((flip(seq, 2), row), seq // 2 % 2)]
+    return {
+        "ab": near,
+        "xy": near[:1] + along + near[3:],
+        "z": near[:1] + near[3:] + near[1:3],
+    }
+
+
 class Chain:
-    def __init__(self, order, first, number, rows_chunk, start, period, grads, sums, send, receive, came):
-        self.order, self.first, self.number = order, first, number
-        self.start, self.period = start, period
-        self.grads, self.sums, self.send, self.receive, self.came = grads, sums, send, receive, came
-        sizes, height, wide = [], rows_chunk, grads.shape[1]
-        for _ in order:
-            if height % 32 == 0:
-                height //= 2
-            else:
-                wide //= 2
-            sizes.append((height, wide))
-        self.sizes, self.rows_chunk = sizes, rows_chunk
-        self.last = start + (number - 1) * period + 2 * len(order)
+    def __init__(self, order, entry, dims, down, grads, sums, mark, came, piece, send, receive, keep):
+        self.first, self.number, self.start, self.period, stretch = entry
+        stretch = list(stretch) + [stretch[-1]] * (len(order) - len(stretch))
+        self.after = [0]
+        for wait in stretch + stretch[::-1]:
+            self.after.append(self.after[-1] + wait)
+        self.order, self.dims, self.down = order, dims, down
+        self.grads, self.sums, self.mark = grads, sums, mark
+        self.came, self.piece = came, piece
+        self.send, self.receive, self.keep = send, receive, keep
+        self.sizes = halves(len(order), dims)
+        self.last = self.start + (self.number - 1) * self.period + self.after[-1]
 
     def places(self, chunk):
-        row, column = chunk * self.rows_chunk, 0
-        before = self.rows_chunk
+        row, column = (chunk * self.dims[0], 0) if self.down else (0, chunk * self.dims[1])
+        before = self.dims[0]
         found = []
         for (height, wide), (_, bit) in zip(self.sizes, self.order):
             if height < before:
@@ -413,8 +393,6 @@
 
     def at(self, ref, place, size):
         row, column = place
-        if size[1] == ref.shape[1]:
-            return ref.at[pl.ds(pl.multiple_of(row, 16), size[0])]
         return ref.at[
             pl.ds(pl.multiple_of(row, 16), size[0]), pl.ds(pl.multiple_of(column, PAIR), size[1])
         ]
@@ -424,20 +402,28 @@
         i = stage if stage < n else 2 * n - 1 - stage
         kept, sent = places[i]
         size, device = self.sizes[i], self.order[i][0]
-        sems = self.send.at[stage, chunk], self.receive.at[stage, chunk]
+        mark = chunk + self.mark
+        pair = self.send.at[stage, mark], self.receive.at[stage, mark]
         if stage < n:
-            slot = self.came[i].at[chunk - self.first]
-            return remote(self.at(self.grads, sent, size), slot, *sems, device)
-        part = self.at(self.sums, kept, size)
-        return remote(part, part, *sems, device)
+            return remote(self.at(self.grads, sent, size), self.came[i].at[chunk], *pair, device)
+        target = self.at(self.sums, kept, size)
+        return remote(self.piece.at[chunk] if stage == n else target, target, *pair, device)
+
+    def own(self, chunk, places):
+        target = self.at(self.sums, places[-1][0], self.sizes[-1])
+        return pltpu.make_async_copy(self.piece.at[chunk], target, self.keep.at[chunk + self.mark])
 
     def step(self, t):
         for stage in range(2 * len(self.order), -1, -1):
-            since = t - stage - self.start
-            index = since // self.period
-            pl.when((since >= 0) & (since % self.period == 0) & (index < self.number))(
-                functools.partial(self.advance, stage, index + self.first)
-            )
+            since = t - self.after[stage] - self.start
+            if self.number == 1:
+                pl.when(since == 0)(functools.partial(self.advance, stage, self.first))
+                continue
+            index = since // self.period if self.period > 1 else since
+            here = (since >= 0) & (index < self.number)
+            if self.period > 1:
+                here &= since % self.period == 0
+            pl.when(here)(functools.partial(self.advance, stage, index + self.first))
 
     def advance(self, stage, chunk):
         n = len(self.order)
@@ -445,160 +431,31 @@
         if stage > 0:
             self.copy(chunk, places, stage - 1).wait()
         if 0 < stage <= n:
-            i = stage - 1
-            height, wide = self.sizes[i]
-            tile = min(height, 32)
-            (row, column), _ = places[i]
-            target = self.grads if stage < n else self.sums
+            height, wide = self.sizes[stage - 1]
+            row, column = places[stage - 1][0]
+            tile = 16 if height % 32 else 32
 
             def add(k, carry):
-                place, size = (row + k * tile, column), (tile, wide)
-                mine = self.at(self.grads, place, size)
-                theirs = self.came[i].at[chunk - self.first, pl.ds(pl.multiple_of(k * tile, 16), tile)]
-                total = mine[...].astype(F32) + theirs[...].astype(F32)
-                self.at(target, place, size)[...] = total.astype(BF)
+                at = pl.ds(pl.multiple_of(k * tile, 16), tile)
+                mine = self.at(self.grads, (row + k * tile, column), (tile, wide))
+                total = (mine[...].astype(F32) + self.came[stage - 1][chunk, at].astype(F32)).astype(BF)
+                if stage < n:
+                    mine[...] = total
+                else:
+                    self.piece[chunk, at] = total
                 return carry
 
             lax.fori_loop(0, height // tile, add, 0)
+        if stage == n:
+            self.own(chunk, places).start()
+        if stage == n + 1:
+            self.own(chunk, places).wait()
         if stage < 2 * n:
             self.copy(chunk, places, stage).start()
 
 
-def sum_kernel(plan, rows, *refs):
-    (grads, tokens, small), (sums, token_out, small_out) = refs[:3], refs[3:6]
-    send, receive, s_send, s_receive, t_send, t_receive, own_sem, small_came = refs[6:14]
-    came = refs[14:]
-    near = links(rows)
-    n = len(near)
-    seq, row = lax.axis_index("seq"), lax.axis_index("rows")
-    seqs = tokens.shape[1] // token_out.shape[1]
-    greet([device for device, _ in near] + [(flip(flip(seq, 1), 2), row)])
-
-    batch, part = tokens.shape[0], token_out.shape[1]
-    def piece(i):
-        to = lax.rem(seq + i, seqs)
-        return remote(
-            tokens.at[:, pl.ds(pl.multiple_of(to * part, 16), part)],
-            token_out.at[pl.ds(seq * batch, batch)],
-            t_send.at[i], t_receive.at[i], (to, row),
-        )
-    for i in range(1, seqs):
-        piece(i).start()
-    own = pltpu.make_async_copy(
-        tokens.at[:, pl.ds(pl.multiple_of(seq * part, 16), part)],
-        token_out.at[pl.ds(seq * batch, batch)], own_sem,
-    )
-    own.start()
-
-    small_out[...] = small[...]
-    orders = {"ab": near, "z": near[:1] + near[3:] + near[1:3]}
-    chains, at = [], 0
-    for name, first, number, rows_chunk, start, period in plan:
-        chains.append(
-            Chain(orders[name], first, number, rows_chunk, start, period,
-                  grads, sums, send, receive, came[at : at + n])
-        )
-        at += n
-
-    def small_copy(i):
-        source = small_out if i == 0 else small_came.at[n + i - 1]
-        return remote(source, small_came.at[i], s_send.at[i], s_receive.at[i], near[i][0])
-
-    def step(t, carry):
-        for chain in chains:
-            chain.step(t)
-        for i in range(n + 1):
-            @pl.when(t == i)
-            def _(i=i):
-                if i > 0:
-                    small_copy(i - 1).wait()
-                    before = small_out if i == 1 else small_came.at[n + i - 2]
-                    after = small_out if i == n else small_came.at[n + i - 1]
-                    after[...] = before[...] + small_came[i - 1]
-                if i < n:
-                    small_copy(i).start()
-        return carry
-
-    lax.fori_loop(0, max(max(chain.last for chain in chains), n) + 1, step, 0)
-    own.wait()
-    for i in range(1, seqs):
-        piece(i).wait()
-
-
-def sum_all(grads, tokens, small, devices, rows, seqs):
-    n = len(bin(devices)) - 3
-    chunk = 1024
-    plan = [("ab", 0, 9, chunk, 0, 1)]
-    batch, length, width = tokens.shape
-    total = grads.shape[0]
-    vmem = pl.BlockSpec(memory_space=pltpu.VMEM)
-    came = []
-    for _, _, number, height, _, _ in plan:
-        wide = width
-        for _ in range(n):
-            if height % 32 == 0:
-                height //= 2
-            else:
-                wide //= 2
-            came.append(pltpu.VMEM((number, height, wide), BF))
-    chunks = sum(p[2] for p in plan)
-    return pl.pallas_call(
-        functools.partial(sum_kernel, plan, rows),
-        in_specs=[vmem] * 3,
-        out_specs=[vmem] * 3,
-        out_shape=[
-            shape_of(grads.shape, BF),
-            shape_of((batch * seqs, length // seqs, width), BF),
-            shape_of(small.shape, F32),
-        ],
-        scratch_shapes=[
-            pltpu.SemaphoreType.DMA((2 * n, chunks)),
-            pltpu.SemaphoreType.DMA((2 * n, chunks)),
-            pltpu.SemaphoreType.DMA((n,)),
-            pltpu.SemaphoreType.DMA((n,)),
-            pltpu.SemaphoreType.DMA((seqs,)),
-            pltpu.SemaphoreType.DMA((seqs,)),
-            pltpu.SemaphoreType.DMA,
-            pltpu.VMEM((2 * n,) + small.shape, F32),
-        ] + came,
-        cost_estimate=pl.CostEstimate(flops=total * width * 4, bytes_accessed=total * width * 8, transcendentals=0),
-        compiler_params=pltpu.CompilerParams(
-            vmem_limit_bytes=60 << 20, collective_id=1, has_side_effects=True
-        ),
-    )(grads, tokens, small)
-
-
-def pool_back_kernel(r2_ref, gain_ref, ids_ref, de_ref, dr_ref, df_ref, sum_ref):
-    length, width = r2_ref.shape[1:]
-    xhat, scale = normalize(r2_ref[0])
-    lane = lax.broadcasted_iota(jnp.int32, (length, PAIR), 1)
-    hot = (lane % SEG_ROW == ids_ref[0]) & (lane < 3 * SEG_ROW)
-    hot = jnp.where(hot, 1.0, 0.0).astype(BF)
-    pieces = list(split3(de_ref[0])) + [jnp.zeros((PAIR - 3 * SEG_ROW, width), BF)]
-    d_y = dot(hot, jnp.concatenate(pieces, axis=0))
-    d_r = norm_back(d_y, gain_ref[...], xhat, scale)
-    dr_ref[0] = d_r
-    d_f = d_r.astype(BF)
-    df_ref[0] = d_f
-    sum_ref[0, 0:1] = jnp.sum(d_f.astype(F32), axis=0, keepdims=True)
-
-
-def pool_back(r2, gain, ids_col, de):
-    batch, length, width = r2.shape
-    row = pl.BlockSpec((1, length, width), lambda b: (b, 0, 0))
-    eight = pl.BlockSpec((1, 8, width), lambda b: (b, 0, 0))
-    return call(
-        pool_back_kernel,
-        (batch,),
-        [row, pl.BlockSpec((1, width), lambda b: (0, 0)),
-         pl.BlockSpec((1, length, 1), lambda b: (b, 0, 0)),
-         pl.BlockSpec((1, SEG_ROW, width), lambda b: (b, 0, 0))],
-        [row, row, eight],
-        [shape_of(r2.shape, F32), shape_of(r2.shape, BF), shape_of((batch, 8, width), F32)],
-        [],
-        batch * length * width * 300,
-        batch * length * width * 10,
-    )(r2, gain, ids_col, de)
+def sems(*dims):
+    return [pltpu.SemaphoreType.DMA(dims)] * 2
 
 
 def feed_back_kernel(
@@ -653,6 +510,344 @@
         batch * length * width * (4 * ff + 2 * width),
         batch * length * (20 * width + 4 * ff) + 4 * batch * width * ff,
     )(df, dr2, slope, wo, wi, r, gain, wa)
+
+
+def fixed(dims):
+    return pl.BlockSpec(dims, lambda g: (0,) * len(dims), pipeline_mode=pl.Buffered(1))
+
+
+def back_kernel(rows, *refs):
+    (act_ref, df_ref, du_ref, h_ref, q_ref, k_ref, v_ref, o_ref, do_ref, pt_ref, x_ref, da_ref, dr_ref,
+     wq_ref, wk_ref, wv_ref, small_ref) = refs[:17]
+    sums, (token_out, small_out) = refs[17:20], refs[20:22]
+    (g_outer, g_inner, g_attn, g_total, go_total, dx, tokens, small_came, send, receive, s_send,
+     s_receive, t_send, t_receive, keep, other) = refs[22:38]
+    landing = refs[38:]
+    step = pl.program_id(0)
+    length = q_ref.shape[1]
+    count, width = x_ref.shape
+    batch = count // length
+    outer, inner = sums[0].shape[0] // CHUNK, sums[1].shape[1] // CHUNK
+    quads = width // QUAD
+    kinds = orders(rows)
+    near = kinds["ab"]
+    n = len(near)
+    seq, row_place = lax.axis_index("seq"), lax.axis_index("rows")
+    seqs = token_out.shape[0] // batch
+    part = length // seqs
+    groups = [
+        ((CHUNK, width), True, g_outer, sums[0], 0),
+        ((width, CHUNK), False, g_inner, sums[1], outer),
+        ((CHUNK, width), True, g_attn, sums[2], outer + inner),
+    ]
+    chains = []
+    for kind, group, *entry in plan(outer, inner, quads, batch):
+        came = landing[group * (n + 1) : group * (n + 1) + n]
+        piece = landing[group * (n + 1) + n]
+        chains.append(
+            Chain(kinds[kind], entry, *groups[group], came, piece, send, receive, keep)
+        )
+    before = outer + inner
+    ticks = before + 2 * quads * batch
+    last = max(max(chain.last for chain in chains), ticks + n)
+    u = jnp.maximum(step - before, 0)
+
+    def tick(t):
+        for chain in chains:
+            chain.step(t)
+
+    def piece(i):
+        to = lax.rem(seq + i, seqs)
+        return remote(
+            tokens.at[:, pl.ds(pl.multiple_of(to * part, part), part)],
+            token_out.at[pl.ds(seq * batch, batch)],
+            t_send.at[i - 1], t_receive.at[i - 1], (to, row_place),
+        )
+
+    def small_copy(i):
+        source = small_out if i == 0 else small_came.at[n + i - 1]
+        return remote(source, small_came.at[i], s_send.at[i], s_receive.at[i], near[i][0])
+
+    load_dx = pltpu.make_async_copy(dr_ref, dx, other.at[0])
+
+    @pl.when(step == 0)
+    def _():
+        greet([device for device, _ in near] + [(flip(flip(seq, 1), 2), row_place)])
+        small_out[...] = small_ref[...]
+        load_dx.start()
+
+    tick(step + u)
+
+    @pl.when(step < outer)
+    def _():
+        at = pl.ds(pl.multiple_of(step * CHUNK, CHUNK), CHUNK)
+        g_outer[at] = t_dot(act_ref[...], df_ref[...]).astype(BF)
+
+    @pl.when((step >= outer) & (step < before))
+    def _():
+        at = pl.ds(pl.multiple_of((step - outer) * CHUNK, CHUNK), CHUNK)
+        g_inner[:, at] = t_dot(h_ref[...], du_ref[...]).astype(BF)
+
+    @pl.when(step == before)
+    def _():
+        load_dx.wait()
+
+    @pl.when(step >= before)
+    def _():
+        attend_back_step(
+            u, lambda: tick(before + 2 * u + 1), q_ref, k_ref, v_ref, o_ref, do_ref, pt_ref, x_ref, da_ref,
+            wq_ref, wk_ref, wv_ref, g_attn, g_total, go_total, dx, small_out,
+        )
+
+    @pl.when(step == pl.num_programs(0) - 1)
+    def _():
+        for b in range(batch):
+            tokens[b] = dx[b * length : (b + 1) * length].astype(BF)
+        for i in range(1, seqs):
+            piece(i).start()
+        own = pltpu.make_async_copy(
+            tokens.at[:, pl.ds(pl.multiple_of(seq * part, part), part)],
+            token_out.at[pl.ds(seq * batch, batch)], other.at[1],
+        )
+        own.start()
+
+        def rest(t, carry):
+            tick(t)
+            for i in range(n + 1):
+                @pl.when(t == ticks + i)
+                def _(i=i):
+                    if i > 0:
+                        small_copy(i - 1).wait()
+                        held = small_out if i == 1 else small_came.at[n + i - 2]
+                        after = small_out if i == n else small_came.at[n + i - 1]
+                        after[...] = held[...] + small_came[i - 1]
+                    if i < n:
+                        small_copy(i).start()
+            return carry
+
+        lax.fori_loop(ticks, last + 1, rest, 0)
+        own.wait()
+        for i in range(1, seqs):
+            piece(i).wait()
+
+
+def attend_back_step(
+    u, between, q_ref, k_ref, v_ref, o_ref, do_ref, pt_ref, x_ref, da_ref, wq_ref, wk_ref, wv_ref,
+    grads, g_total, go_total, dx, small_out,
+):
+    hd = PAIR // 2
+    length = q_ref.shape[1]
+    count, width = x_ref.shape
+    batch = count // length
+    quad, row = lax.div(u, batch), lax.rem(u, batch)
+    mine = pl.ds(pl.multiple_of(row * length, length), length)
+    lane = lax.broadcasted_iota(jnp.int32, (length, PAIR), 1)
+    lane8 = lax.broadcasted_iota(jnp.int32, (8, PAIR), 1)
+    dqs, dks, dvs = [], [], []
+    for pair in range(QUAD // PAIR):
+        if pair == 1:
+            between()
+        at = slice(pair * PAIR, (pair + 1) * PAIR)
+        q, k, v, o, do = (ref[0, :, at] for ref in (q_ref, k_ref, v_ref, o_ref, do_ref))
+        kt = k.T
+        prod = o.astype(F32) * do.astype(F32)
+        high = prod.astype(BF)
+        low = (prod - high.astype(F32)).astype(BF)
+        dk = dv = None
+        dqt = []
+        for h in range(2):
+            here = (lane >= hd) if h else (lane < hd)
+            ones = jnp.where((lane8 >= hd) if h else (lane8 < hd), 1.0, 0.0).astype(BF)
+            do_h = jnp.where(here, do, 0)
+            q_h = jnp.where(here, q, 0)
+            mixed = (dot_t(ones, high) + dot_t(ones, low))[0:1]
+            pt = pt_ref[0, 2 * pair + h]
+            ds = (pt.astype(F32) * (dot_t(v, do_h) - mixed)).astype(BF)
+            dv_h, dk_h = dot(pt, do_h), dot(ds, q_h)
+            dv = dv_h if dv is None else dv + dv_h
+            dk = dk_h if dk is None else dk + dk_h
+            dqt.append(dot(kt[h * hd : (h + 1) * hd], ds))
+        dqs.append((jnp.concatenate(dqt, axis=0).T * (hd ** (-0.5))).astype(BF))
+        dks.append(dk.astype(BF))
+        dvs.append(dv.astype(BF))
+    d_all = jnp.concatenate(dqs + dks + dvs, axis=1)
+    column = jnp.sum(d_all.astype(F32), axis=0, keepdims=True)
+    for j in range(width // QUAD):
+        @pl.when(quad == j)
+        def _(j=j):
+            at = slice(j * QUAD, (j + 1) * QUAD)
+            small_out[0:1, at] += column[:, 0:QUAD]
+            small_out[1:2, at] += column[:, 2 * QUAD :]
+    weights = jnp.concatenate([wq_ref[...], wk_ref[...], wv_ref[...]], axis=1)
+    d_x = dot_t(d_all, weights)
+    g_all = t_dot(x_ref[mine], d_all)
+    g_o = t_dot(o_ref[0], da_ref[mine])
+
+    dx[mine] += d_x
+
+    @pl.when(row == 0)
+    def _():
+        g_total[...] = g_all
+        go_total[...] = g_o
+
+    @pl.when((row > 0) & (row < batch - 1))
+    def _():
+        g_total[...] += g_all
+        go_total[...] += g_o
+
+    @pl.when(row == batch - 1)
+    def _():
+        base = pl.multiple_of(quad * CHUNK, CHUNK)
+        grads[pl.ds(base, width)] = (g_total[...] + g_all).astype(BF)
+        grads[pl.ds(pl.multiple_of(base + width, QUAD), QUAD)] = (go_total[...] + g_o).astype(BF)
+
+
+def back(act, df, du, hidden, q, k, v, o, do, pt, x, da, dr, wq, wk, wv, small, devices, rows, seqs):
+    batch, length, width = q.shape
+    count, ff = act.shape
+    quads, outer, inner = width // QUAD, ff // CHUNK, ff // CHUNK
+    n = len(bin(devices)) - 3
+    before = outer + inner
+    of = lambda g: jnp.maximum(g - before, 0)
+    quad = pl.BlockSpec((1, length, QUAD), lambda g: (of(g) % batch, 0, of(g) // batch))
+    cols = pl.BlockSpec((width, QUAD), lambda g: (0, of(g) // batch))
+    heads = QUAD // (width // HEADS)
+    vmem = pl.BlockSpec(memory_space=pltpu.VMEM)
+    hbm = pl.BlockSpec(memory_space=pl.ANY)
+    chunk = lambda first: pl.BlockSpec(
+        (count, CHUNK), lambda g: (0, jnp.clip(g - first, 0, ff // CHUNK - 1)), pipeline_mode=pl.Buffered(1)
+    )
+    landing = []
+    for dims, number in (((CHUNK, width), outer), ((width, CHUNK), inner), ((CHUNK, width), quads)):
+        sizes = halves(n, dims)
+        landing += [pltpu.VMEM((number,) + size, BF) for size in sizes + sizes[-1:]]
+    chunks = outer + inner + quads
+    return pl.pallas_call(
+        functools.partial(back_kernel, rows),
+        grid=(before + quads * batch,),
+        in_specs=[chunk(0), fixed((count, width)), chunk(outer), fixed((count, width))]
+        + [quad] * 5
+        + [pl.BlockSpec((1, heads, length, length), lambda g: (of(g) % batch, of(g) // batch, 0, 0)),
+           fixed((count, width)), fixed((count, width)), hbm, cols, cols, cols, vmem],
+        out_specs=[hbm] * 4 + [vmem],
+        out_shape=[
+            shape_of((ff, width), BF), shape_of((width, ff), BF), shape_of((quads * CHUNK, width), BF),
+            shape_of((batch * seqs, length // seqs, width), BF),
+            shape_of(small.shape, F32),
+        ],
+        scratch_shapes=[
+            pltpu.VMEM((ff, width), BF), pltpu.VMEM((width, ff), BF), pltpu.VMEM((quads * CHUNK, width), BF),
+            pltpu.VMEM((width, width), F32), pltpu.VMEM((QUAD, width), F32), pltpu.VMEM((count, width), F32),
+            pltpu.VMEM((batch, length, width), BF), pltpu.VMEM((2 * n,) + small.shape, F32),
+        ] + sems(2 * n, chunks) + sems(n) + sems(seqs - 1)
+        + [pltpu.SemaphoreType.DMA((chunks,)), pltpu.SemaphoreType.DMA((2,))] + landing,
+        cost_estimate=pl.CostEstimate(
+            flops=count * width * (16 * length + 16 * width), bytes_accessed=4 * count * (4 * width + HEADS * length),
+            transcendentals=0,
+        ),
+        compiler_params=pltpu.CompilerParams(
+            vmem_limit_bytes=63 << 20, collective_id=2, has_side_effects=True
+        ),
+    )(act, df, du, hidden, q, k, v, o, do, pt, x, da, dr, wq, wk, wv, small)
+
+
+def widen_kernel(outer_in, inner_in, attn_in, outer, inner, g_q, g_k, g_v, g_o, read, wide, r_sem, w_sem):
+    width, ff = inner.shape
+    jobs = []
+    for i in range(ff // width):
+        at = slice(i * width, (i + 1) * width)
+        jobs.append((outer_in.at[at], [(slice(0, width), slice(0, width), outer.at[at])]))
+    for i in range(ff // width):
+        at = slice(i * width, (i + 1) * width)
+        jobs.append((inner_in.at[:, at], [(slice(0, width), slice(0, width), inner.at[:, at])]))
+    for j in range(width // QUAD):
+        at = slice(j * QUAD, (j + 1) * QUAD)
+        parts = [
+            (slice(0, width), slice(m * QUAD, (m + 1) * QUAD), g.at[:, at]) for m, g in enumerate((g_q, g_k, g_v))
+        ]
+        parts.append((slice(width, CHUNK), slice(0, width), g_o.at[at]))
+        jobs.append((attn_in.at[j * CHUNK : (j + 1) * CHUNK], parts))
+
+    def reader(i):
+        source = jobs[i][0]
+        return pltpu.make_async_copy(source, read.at[i % 2, 0 : source.shape[0]], r_sem.at[i % 2])
+
+    def writers(i):
+        return [
+            pltpu.make_async_copy(wide.at[i % 2, r, c], target, w_sem.at[i % 2, m])
+            for m, (r, c, target) in enumerate(jobs[i][1])
+        ]
+
+    reader(0).start()
+    for i in range(len(jobs)):
+        reader(i).wait()
+        if i + 1 < len(jobs):
+            reader(i + 1).start()
+        if i >= 2:
+            for copy in writers(i - 2):
+                copy.wait()
+
+        def cast(k, carry, i=i):
+            at = pl.ds(pl.multiple_of(k * 64, 64), 64)
+            wide[i % 2, at] = read[i % 2, at].astype(F32)
+            return carry
+
+        lax.fori_loop(0, jobs[i][0].shape[0] // 64, cast, 0)
+        for copy in writers(i):
+            copy.start()
+    for i in (len(jobs) - 2, len(jobs) - 1):
+        for copy in writers(i):
+            copy.wait()
+
+
+def widen(outer, inner, attn):
+    ff, width = outer.shape
+    hbm = pl.BlockSpec(memory_space=pl.ANY)
+    square = shape_of((width, width), F32)
+    return pl.pallas_call(
+        widen_kernel,
+        in_specs=[hbm] * 3,
+        out_specs=[hbm] * 6,
+        out_shape=[shape_of((ff, width), F32), shape_of((width, ff), F32)] + [square] * 4,
+        scratch_shapes=[
+            pltpu.VMEM((2, CHUNK, width), BF), pltpu.VMEM((2, CHUNK, width), F32),
+            pltpu.SemaphoreType.DMA((2,)), pltpu.SemaphoreType.DMA((2, 4)),
+        ],
+        compiler_params=pltpu.CompilerParams(vmem_limit_bytes=32 << 20),
+    )(outer, inner, attn)
+
+
+def pool_back_kernel(r2_ref, gain_ref, ids_ref, de_ref, dr_ref, df_ref, sum_ref):
+    length, width = r2_ref.shape[1:]
+    xhat, scale = normalize(r2_ref[0])
+    lane = lax.broadcasted_iota(jnp.int32, (length, PAIR), 1)
+    hot = (lane % SEG_ROW == ids_ref[0]) & (lane < 3 * SEG_ROW)
+    hot = jnp.where(hot, 1.0, 0.0).astype(BF)
+    pieces = list(split3(de_ref[0])) + [jnp.zeros((PAIR - 3 * SEG_ROW, width), BF)]
+    d_y = dot(hot, jnp.concatenate(pieces, axis=0))
+    d_r = norm_back(d_y, gain_ref[...], xhat, scale)
+    dr_ref[0] = d_r
+    d_f = d_r.astype(BF)
+    df_ref[0] = d_f
+    sum_ref[0, 0:1] = jnp.sum(d_f.astype(F32), axis=0, keepdims=True)
+
+
+def pool_back(r2, gain, ids_col, de):
+    batch, length, width = r2.shape
+    row = pl.BlockSpec((1, length, width), lambda b: (b, 0, 0))
+    eight = pl.BlockSpec((1, 8, width), lambda b: (b, 0, 0))
+    return call(
+        pool_back_kernel,
+        (batch,),
+        [row, pl.BlockSpec((1, width), lambda b: (0, 0)),
+         pl.BlockSpec((1, length, 1), lambda b: (b, 0, 0)),
+         pl.BlockSpec((1, SEG_ROW, width), lambda b: (b, 0, 0))],
+        [row, row, eight],
+        [shape_of(r2.shape, F32), shape_of(r2.shape, BF), shape_of((batch, 8, width), F32)],
+        [],
+        batch * length * width * 300,
+        batch * length * width * 10,
+    )(r2, gain, ids_col, de)
 
 
 def local(
@@ -710,69 +905,40 @@
     d_two, d_outer, outer_sum = pool_back(
         r_two, vec(ffn_gain), ids.reshape(batch, length, 1), d_e.reshape(batch, SEG_ROW, width)
     )
-    g_outer = t_dot(flat2(active), flat2(d_outer)).astype(BF)
     d_inner, d_one, d_attn, d_o, row_sums, inner_sum = feed_back(
         d_outer, d_two, slope, outer_weight, inner_weight, r_one, vec(attn_gain), output_weight
     )
-    d_inner2 = flat2(d_inner)
-    g_inner = jnp.concatenate(
-        [t_dot(flat2(hidden), d_inner2[:, i * width : (i + 1) * width]).astype(BF) for i in range(ff // width)],
-        axis=0,
-    )
-    d_q, d_k, d_v, head_sums = attend_back(q, k, v, o, d_o, pt)
-    d_q, d_k, d_v = flat2(d_q), flat2(d_k), flat2(d_v)
-    flat = flat2(x)
-    g_attn = jnp.concatenate(
-        [t_dot(flat, d_q).astype(BF), t_dot(flat, d_k).astype(BF), t_dot(flat, d_v).astype(BF),
-         t_dot(flat2(o), flat2(d_attn)).astype(BF)], axis=0
-    )
-    row_sums, head_sums = jnp.sum(row_sums, axis=0), jnp.sum(head_sums, axis=0)
     small = jnp.concatenate(
         [
-            head_sums[0], head_sums[1], row_sums[0], row_sums[1], row_sums[2],
-            jnp.sum(inner_sum[:, 0], axis=0), jnp.sum(outer_sum[:, 0], axis=0),
-            loss_vec[0], loss_vec[1], loss_vec[2],
-        ]
-    ).reshape(-1, 128)
+            jnp.zeros((2, width), F32), jnp.sum(row_sums, axis=0)[:3], jnp.sum(outer_sum, axis=0)[:1],
+            loss_vec[:3], jnp.sum(inner_sum, axis=0)[0].reshape(-1, width),
+        ],
+        axis=0,
+    )
     small = jnp.pad(small, ((0, -small.shape[0] % 8), (0, 0)))
-    token_grad = (
-        flat2(d_one) + dot_t(d_q, query_weight) + dot_t(d_k, key_weight) + dot_t(d_v, value_weight)
-    ).astype(BF)
-    sums, grad_tokens, small = sum_all(
-        jnp.concatenate([g_outer, g_inner, g_attn], axis=0),
-        token_grad.reshape(batch, length, width), small, devices, rows, seqs,
-    )
-    grad_tokens = grad_tokens.astype(F32)
-    small = small.reshape(-1)
-    sum_outer = sums[:ff].astype(F32)
-    sum_inner = jnp.concatenate(
-        [sums[ff + i * width : ff + (i + 1) * width] for i in range(ff // width)], axis=1
-    ).astype(F32)
-    sum_attn = sums[2 * ff :].astype(F32)
-    sizes = [width] * 5 + [ff] + [width] * 4
-    pieces, at = [], 0
-    for size in sizes:
-        pieces.append(small[at : at + size])
-        at += size
-    qb, vb, ob, ag, ash, ib, wb, fg, fs, ls = pieces
+    *sums, grad_tokens, small = back(
+        flat2(active), flat2(d_outer), flat2(d_inner), flat2(hidden), q, k, v, o, d_o, pt, flat2(x),
+        flat2(d_attn), flat2(d_one), query_weight, key_weight, value_weight, small, devices, rows, seqs,
+    )
+    g_outer, g_inner, g_query, g_key, g_value, g_output = widen(*sums)
     return (
-        ls[0] / (own_segs * devices),
-        grad_tokens,
-        sum_attn[:width],
-        qb,
-        sum_attn[width : 2 * width],
-        sum_attn[2 * width : 3 * width],
-        vb,
-        sum_attn[3 * width :],
-        ob,
-        ag,
-        ash,
-        sum_inner,
-        ib,
-        sum_outer,
-        wb,
-        fg,
-        fs,
+        small[8, 0] / (own_segs * devices),
+        grad_tokens.astype(F32),
+        g_query,
+        small[0],
+        g_key,
+        g_value,
+        small[1],
+        g_output,
+        small[2],
+        small[3],
+        small[4],
+        g_inner,
+        small[9 : 9 + ff // width].reshape(-1),
+        g_outer,
+        small[5],
+        small[6],
+        small[7],
     )
 
 

time: 413 us -> 357 us (0.86); the launches traced: 405 us -> 355 us
  matrix products: 28.7 us -> 0 us
  other arithmetic: 20.1 us -> 3.8 us
  local copies, waits for them, and re-layouts: 30.1 us -> 24 us
    dot_general x12 -> x0, matrix products: 28.7 us -> none  [the longest x9 20.6 us: t_dot(): lax.dot_general(a, b, (((0,), (0,)), ((), ())), preferred_element_type=F32)]
    convert_element_type x3 -> x1, other arithmetic: 19.8 us -> 3.5 us  [local(): grad_tokens.astype(F32)]
    slice x8 -> x7, local copies, waits for them, and re-layouts: 14.7 us -> 3.87 us  [the longest x1 1.89 us: local(): small[7]]
    unnamed x83 -> x52, local copies, waits for them, and re-layouts: 11.4 us -> 15.5 us
where the time goes in v3:
time: 357 us; the launch traced here: 355 us
  Pallas kernels  300 us (84%)
  local copies, waits for them, and re-layouts  24 us (7%)
  waiting for transfers between devices  19.6 us (5%)
  starting transfers between devices  4.48 us (1%)
  other arithmetic  3.8 us (1%)
    pallas_call x1, Pallas kernels, back(): pl.pallas_call(functools.partial(back_kernel, rows), grid=(before + quads...  178 us
    pallas_call x1, Pallas kernels, contrast(): pl.pallas_call(functools.partial(contrast_kernel, rows), in_specs=[vmem]...  32.2 us
    pallas_call x1, Pallas kernels, feed(): call(feed_kernel, (batch, ff // width), [row, vec, vec, pl.BlockSpec((wid...  26 us
    pallas_call x1, Pallas kernels, attend(): call(attend_kernel, (batch, width // QUAD), [row, cols, bias, cols, cols,...  25.5 us
    pallas_call x1, Pallas kernels, feed_back(): call(feed_back_kernel, (batch, ff // width), [row, row, chunk, pl.BlockSp...  23.7 us
    all_to_all x1, waiting for transfers between devices, local(): x = lax.all_to_all(tokens, 'seq', split_axis=0, concat_axis=1, tiled=True)  19.6 us
    unnamed x52, local copies, waits for them, and re-layouts  15.5 us
    pallas_call x1, Pallas kernels, widen(): pl.pallas_call(widen_kernel, in_specs=[hbm] * 3, out_specs=[hbm] * 6, out...  10.7 us
  transfers between devices with their start and end apart: 1, of which 1 were waited for; matrix products, arithmetic and copies ran while one was open for 0% of the time, Pallas kernels for 0%

profile of v3, /device:TPU:0, one launch (start us, length us, event | category | flops | bytes accessed | tf_op | source)
XLA Modules:
  0.0 354.8 jit_solution(12467168146529903021)
XLA Ops:
  0.7 0.0 copy-start
  0.7 0.0 copy-start.17
  0.7 0.0 copy-start.18
  0.7 0.0 copy-start.19
  0.7 0.0 copy-start.20
  0.7 0.0 copy-start.21
  0.7 0.0 copy-start.22
  0.7 0.0 copy-start.23
  0.7 0.0 copy-start.24
  0.8 4.5 %all-to-all-start = ((bf16[8,128,768]{2,1,0:T(8,128)(2,1)}), bf16[8,128,768]{2,1,0:T(8,128)(2,1)}, u32[]{:S(2)}, u32[]{:S(2)}) async-start(bf16[8,128,768]{2,1,0:T(8,128)(2,1)} %param.18), calls=%async_computation | async-start | bytes 3145728 | tf_op jit(solution)/shard_map/all_to_all | solution.py:892
  5.3 0.0 copy-start.8
  5.3 0.0 copy-done.19
  5.4 0.0 copy-done.21
  5.5 0.1 dynamic-slice_bitcast_fusion
  5.6 0.1 copy.39
  5.7 0.1 stack.32
  5.9 0.2 copy.41.ids_ref
  6.1 0.3 convert_reduce_fusion
  6.4 0.1 reshape.182.counts_ref
  6.4 19.6 %all-to-all-done = bf16[8,128,768]{2,1,0:T(8,128)(2,1)} async-done(((bf16[8,128,768]{2,1,0:T(8,128)(2,1)}), bf16[8,128,768]{2,1,0:T(8,128)(2,1)}, u32[]{:S(2)}, u32[]{:S(2)}) %all-to-all-start) | async-done | bytes 1572896 | tf_op jit(solution)/shard_map/all_to_all | solution.py:892
  26.1 2.7 copy.38
  28.7 0.0 copy-done.8
  28.7 1.3 copy-done.10
  30.0 1.3 copy-done.11
  31.3 1.3 copy-done.12
  32.5 25.5 %shard_map.305 = (bf16[2,512,768]{2,1,0:T(8,128)(2,1)}, bf16[2,512,768]{2,1,0:T(8,128)(2,1)}, bf16[2,512,768]{2,1,0:T(8,128)(2,1)}, bf16[2,512,768]{2,1,0:T(8,12...) custom-call(bf16[2,512,768]{2,1,0:T(8,128)(2,1)} %bitcast.27, bf16[768,768]{1,0:T(8,128)(2,1)S(1)} %copy-done.10, ...), custom_call_target="tpu_custom_call" | custom-call | flops 8053063680 | bytes 28311552 | tf_op jit(solution)/shard_map/pallas_call | solution.py:128
  58.0 26.0 %shard_map.306 = (bf16[2,512,768]{2,1,0:T(8,128)(2,1)S(1)}, bf16[2,512,3072]{2,1,0:T(8,128)(2,1)}, bf16[2,512,3072]{2,1,0:T(8,128)(2,1)}, f32[2,512,768]{2,1,0:T(8,128)S(1)}, f32[2,8,768]{2,1,0:T(8,128)S(1)}) custom-call(f32[2,512,768]{2,1,0:T(8,128)} %get-tuple-element.50.r_ref, f32[1,768]{1,0:T(1,128)S(1)} %reshape.171.g_ref.gain_ref, ...), custom_call_target="tpu_custom_call" | custom-call | flops 9663676416 | bytes 39321600 | tf_op jit(solution)/shard_map/pallas_call | solution.py:193
  84.1 1.1 copy-done.13
  85.2 32.2 %shard_map.307 = (f32[16,768]{1,0:T(8,128)S(1)}, f32[8,768]{1,0:T(8,128)S(1)}) custom-call(f32[16,768]{1,0:T(8,128)S(1)} %bitcast.26, f32[1,768]{1,0:T(1,128)S(1)} %reshape.179.gain_ref, f32[1,768]{1,0:T(1,128)S(1)} %reshape.181.shift_ref, f32[16,128]{1,0:T(8,128)S(1)} %convert_element_type.13.tag_ref, f32[16,1]{1,0:T(8,128)S(1)} %reshape.182.counts_ref), custom_call_target="tpu_custom_call" | custom-call | flops 2415919104 | bytes 1572864 | tf_op jit(solution)/shard_map/pallas_call | solution.py:311
  117.5 0.0 copy-done.5
  117.5 3.7 %shard_map.308 = (f32[2,512,768]{2,1,0:T(8,128)S(1)}, bf16[2,512,768]{2,1,0:T(8,128)(2,1)S(1)}, f32[2,8,768]{2,1,0:T(8,128)S(1)}) custom-call(f32[2,512,768]{2,1,0:T(8,128)} %copy-done.5, f32[1,768]{1,0:T(1,128)S(1)} %reshape.179.gain_ref, s32[2,512,1]{2,1,0:T(8,128)S(1)} %copy.41.ids_ref, f32[2,8,768]{2,1,0:T(8,128)S(1)} %bitcast.21), custom_call_target="tpu_custom_call" | custom-call | flops 235929600 | bytes 7864320 | tf_op jit(solution)/shard_map/pallas_call | solution.py:839
  121.2 1.7 copy-done.6
  122.8 0.0 copy-start.9
  122.9 1.8 copy-done.9
  124.7 23.7 %shard_map.309 = (bf16[2,512,3072]{2,1,0:T(8,128)(2,1)}, f32[2,512,768]{2,1,0:T(8,128)}, bf16[2,512,768]{2,1,0:T(8,128)(2,1)S(1)}, bf16[2,512,768]{2,1,0:T(8,128...) custom-call(bf16[2,512,768]{2,1,0:T(8,128)(2,1)S(1)} %get-tuple-element.55.df_ref, ...), custom_call_target="tpu_custom_call" | custom-call | flops 10871635968 | bytes 47185920 | tf_op jit(solution)/shard_map/pallas_call | solution.py:498
  148.4 1.1 copy-done.14
  149.6 1.1 copy-done.15
  150.8 0.2 concatenate.3
  151.0 0.6 pad.4.refs_16_
  151.6 178.0 %shard_map.310 = (bf16[3072,768]{1,0:T(8,128)(2,1)}, bf16[768,3072]{1,0:T(8,128)(2,1)}, bf16[3072,768]{1,0:T(8,128)(2,1)}, bf16[8,128,768]{2,1,0:T(8,128)(2,1)}, f32[16,768]{1,0:T(8,128)}) custom-call(bf16[1024,3072]{1,0:T(8,128)(2,1)} %bitcast.30, bf16[1024,768]{1,0:T(8,128)(2,1)} %bitcast.23, bf16[1024,3072]{1,0:T(8,128)(2,1)} %bitcast.31, ...), custom_call_target="tpu_custom_call" | custom-call | flops 16106127360 | bytes 37748736 | tf_op jit(solution)/shard_map/pallas_call | solution.py:725
  329.6 1.2 slice.50
  330.8 0.7 slice.56
  331.6 1.9 slice_reduce_fusion.1
  333.5 0.6 reshape.163
  334.1 3.5 convert_element_type.15
  338.2 2.3 copy-done.3
  340.6 2.3 copy-done.4
  342.9 10.7 %shard_map.311 = (f32[3072,768]{1,0:T(8,128)}, f32[768,3072]{1,0:T(8,128)}, f32[768,768]{1,0:T(8,128)}, f32[768,768]{1,0:T(8,128)}, f32[768,768]{1,0:T(8,128)}, /*index=5*/f32[768,768]{1,0:T(8,128)}) custom-call(bf16[3072,768]{1,0:T(8,128)(2,1)S(1)} %copy-done.2, bf16[768,3072]{1,0:T(8,128)(2,1)S(1)} %copy-done.3, bf16[3072,768]{1,0:T(8,128)(2,1)S(1)} %copy-done.4), custom_call_target="tpu_custom_call" | custom-call | tf_op jit(solution)/shard_map/pallas_call | solution.py:807
  (57 shorter events, 0.2 us)
Async XLA Ops:
  0.7 4.8 %copy-start = (s32[8,512]{1,0:T(8,128)S(1)}, s32[8,512]{1,0:T(8,128)}, u32[]{:S(2)}) copy-start(s32[8,512]{1,0:T(8,128)} %param.34) | copy-start | bytes 49156
  0.7 4.6 %copy-start.17 = (bf16[768]{0:T(1024)(128)(2,1)S(1)}, bf16[768]{0:T(1024)(128)(2,1)}, u32[]{:S(2)}) copy-start(bf16[768]{0:T(1024)(128)(2,1)} %param.26) | copy-start | bytes 4612
  0.7 4.6 %copy-start.18 = (bf16[768]{0:T(1024)(128)(2,1)S(1)}, bf16[768]{0:T(1024)(128)(2,1)}, u32[]{:S(2)}) copy-start(bf16[768]{0:T(1024)(128)(2,1)} %param.32) | copy-start | bytes 4612
  0.7 4.6 %copy-start.19 = (bf16[768]{0:T(1024)(128)(2,1)S(1)}, bf16[768]{0:T(1024)(128)(2,1)}, u32[]{:S(2)}) copy-start(bf16[768]{0:T(1024)(128)(2,1)} %param.20) | copy-start | bytes 4612
  0.7 4.6 %copy-start.20 = (bf16[768]{0:T(1024)(128)(2,1)S(1)}, bf16[768]{0:T(1024)(128)(2,1)}, u32[]{:S(2)}) copy-start(bf16[768]{0:T(1024)(128)(2,1)} %param.23) | copy-start | bytes 4612
  0.7 4.7 %copy-start.21 = (bf16[768]{0:T(1024)(128)(2,1)S(1)}, bf16[768]{0:T(1024)(128)(2,1)}, u32[]{:S(2)}) copy-start(bf16[768]{0:T(1024)(128)(2,1)} %param.25) | copy-start | bytes 4612
  0.7 4.7 %copy-start.22 = (bf16[768]{0:T(1024)(128)(2,1)S(1)}, bf16[768]{0:T(1024)(128)(2,1)}, u32[]{:S(2)}) copy-start(bf16[768]{0:T(1024)(128)(2,1)} %param.27) | copy-start | bytes 4612
  0.7 4.7 %copy-start.23 = (bf16[768]{0:T(1024)(128)(2,1)S(1)}, bf16[768]{0:T(1024)(128)(2,1)}, u32[]{:S(2)}) copy-start(bf16[768]{0:T(1024)(128)(2,1)} %param.31) | copy-start | bytes 4612
  0.7 4.7 %copy-start.24 = (bf16[768]{0:T(1024)(128)(2,1)S(1)}, bf16[768]{0:T(1024)(128)(2,1)}, u32[]{:S(2)}) copy-start(bf16[768]{0:T(1024)(128)(2,1)} %param.33) | copy-start | bytes 4612
  0.8 4.7 %copy-start.25 = (s32[64]{0:T(128)S(1)}, s32[64]{0:T(128)}, u32[]{:S(2)}) copy-start(s32[64]{0:T(128)} %param.35) | copy-start | bytes 772
  0.8 5.1 %copy-start.16 = (bf16[3072]{0:T(1024)(128)(2,1)S(1)}, bf16[3072]{0:T(1024)(128)(2,1)}, u32[]{:S(2)}) copy-start(bf16[3072]{0:T(1024)(128)(2,1)} %param.29) | copy-start | bytes 18436
  0.8 25.3 %all-to-all-start = ((bf16[8,128,768]{2,1,0:T(8,128)(2,1)}), bf16[8,128,768]{2,1,0:T(8,128)(2,1)}, u32[]{:S(2)}, u32[]{:S(2)}) async-start(bf16[8,128,768]{2,1,0:T(8,128)(2,1)} %param.18), calls=%async_computation | async-start | bytes 3145728 | tf_op jit(solution)/shard_map/all_to_all | solution.py:892
  5.3 23.5 %copy-start.8 = (bf16[768,768]{1,0:T(8,128)(2,1)S(1)}, bf16[768,768]{1,0:T(8,128)(2,1)}, u32[]{:S(2)}) copy-start(bf16[768,768]{1,0:T(8,128)(2,1)} %wa_ref.1) | copy-start | bytes 3538948
  28.7 1.3 copy-start.10
  30.0 1.3 copy-start.11
  31.3 1.3 copy-start.12
  84.1 1.1 copy-start.13
  85.2 32.3 %copy-start.5 = (f32[2,512,768]{2,1,0:T(8,128)}, f32[2,512,768]{2,1,0:T(8,128)S(1)}, u32[]{:S(2)}) copy-start(f32[2,512,768]{2,1,0:T(8,128)S(1)} %get-tuple-element.52.r2_ref) | copy-start | bytes 9437188
  121.1 1.7 copy-start.6
  122.8 25.6 %copy-start.7 = (bf16[2,512,768]{2,1,0:T(8,128)(2,1)}, bf16[2,512,768]{2,1,0:T(8,128)(2,1)S(1)}, u32[]{:S(2)}) copy-start(bf16[2,512,768]{2,1,0:T(8,128)(2,1)S(1)} %get-tuple-element.55.df_ref) | copy-start | bytes 4718596
  122.8 1.8 copy-start.9
  148.4 1.1 copy-start.14
  149.6 1.1 copy-start.15
  334.1 4.2 %copy-start.2 = (bf16[3072,768]{1,0:T(8,128)(2,1)S(1)}, bf16[3072,768]{1,0:T(8,128)(2,1)}, u32[]{:S(2)}) copy-start(bf16[3072,768]{1,0:T(8,128)(2,1)} %get-tuple-element.74.outer_in) | copy-start | bytes 14155780
  338.2 2.3 copy-start.3
  340.6 2.3 copy-start.4
  342.9 10.7 %copy-start.1 = (s32[8,512]{1,0:T(8,128)S(1)}, s32[8,512]{1,0:T(8,128)}, u32[]{:S(2)}) copy-start(s32[8,512]{1,0:T(8,128)} %param.34) | copy-start | bytes 49156

commit v4 on v3

v4 whole, which is shorter than its diff:
```python
import functools

import jax
import jax.numpy as jnp
from jax import lax
from jax.experimental import pallas as pl
from jax.experimental.pallas import tpu as pltpu
from jax.sharding import PartitionSpec as P

HEADS = 12
SEG_ROW = 8
HIGHEST = lax.Precision.HIGHEST
NORM_EPS = 1e-12
POOL_EPS = 1e-06
INV_TEMPER = 100.0
MASKED = -1000000000.0
INV_ROOT_TWO_PI = 0.3989422804014327
INV_ROOT_TWO = 0.7071067811865476
BF = jnp.bfloat16
F32 = jnp.float32
MESH = pl.DeviceIdType.MESH


def dot(a, b):
    return jnp.dot(a, b, preferred_element_type=F32)


def dot_t(a, b, precision=None):
    return lax.dot_general(
        a, b, (((1,), (1,)), ((), ())), preferred_element_type=F32, precision=precision
    )


def t_dot(a, b):
    return lax.dot_general(a, b, (((0,), (0,)), ((), ())), preferred_element_type=F32)


def normalize(resid):
    center = resid - jnp.mean(resid, axis=-1, keepdims=True)
    spread = jnp.mean(center * center, axis=-1, keepdims=True)
    scale = lax.rsqrt(spread + NORM_EPS)
    return center * scale, scale


def norm_back(grad, gain, xhat, scale):
    q = grad * gain
    return scale * (
        q - jnp.mean(q, axis=-1, keepdims=True) - xhat * jnp.mean(q * xhat, axis=-1, keepdims=True)
    )


def split3(a):
    hi = a.astype(BF)
    rest = a - hi.astype(F32)
    mid = rest.astype(BF)
    return hi, mid, (rest - mid.astype(F32)).astype(BF)


def call(kernel, grid, in_specs, out_specs, out_shape, scratch, flops, moved, vmem=62):
    return pl.pallas_call(
        kernel,
        grid=grid,
        in_specs=in_specs,
        out_specs=out_specs,
        out_shape=out_shape,
        scratch_shapes=scratch,
        cost_estimate=pl.CostEstimate(flops=flops, bytes_accessed=moved, transcendentals=0),
        compiler_params=pltpu.CompilerParams(vmem_limit_bytes=vmem << 20),
    )


def shape_of(dims, dtype):
    return jax.ShapeDtypeStruct(dims, dtype)


PAIR = 128
QUAD = 256


def attend_kernel(
    tokens_ref, wq_ref, wk_ref, wv_ref, wo_ref, bias_ref, row_ref, ids_ref,
    q_ref, k_ref, v_ref, o_ref, pt_ref, r_ref, x_out, x_ref, apart_q, apart_k, send, receive, own_sem,
):
    row, quad = pl.program_id(0), pl.program_id(1)
    batch, length = x_ref.shape[0], x_ref.shape[1]
    part = tokens_ref.shape[1]
    seqs = length // part
    hd = PAIR // 2
    seq, place = lax.axis_index("seq"), lax.axis_index("rows")

    def target(b):
        return x_ref.at[b, pl.ds(pl.multiple_of(seq * part, part), part)]

    def piece(i, b):
        to = lax.rem(seq + i, seqs)
        return remote(
            tokens_ref.at[to * batch + b], target(b), send.at[b, i - 1], receive.at[b, i - 1], (to, place)
        )

    def own(b):
        return pltpu.make_async_copy(tokens_ref.at[seq * batch + b], target(b), own_sem.at[b])

    def keep(b):
        return pltpu.make_async_copy(x_ref.at[b], x_out.at[b], own_sem.at[batch + b])

    @pl.when((row == 0) & (quad == 0))
    def _():
        greet([(lax.rem(seq + i, seqs), place) for i in range(1, seqs)])
        for b in range(batch):
            for i in range(1, seqs):
                piece(i, b).start()
            own(b).start()

    for b in range(batch):
        @pl.when((row == b) & (quad == 0))
        def _(b=b):
            hot = lax.broadcasted_iota(jnp.int32, (PAIR, length), 0) == ids_ref[pl.ds(seq * batch + b, 1), :]
            hot = jnp.where(hot, 1.0, 0.0).T
            real = lax.broadcasted_iota(jnp.int32, (length, PAIR), 1) < SEG_ROW
            apart_q[...] = (hot * -(2.0**30)).astype(BF)
            apart_k[...] = jnp.where(real, 1.0 - hot, 0.0).astype(BF)
            own(b).wait()
            for i in range(1, seqs):
                piece(i, b).wait()
            keep(b).start()

    x = x_ref[row]
    q = (dot(x, wq_ref[...]) + bias_ref[0:1]).astype(BF) * jnp.asarray(hd ** (-0.5), BF)
    k = dot(x, wk_ref[...]).astype(BF)
    v = (dot(x, wv_ref[...]) + bias_ref[1:2]).astype(BF)
    q_ref[0], k_ref[0], v_ref[0] = q, k, v
    lane = lax.broadcasted_iota(jnp.int32, (length, PAIR), 1)
    outs = []
    for pair in range(QUAD // PAIR):
        at = slice(pair * PAIR, (pair + 1) * PAIR)
        keys = jnp.concatenate([k[:, at], apart_k[...]], axis=1)
        vt = v[:, at].T
        parts = []
        for h in range(2):
            mine = (lane >= hd) if h else (lane < hd)
            queries = jnp.concatenate([jnp.where(mine, q[:, at], 0), apart_q[...]], axis=1)
            st = dot_t(keys, queries)
            expo = jnp.exp(st - jnp.max(st, axis=0, keepdims=True))
            pt = (expo * (1.0 / jnp.sum(expo, axis=0, keepdims=True))).astype(BF)
            pt_ref[0, 2 * pair + h] = pt
            parts.append(dot(vt[h * hd : (h + 1) * hd], pt))
        outs.append(jnp.concatenate(parts, axis=0).T)
    o = jnp.concatenate(outs, axis=1).astype(BF)
    o_ref[0] = o
    part_sum = dot(o, wo_ref[...])

    @pl.when(quad == 0)
    def _():
        r_ref[0] = x.astype(F32) + row_ref[2:3] + part_sum

    @pl.when(quad > 0)
    def _():
        r_ref[0] += part_sum

    @pl.when((row == batch - 1) & (quad == pl.num_programs(1) - 1))
    def _():
        for b in range(batch):
            keep(b).wait()


def attend(tokens, wq, wk, wv, wo, vectors, ids, seqs):
    rows, part, width = tokens.shape
    batch, length = rows // seqs, part * seqs
    row = pl.BlockSpec((1, length, width), lambda b, j: (b, 0, 0))
    cols = pl.BlockSpec((width, QUAD), lambda b, j: (0, j))
    quad = pl.BlockSpec((1, length, QUAD), lambda b, j: (b, 0, j))
    heads = QUAD // (width // HEADS)
    vmem = pl.BlockSpec(memory_space=pltpu.VMEM)
    dims = (batch, length, width)
    act = shape_of(dims, BF)
    return pl.pallas_call(
        attend_kernel,
        grid=(batch, width // QUAD),
        in_specs=[pl.BlockSpec(memory_space=pl.ANY), cols, cols, cols,
                  pl.BlockSpec((QUAD, width), lambda b, j: (j, 0)),
                  pl.BlockSpec((8, QUAD), lambda b, j: (0, j)), vmem, vmem],
        out_specs=[quad, quad, quad, quad,
                   pl.BlockSpec((1, heads, length, length), lambda b, j: (b, j, 0, 0)), row,
                   pl.BlockSpec(memory_space=pl.ANY)],
        out_shape=[act, act, act, act, shape_of((batch, HEADS, length, length), BF), shape_of(dims, F32), act],
        scratch_shapes=[pltpu.VMEM(dims, BF)] + [pltpu.VMEM((length, PAIR), BF)] * 2
        + [pltpu.SemaphoreType.DMA((batch, seqs - 1))] * 2 + [pltpu.SemaphoreType.DMA((2 * batch,))],
        cost_estimate=pl.CostEstimate(
            flops=batch * length * width * (8 * width + 8 * length),
            bytes_accessed=batch * length * (14 * width + 2 * HEADS * length) + 8 * width * width,
            transcendentals=0,
        ),
        compiler_params=pltpu.CompilerParams(
            vmem_limit_bytes=62 << 20, collective_id=1, has_side_effects=True
        ),
    )(tokens, wq, wk, wv, wo, vectors, vectors, ids)


def gelu_both(u):
    cdf = 0.5 + 0.5 * lax.erf(u * INV_ROOT_TWO)
    return u * cdf, cdf + (INV_ROOT_TWO_PI * u) * jnp.exp(-0.5 * u * u)


def own_row(ids_ref, b):
    return lax.axis_index("seq") * (ids_ref.shape[0] // lax.axis_size("seq")) + b


FEED_VMEM = 62
FBACK_VMEM = 62


def feed_kernel(
    r_ref, vec_ref, wi_ref, wo_ref, ids_ref,
    h_ref, act_ref, slope_ref, r2_ref, pool_ref, hidden,
):
    step = pl.program_id(0)
    batch = r_ref.shape[0]

    @pl.when(step == 0)
    def _():
        for b in range(batch):
            xhat, _ = normalize(r_ref[b])
            h = xhat * vec_ref[3:4] + vec_ref[4:5]
            hidden[b] = h + vec_ref[5:6]
            h_ref[b] = h.astype(BF)

    bias = vec_ref[pl.ds(8 + step, 1)]
    for b in range(batch):
        act, slope = gelu_both(dot(h_ref[b], wi_ref[...]) + bias)
        act = act.astype(BF)
        act_ref[b] = act
        slope_ref[b] = slope.astype(BF)
        hidden[b] += dot(act, wo_ref[...])

    @pl.when(step == pl.num_programs(0) - 1)
    def _():
        for b in range(batch):
            r2 = hidden[b]
            r2_ref[b] = r2
            xhat, _ = normalize(r2)
            ids = ids_ref[pl.ds(own_row(ids_ref, b), 1)]
            hot = lax.broadcasted_iota(jnp.int32, (SEG_ROW, r2.shape[0]), 0) == ids
            counts = jnp.sum(jnp.where(hot, 1.0, 0.0), axis=1, keepdims=True)
            hot = jnp.where(hot, 1.0, 0.0).astype(BF)
            total = sum(dot(hot, piece) for piece in split3(xhat))
            pool_ref[b] = total / counts


def feed(r, vectors, wi, wo, ids):
    batch, length, width = r.shape
    ff = wi.shape[1]
    whole = pl.BlockSpec(r.shape, lambda c: (0, 0, 0))
    vec = pl.BlockSpec(memory_space=pltpu.VMEM)
    chunk = pl.BlockSpec((batch, length, width), lambda c: (0, 0, c))
    wide = shape_of((batch, length, ff), BF)
    return call(
        feed_kernel,
        (ff // width,),
        [whole, vec, pl.BlockSpec((width, width), lambda c: (0, c)),
         pl.BlockSpec((width, width), lambda c: (c, 0)), vec],
        [whole, chunk, chunk, whole, pl.BlockSpec((batch, SEG_ROW, width), lambda c: (0, 0, 0))],
        [shape_of(r.shape, BF), wide, wide, shape_of(r.shape, F32), shape_of((batch, SEG_ROW, width), F32)],
        [pltpu.VMEM(r.shape, F32)],
        4 * batch * length * width * ff,
        batch * length * (10 * width + 4 * ff) + 4 * width * ff,
        FEED_VMEM,
    )(r, vectors, wi, wo, ids)


def flip(v, step):
    return v + step * (1 - 2 * (v // step % 2))


def links(rows):
    seq, row = lax.axis_index("seq"), lax.axis_index("rows")
    core, y, x = seq % 2, seq // 2 % 2, row % 2
    other = 1 - core
    found = [
        ((flip(seq, 1), row), core),
        ((seq + core * 2 * (1 - 2 * y), row + other * (1 - 2 * x)), core * y + other * x),
        ((seq + other * 2 * (1 - 2 * y), row + core * (1 - 2 * x)), other * y + core * x),
    ]
    step = 2
    while step < rows:
        found.append(((seq, flip(row, step)), row // step % 2))
        step *= 2
    return found


def greet(devices):
    barrier = pltpu.get_barrier_semaphore()
    for device in devices:
        pl.semaphore_signal(barrier, inc=1, device_id=device, device_id_type=MESH)
    pl.semaphore_wait(barrier, len(devices))


def remote(source, target, send, receive, device):
    return pltpu.make_async_remote_copy(
        src_ref=source, dst_ref=target, send_sem=send, recv_sem=receive,
        device_id=device, device_id_type=MESH,
    )


def contrast_kernel(
    rows, xpool_ref, in_ref, ids_ref, positives_ref,
    de_ref, vec_ref, all_ref, lse_ref, send, receive,
):
    own, width = xpool_ref.shape
    total = all_ref.shape[0]
    near = links(rows)
    hops = near[3:][::-1] + near[1:3] + near[:1]
    greet([device for device, _ in hops])
    e_own = xpool_ref[...] * in_ref[6:7] + in_ref[7:8]
    seq = lax.axis_index("seq")
    sub = lax.broadcasted_iota(jnp.int32, (own, PAIR), 0)
    lane = lax.broadcasted_iota(jnp.int32, (own, PAIR), 1)
    first = lax.axis_index("rows") * positives_ref.shape[0] + seq * own
    tag = jnp.where(lane == 1, first + sub, 0)
    for i in range(own):
        tag = jnp.where((lane == 0) & (sub == i), positives_ref[seq * own + i], tag)
    tag = tag.astype(F32)
    all_ref[0:own, 0:width] = e_own
    all_ref[0:own, width:] = tag
    have = own
    for i, (device, _) in enumerate(hops):
        copy = remote(
            all_ref.at[0:have], all_ref.at[have : 2 * have], send.at[i], receive.at[i], device
        )
        copy.start()
        copy.wait()
        have *= 2

    def unit(e):
        rho = lax.rsqrt(jnp.sum(e * e, axis=1, keepdims=True) + POOL_EPS)
        return e * rho, rho

    n_all, _ = unit(all_ref[:, 0:width])
    pick = lax.broadcasted_iota(jnp.int32, (8, PAIR), 0) == lax.broadcasted_iota(jnp.int32, (8, PAIR), 1)
    tags = dot_t(pick.astype(F32), all_ref[:, width:], HIGHEST)
    pos_all, id_all = tags[0:1], tags[1:2]
    block = min(total, 512)
    for b in range(total // block):
        n_b, _ = unit(all_ref[b * block : (b + 1) * block, 0:width])
        c = dot_t(n_all, n_b, HIGHEST) * INV_TEMPER
        i = lax.broadcasted_iota(jnp.int32, c.shape, 0)
        j = lax.broadcasted_iota(jnp.int32, c.shape, 1) + b * block
        c = jnp.where(i == j, MASKED, c)
        top = jnp.max(c, axis=0, keepdims=True)
        lse_ref[:, b * block : (b + 1) * block] = (
            jnp.log(jnp.sum(jnp.exp(c - top), axis=0, keepdims=True)) + top
        )
    n_own, rho = unit(e_own)
    pos_own, id_own = tag[:, 0:1], tag[:, 1:2]
    c = dot_t(n_own, n_all, HIGHEST) * INV_TEMPER
    c = jnp.where(id_own == id_all, MASKED, c)
    top = jnp.max(c, axis=1, keepdims=True)
    lse_own = jnp.log(jnp.sum(jnp.exp(c - top), axis=1, keepdims=True)) + top
    chosen = id_all == pos_own
    picked = jnp.sum(jnp.where(chosen, c, 0.0), axis=1, keepdims=True)
    weight = (
        jnp.exp(c - lse_own)
        + jnp.exp(c - lse_ref[...])
        - jnp.where(chosen, 1.0, 0.0)
        - jnp.where(id_own == pos_all, 1.0, 0.0)
    )
    d_n = INV_TEMPER * jnp.dot(weight, n_all, precision=HIGHEST, preferred_element_type=F32)
    along = jnp.sum(e_own * d_n, axis=1, keepdims=True)
    d_e = rho * d_n - (rho * rho * rho) * e_own * along
    for b in range(own // SEG_ROW):
        ids = ids_ref[pl.ds(own_row(ids_ref, b), 1)]
        hot = lax.broadcasted_iota(jnp.int32, (SEG_ROW, ids.shape[1]), 0) == ids
        at = slice(b * SEG_ROW, (b + 1) * SEG_ROW)
        de_ref[at] = d_e[at] / jnp.sum(jnp.where(hot, 1.0, 0.0), axis=1, keepdims=True)
    vec_ref[0:1] = jnp.sum(d_e * xpool_ref[...], axis=0, keepdims=True)
    vec_ref[1:2] = jnp.sum(d_e, axis=0, keepdims=True)
    vec_ref[2:3] = jnp.broadcast_to(jnp.sum(lse_own - picked), (1, vec_ref.shape[1]))
    vec_ref[3:8] = jnp.zeros((5, vec_ref.shape[1]), F32)


def contrast(xpool, vectors, ids, positives, devices, rows):
    own, width = xpool.shape
    total = own * devices
    vmem = pl.BlockSpec(memory_space=pltpu.VMEM)
    stages = len(bin(devices)) - 3
    return pl.pallas_call(
        functools.partial(contrast_kernel, rows),
        in_specs=[vmem] * 3 + [pl.BlockSpec(memory_space=pltpu.SMEM)],
        out_specs=[vmem, vmem],
        out_shape=[shape_of((own, width), F32), shape_of((8, width), F32)],
        scratch_shapes=[
            pltpu.VMEM((total, width + PAIR), F32),
            pltpu.VMEM((1, total), F32),
            pltpu.SemaphoreType.DMA((stages,)),
            pltpu.SemaphoreType.DMA((stages,)),
        ],
        cost_estimate=pl.CostEstimate(
            flops=12 * total * total * width, bytes_accessed=4 * total * width, transcendentals=0
        ),
        compiler_params=pltpu.CompilerParams(
            vmem_limit_bytes=62 << 20, collective_id=0, has_side_effects=True
        ),
    )(xpool, vectors, ids, positives)


CHUNK = 1024


def halves(steps, dims):
    sizes, (height, wide) = [], dims
    for _ in range(steps):
        if height % 32 == 0:
            height //= 2
        else:
            wide //= 2
        sizes.append((height, wide))
    return sizes


def plan(outer, parts, quads, batch):
    attention = outer + 2 * parts
    return [
        ("ab", 0, 0, outer, 1, 1, (1, 3, 2, 1)),
        ("ab", 1, 0, outer, outer + 4, 2, (1, 3, 2, 1)),
        ("ab", 2, 0, quads, attention + 2 * batch, 2 * batch, (1, 2, 2, 1)),
    ]


def orders(rows):
    near = links(rows)
    seq, row = lax.axis_index("seq"), lax.axis_index("rows")
    along = [((seq, flip(row, 1)), row % 2), ((flip(seq, 2), row), seq // 2 % 2)]
    return {
        "ab": near,
        "xy": near[:1] + along + near[3:],
        "z": near[:1] + near[3:] + near[1:3],
    }


class Chain:
    def __init__(self, order, entry, dims, down, grads, sums, mark, came, piece, send, receive, keep):
        self.first, self.number, self.start, self.period, stretch = entry
        stretch = list(stretch) + [stretch[-1]] * (len(order) - len(stretch))
        self.after = [0]
        for wait in stretch + stretch[::-1]:
            self.after.append(self.after[-1] + wait)
        self.order, self.dims, self.down = order, dims, down
        self.grads, self.sums, self.mark = grads, sums, mark
        self.came, self.piece = came, piece
        self.send, self.receive, self.keep = send, receive, keep
        self.sizes = halves(len(order), dims)
        self.last = self.start + (self.number - 1) * self.period + self.after[-1]

    def places(self, chunk):
        row, column = (chunk * self.dims[0], 0) if self.down else (0, chunk * self.dims[1])
        before = self.dims[0]
        found = []
        for (height, wide), (_, bit) in zip(self.sizes, self.order):
            if height < before:
                kept = (row + bit * height, column)
                sent = (row + (1 - bit) * height, column)
            else:
                kept = (row, column + bit * wide)
                sent = (row, column + (1 - bit) * wide)
            found.append((kept, sent))
            (row, column), before = kept, height
        return found

    def at(self, ref, place, size):
        row, column = place
        return ref.at[
            pl.ds(pl.multiple_of(row, 16), size[0]), pl.ds(pl.multiple_of(column, PAIR), size[1])
        ]

    def copy(self, chunk, places, stage):
        n = len(self.order)
        i = stage if stage < n else 2 * n - 1 - stage
        kept, sent = places[i]
        size, device = self.sizes[i], self.order[i][0]
        mark = chunk + self.mark
        pair = self.send.at[stage, mark], self.receive.at[stage, mark]
        if stage < n:
            return remote(self.at(self.grads, sent, size), self.came[i].at[chunk], *pair, device)
        target = self.at(self.sums, kept, size)
        return remote(self.piece.at[chunk] if stage == n else target, target, *pair, device)

    def own(self, chunk, places):
        target = self.at(self.sums, places[-1][0], self.sizes[-1])
        return pltpu.make_async_copy(self.piece.at[chunk], target, self.keep.at[chunk + self.mark])

    def step(self, t):
        for stage in range(2 * len(self.order), -1, -1):
            since = t - self.after[stage] - self.start
            if self.number == 1:
                pl.when(since == 0)(functools.partial(self.advance, stage, self.first))
                continue
            index = since // self.period if self.period > 1 else since
            here = (since >= 0) & (index < self.number)
            if self.period > 1:
                here &= since % self.period == 0
            pl.when(here)(functools.partial(self.advance, stage, index + self.first))

    def advance(self, stage, chunk):
        n = len(self.order)
        places = self.places(chunk)
        if stage > 0:
            self.copy(chunk, places, stage - 1).wait()
        if 0 < stage <= n:
            height, wide = self.sizes[stage - 1]
            row, column = places[stage - 1][0]
            tile = 16 if height % 32 else 32

            def add(k, carry):
                at = pl.ds(pl.multiple_of(k * tile, 16), tile)
                mine = self.at(self.grads, (row + k * tile, column), (tile, wide))
                total = (mine[...].astype(F32) + self.came[stage - 1][chunk, at].astype(F32)).astype(BF)
                if stage < n:
                    mine[...] = total
                else:
                    self.piece[chunk, at] = total
                return carry

            lax.fori_loop(0, height // tile, add, 0)
        if stage == n:
            self.own(chunk, places).start()
        if stage == n + 1:
            self.own(chunk, places).wait()
        if stage < 2 * n:
            self.copy(chunk, places, stage).start()


def sems(*dims):
    return [pltpu.SemaphoreType.DMA(dims)] * 2


FEED_BUFFERS = 1
WEIGHT_BUFFERS = 1


def fixed(dims):
    return pl.BlockSpec(dims, lambda g: (0,) * len(dims), pipeline_mode=pl.Buffered(1))


def pool_back_step(ids, d_e, gain, resid):
    length, width = resid.shape
    xhat, scale = normalize(resid)
    sub = lax.broadcasted_iota(jnp.int32, (PAIR, length), 0)
    hot = (sub % SEG_ROW == ids) & (sub < 3 * SEG_ROW)
    hot = jnp.where(hot, 1.0, 0.0).T.astype(BF)
    pieces = list(split3(d_e)) + [jnp.zeros((PAIR - 3 * SEG_ROW, width), BF)]
    d_y = dot(hot, jnp.concatenate(pieces, axis=0))
    return norm_back(d_y, gain, xhat, scale)


def back_kernel(rows, *refs):
    (r2_ref, r1_ref, de_ref, vec_ref, ids_ref, loss_ref, act_ref, slope_ref, wo_ref, wi_ref, h_ref, wa_ref,
     q_ref, k_ref, v_ref, o_ref, pt_ref, x_ref, wq_ref, wk_ref, wv_ref) = refs[:21]
    sums, (token_out, small_out) = refs[21:24], refs[24:26]
    (g_outer, g_inner, g_attn, g_total, dx, d_f, d_u, d_a, d_o, hx, small_came, send, receive, s_send,
     s_receive, t_send, t_receive, keep, other) = refs[26:45]
    landing = refs[45:]
    step = pl.program_id(0)
    length = q_ref.shape[1]
    count, width = dx.shape
    batch = count // length
    outer, parts = sums[0].shape[0] // CHUNK, sums[1].shape[1] // width
    quads = width // QUAD
    kinds = orders(rows)
    near = kinds["ab"]
    n = len(near)
    seq, row_place = lax.axis_index("seq"), lax.axis_index("rows")
    seqs = token_out.shape[0] // batch
    part = length // seqs
    groups = [
        ((CHUNK, width), True, g_outer, sums[0], 0),
        ((width, CHUNK), False, g_inner, sums[1], outer),
        ((CHUNK, width), True, g_attn, sums[2], 2 * outer),
    ]
    chains = []
    for kind, group, *entry in plan(outer, parts, quads, batch):
        came = landing[group * (n + 1) : group * (n + 1) + n]
        piece = landing[group * (n + 1) + n]
        chains.append(Chain(kinds[kind], entry, *groups[group], came, piece, send, receive, keep))
    before = outer + parts
    ticks = outer + 2 * (parts + quads * batch)
    last = max(max(chain.last for chain in chains), ticks + n)
    p = jnp.clip(step - outer, 0, parts - 1)
    u = jnp.maximum(step - before, 0)
    now = step + jnp.maximum(step - outer, 0)

    def tick(t):
        for chain in chains:
            chain.step(t)

    def piece(i, b):
        to = lax.rem(seq + i, seqs)
        return remote(
            d_u.at[pl.ds(pl.multiple_of(b * length + to * part, part), part)],
            token_out.at[seq * batch + b],
            t_send.at[b, i - 1], t_receive.at[b, i - 1], (to, row_place),
        )

    def own_piece(b):
        return pltpu.make_async_copy(
            d_u.at[pl.ds(pl.multiple_of(b * length + seq * part, part), part)],
            token_out.at[seq * batch + b], other.at[3 + b],
        )

    def small_copy(i):
        source = small_out if i == 0 else small_came.at[n + i - 1]
        return remote(source, small_came.at[i], s_send.at[i], s_receive.at[i], near[i][0])

    load_r2 = pltpu.make_async_copy(r2_ref, dx, other.at[0])
    load_r1 = pltpu.make_async_copy(r1_ref, g_total, other.at[2])
    load_h = pltpu.make_async_copy(h_ref, hx, other.at[1])
    load_x = pltpu.make_async_copy(x_ref, hx, other.at[1])

    @pl.when(step == 0)
    def _():
        load_r2.start()
        load_r1.start()
        load_h.start()
        greet([device for device, _ in near] + [(flip(flip(seq, 1), 2), row_place)])
        small_out[...] = jnp.zeros_like(small_out)
        small_out[6:9] = loss_ref[0:3]
        load_r2.wait()
        for b in range(batch):
            at = slice(b * length, (b + 1) * length)
            ids = ids_ref[pl.ds(own_row(ids_ref, b), 1)]
            d_r = pool_back_step(ids, de_ref[b], vec_ref[6:7], dx[at])
            dx[at] = d_r
            low = d_r.astype(BF)
            d_f[at] = low
            small_out[5:6] += jnp.sum(low.astype(F32), axis=0, keepdims=True)

    tick(now)

    @pl.when(step < outer)
    def _():
        at = pl.ds(pl.multiple_of(step * CHUNK, CHUNK), CHUNK)
        g_outer[at] = t_dot(act_ref[...], d_f[...]).astype(BF)

    @pl.when(step == outer)
    def _():
        load_h.wait()

    @pl.when((step >= outer) & (step < before))
    def _():
        for b in range(batch):
            at = slice(b * length, (b + 1) * length)
            low = (dot_t(d_f[at], wo_ref[...]) * slope_ref[at].astype(F32)).astype(BF)
            d_u[at] = low
            small_out[pl.ds(9 + p, 1)] += jnp.sum(low.astype(F32), axis=0, keepdims=True)
            dx[at] += dot_t(low, wi_ref[...])
        tick(now + 1)
        at = pl.ds(pl.multiple_of(p * width, width), width)
        g_inner[:, at] = t_dot(hx[...], d_u[...]).astype(BF)

    @pl.when(step == before - 1)
    def _():
        load_x.start()
        load_r1.wait()
        for b in range(batch):
            at = slice(b * length, (b + 1) * length)
            d_h = dx[at]
            xhat, scale = normalize(g_total[at])
            d_r = norm_back(d_h, vec_ref[3:4], xhat, scale)
            dx[at] = d_r
            low = d_r.astype(BF)
            d_a[at] = low
            d_o[at] = dot_t(low, wa_ref[...]).astype(BF)
            small_out[2:3] += jnp.sum(low.astype(F32), axis=0, keepdims=True)
            small_out[3:4] += jnp.sum(d_h * xhat, axis=0, keepdims=True)
            small_out[4:5] += jnp.sum(d_h, axis=0, keepdims=True)

    @pl.when(step == before)
    def _():
        load_x.wait()

    @pl.when(step >= before)
    def _():
        attend_back_step(
            u, lambda: tick(now + 1), q_ref, k_ref, v_ref, o_ref, d_o, pt_ref, hx, d_a,
            wq_ref, wk_ref, wv_ref, g_attn, g_total, dx, small_out,
        )

    @pl.when(step == pl.num_programs(0) - 1)
    def _():
        d_u[...] = dx[...].astype(BF)
        for b in range(batch):
            for i in range(1, seqs):
                piece(i, b).start()
            own_piece(b).start()

        def rest(t, carry):
            tick(t)
            for i in range(n + 1):
                @pl.when(t == ticks + i)
                def _(i=i):
                    if i > 0:
                        small_copy(i - 1).wait()
                        held = small_out if i == 1 else small_came.at[n + i - 2]
                        after = small_out if i == n else small_came.at[n + i - 1]
                        after[...] = held[...] + small_came[i - 1]
                    if i < n:
                        small_copy(i).start()
            return carry

        lax.fori_loop(ticks, last + 1, rest, 0)
        for b in range(batch):
            own_piece(b).wait()
            for i in range(1, seqs):
                piece(i, b).wait()


def attend_back_step(
    u, between, q_ref, k_ref, v_ref, o_ref, d_o, pt_ref, x_ref, da_ref, wq_ref, wk_ref, wv_ref,
    grads, g_total, dx, small_out,
):
    hd = PAIR // 2
    length = q_ref.shape[1]
    count, width = x_ref.shape
    batch = count // length
    quad, row = lax.div(u, batch), lax.rem(u, batch)
    mine = pl.ds(pl.multiple_of(row * length, length), length)
    lane = lax.broadcasted_iota(jnp.int32, (length, PAIR), 1)
    lane8 = lax.broadcasted_iota(jnp.int32, (8, PAIR), 1)
    dqs, dks, dvs = [], [], []
    for pair in range(QUAD // PAIR):
        if pair == 1:
            between()
        at = slice(pair * PAIR, (pair + 1) * PAIR)
        q, k, v, o = (ref[0, :, at] for ref in (q_ref, k_ref, v_ref, o_ref))
        do = d_o[mine, pl.ds(pl.multiple_of(quad * QUAD + pair * PAIR, PAIR), PAIR)]
        kt = k.T
        prod = o.astype(F32) * do.astype(F32)
        high = prod.astype(BF)
        low = (prod - high.astype(F32)).astype(BF)
        dk = dv = None
        dqt = []
        for h in range(2):
            here = (lane >= hd) if h else (lane < hd)
            ones = jnp.where((lane8 >= hd) if h else (lane8 < hd), 1.0, 0.0).astype(BF)
            do_h = jnp.where(here, do, 0)
            q_h = jnp.where(here, q, 0)
            mixed = (dot_t(ones, high) + dot_t(ones, low))[0:1]
            pt = pt_ref[0, 2 * pair + h]
            ds = (pt.astype(F32) * (dot_t(v, do_h) - mixed)).astype(BF)
            dv_h, dk_h = dot(pt, do_h), dot(ds, q_h)
            dv = dv_h if dv is None else dv + dv_h
            dk = dk_h if dk is None else dk + dk_h
            dqt.append(dot(kt[h * hd : (h + 1) * hd], ds))
        dqs.append((jnp.concatenate(dqt, axis=0).T * (hd ** (-0.5))).astype(BF))
        dks.append(dk.astype(BF))
        dvs.append(dv.astype(BF))
    d_all = jnp.concatenate(dqs + dks + dvs, axis=1)
    column = jnp.sum(d_all.astype(F32), axis=0, keepdims=True)
    for j in range(width // QUAD):
        @pl.when(quad == j)
        def _(j=j):
            at = slice(j * QUAD, (j + 1) * QUAD)
            small_out[0:1, at] += column[:, 0:QUAD]
            small_out[1:2, at] += column[:, 2 * QUAD :]
    weights = jnp.concatenate([wq_ref[...], wk_ref[...], wv_ref[...]], axis=1)
    d_x = dot_t(d_all, weights)
    g_all = t_dot(x_ref[mine], d_all)
    g_o = t_dot(o_ref[0], da_ref[mine])

    dx[mine] += d_x

    top, bottom = slice(0, width), slice(width, width + QUAD)

    @pl.when(row == 0)
    def _():
        g_total[top] = g_all
        g_total[bottom] = g_o

    @pl.when((row > 0) & (row < batch - 1))
    def _():
        g_total[top] += g_all
        g_total[bottom] += g_o

    @pl.when(row == batch - 1)
    def _():
        base = pl.multiple_of(quad * CHUNK, CHUNK)
        grads[pl.ds(base, width)] = (g_total[top] + g_all).astype(BF)
        grads[pl.ds(pl.multiple_of(base + width, QUAD), QUAD)] = (g_total[bottom] + g_o).astype(BF)


def back(r2, r1, de, vectors, ids, loss, act, slope, wo, wi, hidden, wa, q, k, v, o, pt, x, wq, wk, wv,
         devices, rows, seqs):
    batch, length, width = q.shape
    count, ff = act.shape
    quads, outer, parts = width // QUAD, ff // CHUNK, ff // width
    n = len(bin(devices)) - 3
    before = outer + parts
    of = lambda g: jnp.maximum(g - before, 0)
    at = lambda g: jnp.clip(g - outer, 0, parts - 1)
    quad = pl.BlockSpec((1, length, QUAD), lambda g: (of(g) % batch, 0, of(g) // batch))
    cols = pl.BlockSpec((width, QUAD), lambda g: (0, of(g) // batch), pipeline_mode=pl.Buffered(WEIGHT_BUFFERS))
    heads = QUAD // (width // HEADS)
    vmem = pl.BlockSpec(memory_space=pltpu.VMEM)
    hbm = pl.BlockSpec(memory_space=pl.ANY)
    one = pl.Buffered(1)
    landing = []
    for dims, number in (((CHUNK, width), outer), ((width, CHUNK), outer), ((CHUNK, width), quads)):
        sizes = halves(n, dims)
        landing += [pltpu.VMEM((number,) + size, BF) for size in sizes + sizes[-1:]]
    chunks = 2 * outer + quads
    small = shape_of((-(-(9 + parts) // 8) * 8, width), F32)
    return pl.pallas_call(
        functools.partial(back_kernel, rows),
        grid=(before + quads * batch,),
        in_specs=[
            hbm, hbm, vmem, vmem, vmem, vmem,
            pl.BlockSpec((count, CHUNK), lambda g: (0, jnp.clip(g, 0, outer - 1)), pipeline_mode=one),
            pl.BlockSpec((count, width), lambda g: (0, at(g)), pipeline_mode=one),
            pl.BlockSpec((width, width), lambda g: (at(g), 0), pipeline_mode=pl.Buffered(FEED_BUFFERS)),
            pl.BlockSpec((width, width), lambda g: (0, at(g)), pipeline_mode=pl.Buffered(FEED_BUFFERS)),
            hbm, fixed((width, width)),
            quad, quad, quad, quad,
            pl.BlockSpec((1, heads, length, length), lambda g: (of(g) % batch, of(g) // batch, 0, 0)),
            hbm, cols, cols, cols,
        ],
        out_specs=[hbm] * 4 + [vmem],
        out_shape=[
            shape_of((ff, width), BF), shape_of((width, ff), BF), shape_of((quads * CHUNK, width), BF),
            shape_of((batch * seqs, length // seqs, width), BF), small,
        ],
        scratch_shapes=[
            pltpu.VMEM((ff, width), BF), pltpu.VMEM((width, ff), BF), pltpu.VMEM((quads * CHUNK, width), BF),
            pltpu.VMEM((count, width), F32), pltpu.VMEM((count, width), F32),
        ] + [pltpu.VMEM((count, width), BF)] * 4 + [
            pltpu.VMEM((count, width), BF), pltpu.VMEM((2 * n,) + small.shape, F32),
        ] + sems(2 * n, chunks) + sems(n) + sems(batch, seqs - 1)
        + [pltpu.SemaphoreType.DMA((chunks,)), pltpu.SemaphoreType.DMA((3 + batch,))] + landing,
        cost_estimate=pl.CostEstimate(
            flops=count * width * (16 * length + 16 * width), bytes_accessed=4 * count * (4 * width + HEADS * length),
            transcendentals=0,
        ),
        compiler_params=pltpu.CompilerParams(
            vmem_limit_bytes=63 << 20, collective_id=2, has_side_effects=True
        ),
    )(r2, r1, de, vectors, ids, loss, act, slope, wo, wi, hidden, wa, q, k, v, o, pt, x, wq, wk, wv)


RING = 4


def widen_kernel(outer_in, inner_in, attn_in, token_in, outer, inner, g_q, g_k, g_v, g_o, g_tok, read, wide, r_sem, w_sem):
    width, ff = inner.shape
    jobs = []
    for i in range(ff // width):
        at = slice(i * width, (i + 1) * width)
        jobs.append((outer_in.at[at], [(slice(0, width), slice(0, width), outer.at[at])]))
    for i in range(ff // width):
        at = slice(i * width, (i + 1) * width)
        jobs.append((inner_in.at[:, at], [(slice(0, width), slice(0, width), inner.at[:, at])]))
    for j in range(width // QUAD):
        at = slice(j * QUAD, (j + 1) * QUAD)
        parts = [
            (slice(0, width), slice(m * QUAD, (m + 1) * QUAD), g.at[:, at]) for m, g in enumerate((g_q, g_k, g_v))
        ]
        parts.append((slice(width, CHUNK), slice(0, width), g_o.at[at]))
        jobs.append((attn_in.at[j * CHUNK : (j + 1) * CHUNK], parts))

    for at in range(0, g_tok.shape[0], CHUNK):
        at = slice(at, at + CHUNK)
        jobs.append((token_in.at[at], [(slice(0, CHUNK), slice(0, width), g_tok.at[at])]))

    def reader(i):
        source = jobs[i][0]
        return pltpu.make_async_copy(source, read.at[i % RING, 0 : source.shape[0]], r_sem.at[i % RING])

    def writers(i):
        return [
            pltpu.make_async_copy(wide.at[i % RING, r, c], target, w_sem.at[i % RING, m])
            for m, (r, c, target) in enumerate(jobs[i][1])
        ]

    for i in range(RING - 1):
        reader(i).start()
    for i in range(len(jobs)):
        reader(i).wait()
        if i + RING - 1 < len(jobs):
            reader(i + RING - 1).start()
        if i >= RING:
            for copy in writers(i - RING):
                copy.wait()

        def cast(k, carry, i=i):
            at = pl.ds(pl.multiple_of(k * 64, 64), 64)
            wide[i % RING, at] = read[i % RING, at].astype(F32)
            return carry

        lax.fori_loop(0, jobs[i][0].shape[0] // 64, cast, 0)
        for copy in writers(i):
            copy.start()
    for i in range(len(jobs) - RING, len(jobs)):
        for copy in writers(i):
            copy.wait()


def widen(outer, inner, attn, tokens):
    ff, width = outer.shape
    hbm = pl.BlockSpec(memory_space=pl.ANY)
    square = shape_of((width, width), F32)
    return pl.pallas_call(
        widen_kernel,
        in_specs=[hbm] * 4,
        out_specs=[hbm] * 7,
        out_shape=[shape_of((ff, width), F32), shape_of((width, ff), F32)] + [square] * 4
        + [shape_of(tokens.shape, F32)],
        scratch_shapes=[
            pltpu.VMEM((RING, CHUNK, width), BF), pltpu.VMEM((RING, CHUNK, width), F32),
            pltpu.SemaphoreType.DMA((RING,)), pltpu.SemaphoreType.DMA((RING, 4)),
        ],
        compiler_params=pltpu.CompilerParams(vmem_limit_bytes=62 << 20),
    )(outer, inner, attn, tokens)


def local(
    tokens,
    query_weight,
    query_bias,
    key_weight,
    value_weight,
    value_bias,
    output_weight,
    output_bias,
    attn_gain,
    attn_shift,
    inner_weight,
    inner_bias,
    outer_weight,
    outer_bias,
    ffn_gain,
    ffn_shift,
    segment_ids,
    positives,
):
    group_rows, local_len, width = tokens.shape
    ff = inner_weight.shape[1]
    seqs = lax.axis_size("seq")
    batch, length = group_rows // seqs, local_len * seqs
    count = batch * length
    own_segs = batch * SEG_ROW
    rows = lax.axis_size("rows")
    devices = rows * seqs
    flat2 = lambda a: a.reshape(count, a.shape[-1])
    lines = [query_bias, value_bias, output_bias, attn_gain, attn_shift, outer_bias, ffn_gain, ffn_shift]
    lines += [inner_bias[i * width : (i + 1) * width] for i in range(ff // width)]
    place = lax.broadcasted_iota(jnp.int32, (-(-len(lines) // 8) * 8, width), 0)
    vectors = jnp.zeros(place.shape, F32)
    for i, line in enumerate(lines):
        vectors = jnp.where(place == i, line.astype(F32)[None, :], vectors)

    q, k, v, o, pt, r_one, x = attend(
        tokens, query_weight, key_weight, value_weight, output_weight, vectors, segment_ids, seqs
    )
    hidden, active, slope, r_two, xpool = feed(r_one, vectors, inner_weight, outer_weight, segment_ids)
    d_e, loss_vec = contrast(
        xpool.reshape(own_segs, width), vectors, segment_ids, positives, devices, rows
    )
    *sums, grad_tokens, small = back(
        flat2(r_two), flat2(r_one), d_e.reshape(batch, SEG_ROW, width), vectors, segment_ids, loss_vec,
        flat2(active), flat2(slope), outer_weight, inner_weight, flat2(hidden), output_weight,
        q, k, v, o, pt, flat2(x), query_weight, key_weight, value_weight, devices, rows, seqs,
    )
    g_outer, g_inner, g_query, g_key, g_value, g_output, g_tokens = widen(
        *sums, grad_tokens.reshape(count, width)
    )
    return (
        small[8, 0] / (own_segs * devices),
        g_tokens.reshape(tokens.shape),
        g_query,
        small[0],
        g_key,
        g_value,
        small[1],
        g_output,
        small[2],
        small[3],
        small[4],
        g_inner,
        small[9 : 9 + ff // width].reshape(-1),
        g_outer,
        small[5],
        small[6],
        small[7],
    )


def solution(mesh):
    placed = (
        (P("rows", "seq", None),) + (P(),) * 15 + (P("rows", None), P("rows"))
    )
    return jax.shard_map(
        local,
        mesh=mesh,
        in_specs=placed,
        out_specs=(P(), P("rows", "seq", None)) + (P(),) * 15,
        check_vma=False,
    )
```

time: 357 us -> 318 us (0.89)
  waiting for transfers between devices: 19.6 us -> 0 us
  local copies, waits for them, and re-layouts: 24 us -> 4.45 us
  starting transfers between devices: 4.48 us -> 0 us
    all_to_all x1 -> x0, waiting for transfers between devices: 19.6 us -> none  [local(): x = lax.all_to_all(tokens, 'seq', split_axis=0, concat_axis=1, tiled=True)]
    unnamed x52 -> x0, local copies, waits for them, and re-layouts: 15.5 us -> none
    pallas_call x1, Pallas kernels: 178 us -> 193 us  [back(): pl.pallas_call(functools.partial(back_kernel, rows), grid=(before + quads...]
    pallas_call x5 -> x3, Pallas kernels: 89.6 us -> 77 us  [the longest x1 39 us: attend(): pl.pallas_call(attend_kernel, grid=(batch, width // QUAD), in_specs=[pl.B...]
    all_to_all x1 -> x0, starting transfers between devices: 4.48 us -> none  [local(): x = lax.all_to_all(tokens, 'seq', split_axis=0, concat_axis=1, tiled=True)]
  transfers between devices with their start and end apart: 1 -> 0, of which waited for: 1 -> 0; matrix products, arithmetic and copies ran while one was open for 0% -> 0% of each run, Pallas kernels for 0% -> 0%
where the time goes in v4:
time: 318 us; the launch traced here: 317 us
  Pallas kernels  303 us (95%)
  other arithmetic  6.99 us (2%)
  local copies, waits for them, and re-layouts  4.45 us (1%)
    pallas_call x1, Pallas kernels, back(): pl.pallas_call(functools.partial(back_kernel, rows), grid=(before + quads...  193 us
    pallas_call x1, Pallas kernels, attend(): pl.pallas_call(attend_kernel, grid=(batch, width // QUAD), in_specs=[pl.B...  39 us
    pallas_call x1, Pallas kernels, contrast(): pl.pallas_call(functools.partial(contrast_kernel, rows), in_specs=[vmem]...  33.1 us
    pallas_call x1, Pallas kernels, feed(): call(feed_kernel, (ff // width,), [whole, vec, pl.BlockSpec((width, width...  21.8 us
    pallas_call x1, Pallas kernels, widen(): pl.pallas_call(widen_kernel, in_specs=[hbm] * 4, out_specs=[hbm] * 7, out...  16.2 us

profile of v4, /device:TPU:0, one launch (start us, length us, event | category | flops | bytes accessed | tf_op | source)
XLA Modules:
  0.0 317.2 jit_solution(15036994987299421195)
XLA Ops:
  0.7 0.7 convert_element_type.47
  1.4 0.7 convert_element_type.46
  2.1 0.7 convert_element_type.45
  2.8 0.7 convert_element_type.44
  3.5 0.7 convert_element_type.43
  4.1 0.7 convert_element_type.42
  4.8 0.7 convert_element_type.41
  5.5 0.7 convert_element_type.40
  6.2 0.8 slice_convert_fusion.3
  7.0 0.7 select_select_fusion.bias_ref.row_ref.vec_ref.in_ref.refs_3_
  7.7 39.0 %shard_map.305 = (bf16[2,512,768]{2,1,0:T(8,128)(2,1)}, bf16[2,512,768]{2,1,0:T(8,128)(2,1)}, bf16[2,512,768]{2,1,0:T(8,128)(2,1)}, bf16[2,512,768]{2,1,0:T(8,12...) custom-call(bf16[8,128,768]{2,1,0:T(8,128)(2,1)} %tokens_ref.1, ...), custom_call_target="tpu_custom_call" | custom-call | flops 8053063680 | bytes 28311552 | tf_op jit(solution)/shard_map/pallas_call | solution.py:176
  46.7 21.8 %shard_map.306 = (bf16[2,512,768]{2,1,0:T(8,128)(2,1)}, bf16[2,512,3072]{2,1,0:T(8,128)(2,1)}, bf16[2,512,3072]{2,1,0:T(8,128)(2,1)}, f32[2,512,768]{2,1,0:T(8,128)}, f32[2,8,768]{2,1,0:T(8,128)}) custom-call(f32[2,512,768]{2,1,0:T(8,128)} %get-tuple-element.43.r_ref, f32[16,768]{1,0:T(8,128)} %select_select_fusion.bias_ref.row_ref.vec_ref.in_ref.refs_3_, ...), custom_call_target="tpu_custom_call" | custom-call | flops 9663676416 | bytes 29884416 | tf_op jit(solution)/shard_map/pallas_call | solution.py:256
  68.5 33.1 %shard_map.307 = (f32[16,768]{1,0:T(8,128)}, f32[8,768]{1,0:T(8,128)}) custom-call(f32[16,768]{1,0:T(8,128)} %bitcast.20, f32[16,768]{1,0:T(8,128)} %select_select_fusion.bias_ref.row_ref.vec_ref.in_ref.refs_3_, s32[8,512]{1,0:T(8,128)} %refs_4_.1, s32[64]{0:T(128)} %positives_ref.1), custom_call_target="tpu_custom_call" | custom-call | flops 2415919104 | bytes 1572864 | tf_op jit(solution)/shard_map/pallas_call | solution.py:385
  101.6 193.2 %shard_map.308 = (bf16[3072,768]{1,0:T(8,128)(2,1)}, bf16[768,3072]{1,0:T(8,128)(2,1)}, bf16[3072,768]{1,0:T(8,128)(2,1)}, bf16[8,128,768]{2,1,0:T(8,128)(2,1)}, f32[16,768]{1,0:T(8,128)}) custom-call(f32[1024,768]{1,0:T(8,128)} %bitcast.16, f32[1024,768]{1,0:T(8,128)} %bitcast.15, f32[2,8,768]{2,1,0:T(8,128)} %bitcast.19, ...), custom_call_target="tpu_custom_call" | custom-call | flops 16106127360 | bytes 37748736 | tf_op jit(solution)/shard_map/pallas_call | solution.py:810
  294.8 1.2 slice.46
  296.7 0.7 slice.52
  297.4 1.9 slice_reduce_fusion
  299.3 0.6 reshape.91
  299.9 16.2 %shard_map.309 = (f32[3072,768]{1,0:T(8,128)}, f32[768,3072]{1,0:T(8,128)}, f32[768,768]{1,0:T(8,128)}, f32[768,768]{1,0:T(8,128)}, f32[768,768]{1,0:T(8,128)}, /*index=5*/f32[768,768]{1,0:T(8,128)}, f32[1024,768]{1,0:T(8,128)}) custom-call(bf16[3072,768]{1,0:T(8,128)(2,1)} %get-tuple-element.58.outer_in, bf16[768,3072]{1,0:T(8,128)(2,1)} %get-tuple-element.59.inner_in, ...), custom_call_target="tpu_custom_call" | custom-call | tf_op jit(solution)/shard_map/pallas_call | solution.py:907
  (6 shorter events, 0.0 us)

commit v5 on v4

--- a/solution.py
+++ b/solution.py
@@ -420,8 +420,8 @@
     attention = outer + 2 * parts
     return [
         ("ab", 0, 0, outer, 1, 1, (1, 3, 2, 1)),
-        ("ab", 1, 0, outer, outer + 4, 2, (1, 3, 2, 1)),
-        ("ab", 2, 0, quads, attention + 2 * batch, 2 * batch, (1, 2, 2, 1)),
+        ("ab", 1, 0, outer, outer + 4, 2, (1, 2, 2, 1)),
+        ("ab", 2, 0, quads, attention + 2 * batch, 2 * batch, (1, 2, 1, 1)),
     ]
 
 
@@ -533,6 +533,9 @@
 
 
 FEED_BUFFERS = 1
+TOKENS_AT = 2
+TOKENS_STEP = 3
+SMALL_AT = 6
 WEIGHT_BUFFERS = 1
 
 
@@ -582,7 +585,7 @@
         chains.append(Chain(kinds[kind], entry, *groups[group], came, piece, send, receive, keep))
     before = outer + parts
     ticks = outer + 2 * (parts + quads * batch)
-    last = max(max(chain.last for chain in chains), ticks + n)
+    last = max(max(chain.last for chain in chains), ticks + SMALL_AT + n, ticks + TOKENS_AT + batch * TOKENS_STEP)
     p = jnp.clip(step - outer, 0, parts - 1)
     u = jnp.maximum(step - before, 0)
     now = step + jnp.maximum(step - outer, 0)
@@ -687,14 +690,17 @@
     def _():
         d_u[...] = dx[...].astype(BF)
         for b in range(batch):
-            for i in range(1, seqs):
-                piece(i, b).start()
             own_piece(b).start()
 
         def rest(t, carry):
             tick(t)
+            for b in range(batch):
+                @pl.when(t == ticks + TOKENS_AT + b * TOKENS_STEP)
+                def _(b=b):
+                    for i in range(1, seqs):
+                        piece(i, b).start()
             for i in range(n + 1):
-                @pl.when(t == ticks + i)
+                @pl.when(t == ticks + SMALL_AT + i)
                 def _(i=i):
                     if i > 0:
                         small_copy(i - 1).wait()
@@ -950,9 +956,10 @@
     lines = [query_bias, value_bias, output_bias, attn_gain, attn_shift, outer_bias, ffn_gain, ffn_shift]
     lines += [inner_bias[i * width : (i + 1) * width] for i in range(ff // width)]
     place = lax.broadcasted_iota(jnp.int32, (-(-len(lines) // 8) * 8, width), 0)
-    vectors = jnp.zeros(place.shape, F32)
+    vectors = jnp.zeros(place.shape, BF)
     for i, line in enumerate(lines):
-        vectors = jnp.where(place == i, line.astype(F32)[None, :], vectors)
+        vectors = jnp.where(place == i, line[None, :], vectors)
+    vectors = vectors.astype(F32)
 
     q, k, v, o, pt, r_one, x = attend(
         tokens, query_weight, key_weight, value_weight, output_weight, vectors, segment_ids, seqs

time: 318 us -> 298 us (0.937)
  Pallas kernels: 303 us -> 288 us
  other arithmetic: 6.99 us -> 1.55 us
    pallas_call x1, Pallas kernels: 193 us -> 178 us  [back(): pl.pallas_call(functools.partial(back_kernel, rows), grid=(before + quads...]
    convert_element_type x9 -> x1, other arithmetic: 6.24 us -> 1.52 us  [local(): vectors = vectors.astype(F32)]
where the time goes in v5:
time: 298 us; the launch traced here: 297 us
  Pallas kernels  288 us (97%)
  local copies, waits for them, and re-layouts  5.23 us (2%)
    pallas_call x1, Pallas kernels, back(): pl.pallas_call(functools.partial(back_kernel, rows), grid=(before + quads...  178 us
    pallas_call x1, Pallas kernels, attend(): pl.pallas_call(attend_kernel, grid=(batch, width // QUAD), in_specs=[pl.B...  39 us
    pallas_call x1, Pallas kernels, contrast(): pl.pallas_call(functools.partial(contrast_kernel, rows), in_specs=[vmem]...  33.1 us
    pallas_call x1, Pallas kernels, feed(): call(feed_kernel, (ff // width,), [whole, vec, pl.BlockSpec((width, width...  21.8 us
    pallas_call x1, Pallas kernels, widen(): pl.pallas_call(widen_kernel, in_specs=[hbm] * 4, out_specs=[hbm] * 7, out...  16.2 us

profile of v5, /device:TPU:0, one launch (start us, length us, event | category | flops | bytes accessed | tf_op | source)
XLA Modules:
  0.0 297.4 jit_solution(3989189548892294746)
XLA Ops:
  0.7 0.8 fusion
  1.5 1.5 select_convert_fusion.bias_ref.row_ref.vec_ref.in_ref.refs_3_
  3.0 39.0 %shard_map.305 = (bf16[2,512,768]{2,1,0:T(8,128)(2,1)}, bf16[2,512,768]{2,1,0:T(8,128)(2,1)}, bf16[2,512,768]{2,1,0:T(8,128)(2,1)}, bf16[2,512,768]{2,1,0:T(8,12...) custom-call(bf16[8,128,768]{2,1,0:T(8,128)(2,1)} %tokens_ref.1, ...), custom_call_target="tpu_custom_call" | custom-call | flops 8053063680 | bytes 28311552 | tf_op jit(solution)/shard_map/pallas_call | solution.py:176
  42.0 21.8 %shard_map.306 = (bf16[2,512,768]{2,1,0:T(8,128)(2,1)}, bf16[2,512,3072]{2,1,0:T(8,128)(2,1)}, bf16[2,512,3072]{2,1,0:T(8,128)(2,1)}, f32[2,512,768]{2,1,0:T(8,128)}, f32[2,8,768]{2,1,0:T(8,128)}) custom-call(f32[2,512,768]{2,1,0:T(8,128)} %get-tuple-element.43.r_ref, f32[16,768]{1,0:T(8,128)} %select_convert_fusion.bias_ref.row_ref.vec_ref.in_ref.refs_3_, ...), custom_call_target="tpu_custom_call" | custom-call | flops 9663676416 | bytes 29884416 | tf_op jit(solution)/shard_map/pallas_call | solution.py:256
  63.8 33.1 %shard_map.307 = (f32[16,768]{1,0:T(8,128)}, f32[8,768]{1,0:T(8,128)}) custom-call(f32[16,768]{1,0:T(8,128)} %bitcast.20, f32[16,768]{1,0:T(8,128)} %select_convert_fusion.bias_ref.row_ref.vec_ref.in_ref.refs_3_, s32[8,512]{1,0:T(8,128)} %refs_4_.1, s32[64]{0:T(128)} %positives_ref.1), custom_call_target="tpu_custom_call" | custom-call | flops 2415919104 | bytes 1572864 | tf_op jit(solution)/shard_map/pallas_call | solution.py:385
  97.0 178.0 %shard_map.308 = (bf16[3072,768]{1,0:T(8,128)(2,1)}, bf16[768,3072]{1,0:T(8,128)(2,1)}, bf16[3072,768]{1,0:T(8,128)(2,1)}, bf16[8,128,768]{2,1,0:T(8,128)(2,1)}, f32[16,768]{1,0:T(8,128)}) custom-call(f32[1024,768]{1,0:T(8,128)} %bitcast.16, f32[1024,768]{1,0:T(8,128)} %bitcast.15, f32[2,8,768]{2,1,0:T(8,128)} %bitcast.19, ...), custom_call_target="tpu_custom_call" | custom-call | flops 16106127360 | bytes 37748736 | tf_op jit(solution)/shard_map/pallas_call | solution.py:816
  275.0 1.2 slice.46
  276.8 0.7 slice.52
  277.6 1.9 slice_reduce_fusion
  279.5 0.6 reshape.91
  280.1 16.2 %shard_map.309 = (f32[3072,768]{1,0:T(8,128)}, f32[768,3072]{1,0:T(8,128)}, f32[768,768]{1,0:T(8,128)}, f32[768,768]{1,0:T(8,128)}, f32[768,768]{1,0:T(8,128)}, /*index=5*/f32[768,768]{1,0:T(8,128)}, f32[1024,768]{1,0:T(8,128)}) custom-call(bf16[3072,768]{1,0:T(8,128)(2,1)} %get-tuple-element.58.outer_in, bf16[768,3072]{1,0:T(8,128)(2,1)} %get-tuple-element.59.inner_in, ...), custom_call_target="tpu_custom_call" | custom-call | tf_op jit(solution)/shard_map/pallas_call | solution.py:913
  (6 shorter events, 0.0 us)

commit v6 on v5

--- a/solution.py
+++ b/solution.py
@@ -47,6 +47,12 @@
     return scale * (
         q - jnp.mean(q, axis=-1, keepdims=True) - xhat * jnp.mean(q * xhat, axis=-1, keepdims=True)
     )
+
+
+def dot_split(a, b):
+    a_high, b_high = a.astype(BF), b.astype(BF)
+    a_low, b_low = (a - a_high.astype(F32)).astype(BF), (b - b_high.astype(F32)).astype(BF)
+    return dot_t(a_high, b_high) + (dot_t(a_high, b_low) + dot_t(a_low, b_high))
 
 
 def split3(a):
@@ -308,8 +314,9 @@
     own, width = xpool_ref.shape
     total = all_ref.shape[0]
     near = links(rows)
-    hops = near[3:][::-1] + near[1:3] + near[:1]
-    greet([device for device, _ in hops])
+    hops = near[3:][::-1] + near[1:3]
+    sibling = near[0][0]
+    greet([device for device, _ in near])
     e_own = xpool_ref[...] * in_ref[6:7] + in_ref[7:8]
     seq = lax.axis_index("seq")
     sub = lax.broadcasted_iota(jnp.int32, (own, PAIR), 0)
@@ -322,13 +329,26 @@
     all_ref[0:own, 0:width] = e_own
     all_ref[0:own, width:] = tag
     have = own
+
+    def across(i, low, high):
+        return remote(
+            all_ref.at[low:high], all_ref.at[total // 2 + low : total // 2 + high],
+            send.at[len(hops) + i], receive.at[len(hops) + i], sibling,
+        )
+
+    passed = [across(0, 0, have)]
+    passed[0].start()
     for i, (device, _) in enumerate(hops):
         copy = remote(
             all_ref.at[0:have], all_ref.at[have : 2 * have], send.at[i], receive.at[i], device
         )
         copy.start()
         copy.wait()
+        passed.append(across(i + 1, have, 2 * have))
+        passed[-1].start()
         have *= 2
+    for copy in passed:
+        copy.wait()
 
     def unit(e):
         rho = lax.rsqrt(jnp.sum(e * e, axis=1, keepdims=True) + POOL_EPS)
@@ -341,7 +361,7 @@
     block = min(total, 512)
     for b in range(total // block):
         n_b, _ = unit(all_ref[b * block : (b + 1) * block, 0:width])
-        c = dot_t(n_all, n_b, HIGHEST) * INV_TEMPER
+        c = dot_split(n_all, n_b) * INV_TEMPER
         i = lax.broadcasted_iota(jnp.int32, c.shape, 0)
         j = lax.broadcasted_iota(jnp.int32, c.shape, 1) + b * block
         c = jnp.where(i == j, MASKED, c)
@@ -390,8 +410,8 @@
         scratch_shapes=[
             pltpu.VMEM((total, width + PAIR), F32),
             pltpu.VMEM((1, total), F32),
-            pltpu.SemaphoreType.DMA((stages,)),
-            pltpu.SemaphoreType.DMA((stages,)),
+            pltpu.SemaphoreType.DMA((2 * stages,)),
+            pltpu.SemaphoreType.DMA((2 * stages,)),
         ],
         cost_estimate=pl.CostEstimate(
             flops=12 * total * total * width, bytes_accessed=4 * total * width, transcendentals=0

time: 298 us -> 296 us (level)
  no operation moved by 1% of the time
where the time goes in v6:
time: 296 us; the launch traced here: 295 us
  Pallas kernels  286 us (97%)
  local copies, waits for them, and re-layouts  5.23 us (2%)
    pallas_call x1, Pallas kernels, back(): pl.pallas_call(functools.partial(back_kernel, rows), grid=(before + quads...  178 us
    pallas_call x1, Pallas kernels, attend(): pl.pallas_call(attend_kernel, grid=(batch, width // QUAD), in_specs=[pl.B...  39 us
    pallas_call x1, Pallas kernels, contrast(): pl.pallas_call(functools.partial(contrast_kernel, rows), in_specs=[vmem]...  31.5 us
    pallas_call x1, Pallas kernels, feed(): call(feed_kernel, (ff // width,), [whole, vec, pl.BlockSpec((width, width...  21.8 us
    pallas_call x1, Pallas kernels, widen(): pl.pallas_call(widen_kernel, in_specs=[hbm] * 4, out_specs=[hbm] * 7, out...  16.2 us

profile of v6, /device:TPU:0, one launch (start us, length us, event | category | flops | bytes accessed | tf_op | source)
XLA Modules:
  0.0 295.4 jit_solution(8992082484193688018)
XLA Ops:
  0.7 0.8 fusion
  1.5 1.5 select_convert_fusion.bias_ref.row_ref.vec_ref.in_ref.refs_3_
  3.0 39.0 %shard_map.305 = (bf16[2,512,768]{2,1,0:T(8,128)(2,1)}, bf16[2,512,768]{2,1,0:T(8,128)(2,1)}, bf16[2,512,768]{2,1,0:T(8,128)(2,1)}, bf16[2,512,768]{2,1,0:T(8,12...) custom-call(bf16[8,128,768]{2,1,0:T(8,128)(2,1)} %tokens_ref.1, ...), custom_call_target="tpu_custom_call" | custom-call | flops 8053063680 | bytes 28311552 | tf_op jit(solution)/shard_map/pallas_call | solution.py:182
  42.0 21.8 %shard_map.306 = (bf16[2,512,768]{2,1,0:T(8,128)(2,1)}, bf16[2,512,3072]{2,1,0:T(8,128)(2,1)}, bf16[2,512,3072]{2,1,0:T(8,128)(2,1)}, f32[2,512,768]{2,1,0:T(8,128)}, f32[2,8,768]{2,1,0:T(8,128)}) custom-call(f32[2,512,768]{2,1,0:T(8,128)} %get-tuple-element.43.r_ref, f32[16,768]{1,0:T(8,128)} %select_convert_fusion.bias_ref.row_ref.vec_ref.in_ref.refs_3_, ...), custom_call_target="tpu_custom_call" | custom-call | flops 9663676416 | bytes 29884416 | tf_op jit(solution)/shard_map/pallas_call | solution.py:262
  63.8 31.5 %shard_map.307 = (f32[16,768]{1,0:T(8,128)}, f32[8,768]{1,0:T(8,128)}) custom-call(f32[16,768]{1,0:T(8,128)} %bitcast.20, f32[16,768]{1,0:T(8,128)} %select_convert_fusion.bias_ref.row_ref.vec_ref.in_ref.refs_3_, s32[8,512]{1,0:T(8,128)} %refs_4_.1, s32[64]{0:T(128)} %positives_ref.1), custom_call_target="tpu_custom_call" | custom-call | flops 2415919104 | bytes 1572864 | tf_op jit(solution)/shard_map/pallas_call | solution.py:405
  95.3 177.7 %shard_map.308 = (bf16[3072,768]{1,0:T(8,128)(2,1)}, bf16[768,3072]{1,0:T(8,128)(2,1)}, bf16[3072,768]{1,0:T(8,128)(2,1)}, bf16[8,128,768]{2,1,0:T(8,128)(2,1)}, f32[16,768]{1,0:T(8,128)}) custom-call(f32[1024,768]{1,0:T(8,128)} %bitcast.16, f32[1024,768]{1,0:T(8,128)} %bitcast.15, f32[2,8,768]{2,1,0:T(8,128)} %bitcast.19, ...), custom_call_target="tpu_custom_call" | custom-call | flops 16106127360 | bytes 37748736 | tf_op jit(solution)/shard_map/pallas_call | solution.py:836
  273.0 1.2 slice.46
  274.8 0.7 slice.52
  275.6 1.9 slice_reduce_fusion
  277.5 0.6 reshape.91
  278.1 16.2 %shard_map.309 = (f32[3072,768]{1,0:T(8,128)}, f32[768,3072]{1,0:T(8,128)}, f32[768,768]{1,0:T(8,128)}, f32[768,768]{1,0:T(8,128)}, f32[768,768]{1,0:T(8,128)}, /*index=5*/f32[768,768]{1,0:T(8,128)}, f32[1024,768]{1,0:T(8,128)}) custom-call(bf16[3072,768]{1,0:T(8,128)(2,1)} %get-tuple-element.58.outer_in, bf16[768,3072]{1,0:T(8,128)(2,1)} %get-tuple-element.59.inner_in, ...), custom_call_target="tpu_custom_call" | custom-call | tf_op jit(solution)/shard_map/pallas_call | solution.py:933
  (6 shorter events, 0.0 us)
